TPU v7x, 32 devices: a whole 2x2x4 slice. The times are simulated.
32 devices in a mesh: groups: 2 (over y), req: 8 (over z, x), tp: 2 (over core).
Axes of the slice: x: 2, y: 2, z: 4, core: 2. Of those that a mesh axis runs over, the one named last changes fastest.
Arguments:
- projected_queries: bfloat16 [4096, 8192], P(('groups', 'req'), 'tp'), parts along dimension 0, may hold values from -6 to 6
- projected_keys: bfloat16 [4096, 1024], P(('groups', 'req'), 'tp'), parts along dimension 0, may hold values from -6 to 6
- projected_values: bfloat16 [4096, 1024], P(('groups', 'req'), 'tp'), parts along dimension 0, may hold values from -6 to 6
- request_adapter: int32 [8], P('groups'), parts along dimension 0, may hold values from 0 to 7
- adapter_slot_table: int32 [16], P('groups'), parts along dimension 0, may hold values from 0 to 7, each once
- adapter_down_factor: bfloat16 [16, 64, 128, 64], P(('groups', 'req'), 'tp'), parts along dimension 0, may hold values from -0.0625 to 0.0625
- adapter_up_factor: bfloat16 [16, 64, 40, 128], P(('groups', 'req'), None, 'tp'), parts along dimension 0, may hold values from -0.75 to 0.75
Outputs:
- adapter_delta: bfloat16 [4096, 5120], P(('groups', 'req'), 'tp'), parts along dimension 0
There are 2 independent parts, one for each index of `groups`. A program takes and returns all parts, laid end to end along the dimension named above; each array names one. Nothing has to cross between parts.
Inputs may be any that keep to these rules, and one draw needn't show every extreme that they name: `adapter_slot_table`: each slot once.
All inputs are finite; a program needn't handle non-finite values.
Results may differ from a plain program's by a relative error of at most 0.012.
Values may be sent and summed in bfloat16 or wider, within the bound.
No kernel may reach another device: no remote copies, remote signals or barrier semaphores. Data moves between devices by JAX's collectives and lax.ppermute only.
A program may use at most 64 MiB of HBM per device.

v0:
```python
import math

import jax
import jax.numpy as jnp
from jax import lax
from jax.sharding import PartitionSpec as P

QUERY_HEAD_COUNT = 64
KEY_VALUE_HEADS = 8
HEAD_SIZE = 128
ADAPTER_RANK = 64


def shifted(shard, axis, by):
    size = lax.axis_size(axis)
    pairs = [(i, i + by) for i in range(size) if 0 <= i + by < size]
    return lax.ppermute(shard, axis, pairs)


def partial_attend(query_part, key_part, value_part, visible):
    row_count = query_part.shape[0]
    query_group_size = QUERY_HEAD_COUNT // KEY_VALUE_HEADS
    kv_count = key_part.shape[1] // HEAD_SIZE
    score_scale = 1.0 / math.sqrt(HEAD_SIZE)
    start_state = (
        jnp.zeros((row_count, kv_count * query_group_size * HEAD_SIZE), jnp.float32),
        jnp.zeros((row_count, kv_count * query_group_size), jnp.float32),
        jnp.zeros((row_count, kv_count * query_group_size), jnp.float32),
    )

    def head_step(kv_index, carried):
        accum_out, row_peak, row_total = carried
        query_head = lax.dynamic_slice_in_dim(
            query_part, kv_index * query_group_size * HEAD_SIZE, query_group_size * HEAD_SIZE, 1
        )
        query_head = query_head.reshape(row_count, query_group_size, HEAD_SIZE)
        key_head = lax.dynamic_slice_in_dim(key_part, kv_index * HEAD_SIZE, HEAD_SIZE, 1)
        value_head = lax.dynamic_slice_in_dim(value_part, kv_index * HEAD_SIZE, HEAD_SIZE, 1)
        scores = (
            jnp.einsum("tgd,sd->tgs", query_head, key_head, preferred_element_type=jnp.float32)
            * score_scale
        )
        scores = jnp.where(visible[:, None, :], scores, -1e30)
        head_peak = jnp.max(scores, axis=2)
        exp_terms = jnp.where(visible[:, None, :], jnp.exp(scores - head_peak[..., None]), 0.0)
        head_total = jnp.sum(exp_terms, axis=2)
        head_out = jnp.einsum(
            "tgs,sd->tgd",
            exp_terms.astype(jnp.bfloat16),
            value_head,
            preferred_element_type=jnp.float32,
        )
        accum_out = lax.dynamic_update_slice_in_dim(
            accum_out,
            head_out.reshape(row_count, query_group_size * HEAD_SIZE),
            kv_index * query_group_size * HEAD_SIZE,
            1,
        )
        row_peak = lax.dynamic_update_slice_in_dim(
            row_peak, head_peak, kv_index * query_group_size, 1
        )
        row_total = lax.dynamic_update_slice_in_dim(
            row_total, head_total, kv_index * query_group_size, 1
        )
        return (accum_out, row_peak, row_total)

    return lax.fori_loop(0, kv_count, head_step, start_state)


def widen(per_head_values):
    return jnp.repeat(per_head_values, HEAD_SIZE, axis=1)


def finish(parts):
    accum_out, row_peak, row_total = parts
    return (accum_out / widen(row_total)).astype(jnp.bfloat16)


def body(
    projected_queries,
    projected_keys,
    projected_values,
    request_adapter,
    adapter_slot_table,
    adapter_down_factor,
    adapter_up_factor,
):
    row_count = projected_queries.shape[0]
    partner_count = lax.axis_size("req")
    parity = lax.axis_index("req") % 2
    row_line = jnp.arange(row_count)
    causal = row_line[None, :] <= row_line[:, None]
    earlier = shifted((projected_keys, projected_values), "req", 1)
    both_keys = jnp.concatenate([earlier[0], projected_keys], axis=0)
    both_values = jnp.concatenate([earlier[1], projected_values], axis=0)

    def first_span():
        return finish(partial_attend(projected_queries, projected_keys, projected_values, causal))

    def second_span():
        seen_mask = jnp.concatenate([jnp.ones((row_count, row_count), bool), causal], axis=1)
        return finish(partial_attend(projected_queries, both_keys, both_values, seen_mask))

    context = lax.cond(parity == 1, second_span, first_span)
    owned_slots = adapter_down_factor.shape[0]
    local_head = adapter_down_factor.shape[1]
    local_block = adapter_up_factor.shape[2]
    down_cut = jnp.moveaxis(
        adapter_down_factor.reshape(
            owned_slots, local_head, partner_count, HEAD_SIZE // partner_count, ADAPTER_RANK
        ),
        2,
        1,
    )
    up_cut = jnp.moveaxis(
        adapter_up_factor.reshape(
            owned_slots, ADAPTER_RANK, local_block, partner_count, 128 // partner_count
        ),
        3,
        1,
    )
    library_down, library_up = (
        lax.all_to_all(down_cut, "req", split_axis=1, concat_axis=0, tiled=True),
        lax.all_to_all(up_cut, "req", split_axis=1, concat_axis=0, tiled=True),
    )
    library_down = library_down[:, 0]
    library_up = library_up[:, 0]
    slot_line = adapter_slot_table[request_adapter[jnp.arange(partner_count) // 2]]
    down_rows = jnp.take(library_down, slot_line, axis=0)
    up_rows = jnp.take(library_up, slot_line, axis=0)
    down_all, up_all = (
        lax.all_to_all(down_rows, "req", split_axis=0, concat_axis=0, tiled=True),
        lax.all_to_all(up_rows, "req", split_axis=0, concat_axis=0, tiled=True),
    )
    context_split = context.reshape(row_count, down_all.shape[1], partner_count, down_all.shape[2])
    rank_part = jnp.einsum(
        "thrp,rhpk->tk", context_split, down_all, preferred_element_type=jnp.float32
    )
    rank_mix = lax.psum(rank_part.astype(jnp.bfloat16), "tp")
    mixed = jnp.einsum("tk,rkbl->tbrl", rank_mix, up_all, preferred_element_type=jnp.float32)
    mixed = mixed.reshape(row_count, up_all.shape[2] * partner_count * up_all.shape[3])
    return (2.0 * mixed).astype(jnp.bfloat16)


def solution(mesh):
    placed = (
        P(("groups", "req"), "tp"),
        P(("groups", "req"), "tp"),
        P(("groups", "req"), "tp"),
        P("groups"),
        P("groups"),
        P(("groups", "req"), "tp", None, None),
        P(("groups", "req"), None, "tp", None),
    )
    return jax.shard_map(
        body, mesh=mesh, in_specs=placed, out_specs=P(("groups", "req"), "tp"), check_vma=False
    )
```

profile of v0, /device:TPU:17, one launch (start us, length us, event | category | flops | bytes accessed | tf_op | source)
XLA Modules:
  0.0 129.2 jit_solution(1455457761446923830)
XLA Ops:
  0.0 1.4 %copy.54 = bf16[1,64,20,128]{1,3,2,0:T(8,128)(2,1)S(1)} copy(bf16[1,64,20,128]{3,1,2,0:T(8,128)(2,1)} %param.19) | data formatting | bytes 655360 | tf_op args[6]
  1.5 1.2 reshape.189
  2.7 5.6 %all-to-all-start = ((bf16[8,2,10240]{2,1,0:T(2,128)(2,1)}), bf16[8,2,10240]{2,1,0:T(2,128)(2,1)S(1)}, u32[]{:S(2)}, u32[]{:S(2)}) async-start(bf16[8,2,10240]{2,1,0:T(2,128)(2,1)} %reshape.189), calls=%async_computation | async-start | bytes 655360 | tf_op jit(solution)/shard_map/all_to_all | solution.py:124
  9.0 1.5 %reshape.193 = bf16[8,2,16384]{2,1,0:T(2,128)(2,1)} reshape(bf16[8,1,32,16,64]{4,3,2,1,0:T(8,128)(2,1)S(1)} %bitcast.129) | data formatting | bytes 1048576
  11.9 4.3 %all-to-all-done = bf16[8,2,10240]{2,1,0:T(2,128)(2,1)S(1)} async-done(((bf16[8,2,10240]{2,1,0:T(2,128)(2,1)}), bf16[8,2,10240]{2,1,0:T(2,128)(2,1)S(1)}, u32[]{:S(2)}, u32[]{:S(2)}) %all-to-all-start) | async-done | bytes 327712 | tf_op jit(solution)/shard_map/all_to_all | solution.py:124
  16.3 5.5 %all-to-all-start.2 = ((bf16[8,2,16384]{2,1,0:T(2,128)(2,1)}), bf16[8,2,16384]{2,1,0:T(2,128)(2,1)S(1)}, u32[]{:S(2)}, u32[]{:S(2)}) async-start(bf16[8,2,16384]{2,1,0:T(2,128)(2,1)} %reshape.193), calls=%async_computation.2 | async-start | bytes 1048576 | tf_op jit(solution)/shard_map/all_to_all | solution.py:123
  24.3 9.4 %all-to-all-done.2 = bf16[8,2,16384]{2,1,0:T(2,128)(2,1)S(1)} async-done(((bf16[8,2,16384]{2,1,0:T(2,128)(2,1)}), bf16[8,2,16384]{2,1,0:T(2,128)(2,1)S(1)}, u32[]{:S(2)}, u32[]{:S(2)}) %all-to-all-start.2) | async-done | bytes 524320 | tf_op jit(solution)/shard_map/all_to_all | solution.py:123
  33.8 5.9 %all-to-all-start.1 = ((bf16[8,2,10240]{2,1,0:T(2,128)(2,1)}), bf16[8,2,10240]{2,1,0:T(2,128)(2,1)S(1)}, u32[]{:S(2)}, u32[]{:S(2)}) async-start(bf16[8,2,10240]{2,1,0:T(2,128)(2,1)} %reshape.191), calls=%async_computation.1 | async-start | bytes 655360 | tf_op jit(solution)/shard_map/all_to_all | solution.py:133
  41.5 1.5 %reshape.195 = bf16[8,2,16384]{2,1,0:T(2,128)(2,1)} reshape(bf16[8,32,16,64]{3,2,1,0:T(8,128)(2,1)S(1)} %broadcast_select_fusion) | data formatting | bytes 1048576
  43.1 4.6 %all-to-all-done.1 = bf16[8,2,10240]{2,1,0:T(2,128)(2,1)S(1)} async-done(((bf16[8,2,10240]{2,1,0:T(2,128)(2,1)}), bf16[8,2,10240]{2,1,0:T(2,128)(2,1)S(1)}, u32[]{:S(2)}, u32[]{:S(2)}) %all-to-all-start.1) | async-done | bytes 327712 | tf_op jit(solution)/shard_map/all_to_all | solution.py:133
  47.7 5.6 %all-to-all-start.3 = ((bf16[8,2,16384]{2,1,0:T(2,128)(2,1)}), bf16[8,2,16384]{2,1,0:T(2,128)(2,1)}, u32[]{:S(2)}, u32[]{:S(2)}) async-start(bf16[8,2,16384]{2,1,0:T(2,128)(2,1)} %reshape.195), calls=%async_computation.3 | async-start | bytes 1048576 | tf_op jit(solution)/shard_map/all_to_all | solution.py:132
  53.3 3.1 %collective-permute-start.1 = (bf16[256,512]{0,1:T(8,128)(2,1)S(1)}, bf16[256,512]{0,1:T(8,128)(2,1)S(1)}, u32[]{:S(2)}, u32[]{:S(2)}) collective-permute-start(bf16[256,512]{0,1:T(8,128)(2,1)S(1)} %copy.56), channel_id=1, source_target_pairs={{0,2},{2,4},{4,6},{6,8},{8,10},{10,12},{12,14},{1,3},{3,5},{5,7},{... | collective-permute-start | bytes 786440 | tf_op jit(solution)/shard_map/ppermute | solution.py:17
  56.5 3.1 %collective-permute-start = (bf16[256,512]{1,0:T(8,128)(2,1)S(1)}, bf16[256,512]{1,0:T(8,128)(2,1)S(1)}, u32[]{:S(2)}, u32[]{:S(2)}) collective-permute-start(bf16[256,512]{1,0:T(8,128)(2,1)S(1)} %copy-done.4), channel_id=1, source_target_pairs={{0,2},{2,4},{4,6},{6,8},{8,10},{10,12},{12,14},{1,3},{3,5},{5,7},{... | collective-permute-start | bytes 786440 | tf_op jit(solution)/shard_map/ppermute | solution.py:17
  59.6 12.3 %collective-permute-done.1 = bf16[256,512]{0,1:T(8,128)(2,1)S(1)} collective-permute-done((bf16[256,512]{0,1:T(8,128)(2,1)S(1)}, bf16[256,512]{0,1:T(8,128)(2,1)S(1)}, u32[]{:S(2)}, u32[]{:S(2)}) %collective-permute-start.1) | collective-permute-done | bytes 262176 | tf_op jit(solution)/shard_map/ppermute | solution.py:17
  72.0 5.6 %collective-permute-done = bf16[256,512]{1,0:T(8,128)(2,1)S(1)} collective-permute-done((bf16[256,512]{1,0:T(8,128)(2,1)S(1)}, bf16[256,512]{1,0:T(8,128)(2,1)S(1)}, u32[]{:S(2)}, u32[]{:S(2)}) %collective-permute-start) | collective-permute-done | bytes 262176 | tf_op jit(solution)/shard_map/ppermute | solution.py:17
  78.4 37.4 %conditional.1 = (bf16[256,32,8,16]{0,3,2,1:T(8,128)(2,1)S(1)}) conditional(s32[]{:T(128)} %convert_element_type.41, (pred[256,256]{1,0:T(8,128)(4,1)S(1)}, pred[256,256]{1,0:T(8,128)(4,1)S(1)}, bf16[256,4096]{1,0:T(8,128)(2,1)}, bf16[256,512]{1,0:T(8,128)(2,1)S(1)}, bf16[256,512]{1,0:T(8,128)(2,1)S(1)}) %tuple.95, (pred[256,256]{1,0:T(8,128)(4,1)S(1)}, ...), branch_computations={%region_0.5_spmd, %region_5.10_spmd} | conditional | flops 545260032 | bytes 22307336 | solution.py:104
  79.9 2.2 %broadcast.160 = f32[256,4096]{0,1:T(8,128)} broadcast(f32[]{:T(128)} %constant.270.clone), dimensions={} | broadcast | bytes 4194308 | tf_op jit(solution)/shard_map/broadcast.8
  82.1 30.9 %while.33 = (s32[]{:T(128)}, f32[256,4096]{0,1:T(8,128)}, f32[256,32]{0,1:T(8,128)S(1)}, pred[256,256]{0,1:T(8,128)(4,1)}, pred[256,256]{0,1:T(8,128)(4,1)}, /*i...) while((s32[]{:T(128)}, f32[256,4096]{0,1:T(8,128)}, ...), condition=%wide.region_4.4_spmd, body=%wide.region_1.3_spmd.sunk | while | flops 407898624 | bytes 11493743 | solution.py:67
  83.8 2.7 %fusion.112 = f32[256,8,128]{0,2,1:T(8,128)} fusion(f32[256,8,256]{0,2,1:T(8,128)S(1)} %fusion.111, pred[256,256]{0,1:T(8,128)(4,1)} %get-tuple-element.634, pred[256,256]{0,1:T(8,128)(4,1)} %get-tuple-element.635, bf16[256,512]{1,0:T(8,128)(2,1)S(1)} %get-tuple-element.638, s32[]{:T(128)S(6)} %select_n.243), kind=kOutput, calls=%fused_computation.8.clone.1 | convolution fusion | flops 136841472 | bytes 3342340 | tf_op jit(solution)/shard_map/cond/branch_0_fun/while/body/eval_jaxpr/tgs,sd->tgd/dot_general | solution.py:47
  86.5 2.3 %constant_dynamic-update-slice_fusion.10 = f32[256,4096]{0,1:T(8,128)} fusion(f32[256,4096]{0,1:T(8,128)} %get-tuple-element.616, f32[256,1024]{0,1:T(8,128)} %bitcast.126, s32[]{:T(128)S(6)} %select_n.242), kind=kLoop, calls=%fused_computation.23.clone.1 | loop fusion | bytes 2097156 | tf_op jit(solution)/shard_map/cond/branch_0_fun/while/body/eval_jaxpr/dynamic_update_slice | solution.py:53
  91.5 2.7 %fusion.112 = f32[256,8,128]{0,2,1:T(8,128)} fusion(f32[256,8,256]{0,2,1:T(8,128)S(1)} %fusion.111, pred[256,256]{0,1:T(8,128)(4,1)} %get-tuple-element.634, pred[256,256]{0,1:T(8,128)(4,1)} %get-tuple-element.635, bf16[256,512]{1,0:T(8,128)(2,1)S(1)} %get-tuple-element.638, s32[]{:T(128)S(6)} %select_n.243), kind=kOutput, calls=%fused_computation.8.clone.1 | convolution fusion | flops 136841472 | bytes 3342340 | tf_op jit(solution)/shard_map/cond/branch_0_fun/while/body/eval_jaxpr/tgs,sd->tgd/dot_general | solution.py:47
  94.2 2.4 %constant_dynamic-update-slice_fusion.10 = f32[256,4096]{0,1:T(8,128)} fusion(f32[256,4096]{0,1:T(8,128)} %get-tuple-element.616, f32[256,1024]{0,1:T(8,128)} %bitcast.126, s32[]{:T(128)S(6)} %select_n.242), kind=kLoop, calls=%fused_computation.23.clone.1 | loop fusion | bytes 2097156 | tf_op jit(solution)/shard_map/cond/branch_0_fun/while/body/eval_jaxpr/dynamic_update_slice | solution.py:53
  99.3 2.7 %fusion.112 = f32[256,8,128]{0,2,1:T(8,128)} fusion(f32[256,8,256]{0,2,1:T(8,128)S(1)} %fusion.111, pred[256,256]{0,1:T(8,128)(4,1)} %get-tuple-element.634, pred[256,256]{0,1:T(8,128)(4,1)} %get-tuple-element.635, bf16[256,512]{1,0:T(8,128)(2,1)S(1)} %get-tuple-element.638, s32[]{:T(128)S(6)} %select_n.243), kind=kOutput, calls=%fused_computation.8.clone.1 | convolution fusion | flops 136841472 | bytes 3342340 | tf_op jit(solution)/shard_map/cond/branch_0_fun/while/body/eval_jaxpr/tgs,sd->tgd/dot_general | solution.py:47
  102.0 2.3 %constant_dynamic-update-slice_fusion.10 = f32[256,4096]{0,1:T(8,128)} fusion(f32[256,4096]{0,1:T(8,128)} %get-tuple-element.616, f32[256,1024]{0,1:T(8,128)} %bitcast.126, s32[]{:T(128)S(6)} %select_n.242), kind=kLoop, calls=%fused_computation.23.clone.1 | loop fusion | bytes 2097156 | tf_op jit(solution)/shard_map/cond/branch_0_fun/while/body/eval_jaxpr/dynamic_update_slice | solution.py:53
  107.0 2.7 %fusion.112 = f32[256,8,128]{0,2,1:T(8,128)} fusion(f32[256,8,256]{0,2,1:T(8,128)S(1)} %fusion.111, pred[256,256]{0,1:T(8,128)(4,1)} %get-tuple-element.634, pred[256,256]{0,1:T(8,128)(4,1)} %get-tuple-element.635, bf16[256,512]{1,0:T(8,128)(2,1)S(1)} %get-tuple-element.638, s32[]{:T(128)S(6)} %select_n.243), kind=kOutput, calls=%fused_computation.8.clone.1 | convolution fusion | flops 136841472 | bytes 3342340 | tf_op jit(solution)/shard_map/cond/branch_0_fun/while/body/eval_jaxpr/tgs,sd->tgd/dot_general | solution.py:47
  109.7 2.3 %constant_dynamic-update-slice_fusion.10 = f32[256,4096]{0,1:T(8,128)} fusion(f32[256,4096]{0,1:T(8,128)} %get-tuple-element.616, f32[256,1024]{0,1:T(8,128)} %bitcast.126, s32[]{:T(128)S(6)} %select_n.242), kind=kLoop, calls=%fused_computation.23.clone.1 | loop fusion | bytes 2097156 | tf_op jit(solution)/shard_map/cond/branch_0_fun/while/body/eval_jaxpr/dynamic_update_slice | solution.py:53
  113.0 2.5 %fusion.30 = bf16[256,4096]{0,1:T(8,128)(2,1)S(1)} fusion(f32[256,4096]{0,1:T(8,128)} %get-tuple-element.376, f32[256,32]{0,1:T(8,128)S(1)} %get-tuple-element.377), kind=kLoop, calls=%fused_computation.34 | loop fusion | flops 2097152 | bytes 6324224 | tf_op jit(solution)/shard_map/cond/branch_0_fun/convert_element_type | solution.py:76
  115.8 1.3 %copy-done.2 = bf16[256,32,8,16]{0,3,2,1:T(8,128)(2,1)} copy-done((bf16[256,32,8,16]{0,3,2,1:T(8,128)(2,1)}, bf16[256,32,8,16]{0,3,2,1:T(8,128)(2,1)S(1)}, u32[]{:S(2)}) %copy-start.2) | copy-done | bytes 2097176
  117.6 3.2 %reshape.196 = bf16[8,32,16,64]{3,2,1,0:T(8,128)(2,1)} reshape(bf16[8,2,16384]{2,1,0:T(2,128)(2,1)} %all-to-all-done.3) | data formatting | bytes 1048576
  120.8 1.8 %fusion.62 = bf16[256,64]{0,1:T(8,128)(2,1)S(1)} fusion(bf16[256,32,8,16]{0,3,2,1:T(8,128)(2,1)S(1)} %copy-done.3, bf16[8,32,16,64]{3,2,1,0:T(8,128)(2,1)} %reshape.196), kind=kOutput, calls=%fused_computation.65 | convolution fusion | flops 134234112 | bytes 2654208 | tf_op jit(solution)/shard_map/thrp,rhpk->tk/dot_general | solution.py:136
  122.5 4.5 %psum.7 = bf16[256,64]{0,1:T(8,128)(2,1)S(1)} all-reduce(bf16[256,64]{0,1:T(8,128)(2,1)S(1)} %fusion.62), channel_id=1, replica_groups=mesh['groups'=2,'req'=8,'tp'=2] {'tp'}, use_global_device_ids=true, to_apply=%region_10.11 | all-reduce | flops 16384 | bytes 65536 | tf_op jit(solution)/shard_map/psum | solution.py:139
  127.6 1.6 %copy.67 = bf16[256,2560]{1,0:T(8,128)(2,1)} copy(bf16[256,2560]{0,1:T(8,128)(2,1)S(1)} %bitcast.128) | data formatting | bytes 2621440 | tf_op jit(solution)/shard_map/convert_element_type | solution.py:142
  (81 shorter events, 20.7 us)
Async XLA Ops:
  0.0 10.6 %copy-start = (s32[4]{0:T(128)S(1)}, s32[4]{0:T(128)}, u32[]{:S(2)}) copy-start(s32[4]{0:T(128)} %param.16) | copy-start | bytes 52
  0.0 8.3 %copy-start.5 = (bf16[1,32,128,64]{2,3,1,0:T(8,128)(2,1)S(1)}, bf16[1,32,128,64]{2,3,1,0:T(8,128)(2,1)}, u32[]{:S(2)}) copy-start(bf16[1,32,128,64]{2,3,1,0:T(8,128)(2,1)} %param.18) | copy-start | bytes 1572868
  2.7 13.6 %all-to-all-start = ((bf16[8,2,10240]{2,1,0:T(2,128)(2,1)}), bf16[8,2,10240]{2,1,0:T(2,128)(2,1)S(1)}, u32[]{:S(2)}, u32[]{:S(2)}) async-start(bf16[8,2,10240]{2,1,0:T(2,128)(2,1)} %reshape.189), calls=%async_computation | async-start | bytes 655360 | tf_op jit(solution)/shard_map/all_to_all | solution.py:124
  8.8 2.4 %copy-start.1 = (s32[8]{0:T(128)S(1)}, s32[8]{0:T(128)}, u32[]{:S(2)}) copy-start(s32[8]{0:T(128)} %param.17) | copy-start | bytes 100
  16.3 17.5 %all-to-all-start.2 = ((bf16[8,2,16384]{2,1,0:T(2,128)(2,1)}), bf16[8,2,16384]{2,1,0:T(2,128)(2,1)S(1)}, u32[]{:S(2)}, u32[]{:S(2)}) async-start(bf16[8,2,16384]{2,1,0:T(2,128)(2,1)} %reshape.193), calls=%async_computation.2 | async-start | bytes 1048576 | tf_op jit(solution)/shard_map/all_to_all | solution.py:123
  33.8 13.9 %all-to-all-start.1 = ((bf16[8,2,10240]{2,1,0:T(2,128)(2,1)}), bf16[8,2,10240]{2,1,0:T(2,128)(2,1)S(1)}, u32[]{:S(2)}, u32[]{:S(2)}) async-start(bf16[8,2,10240]{2,1,0:T(2,128)(2,1)} %reshape.191), calls=%async_computation.1 | async-start | bytes 655360 | tf_op jit(solution)/shard_map/all_to_all | solution.py:133
  41.3 11.9 %copy-start.6 = (bf16[256,512]{1,0:T(8,128)(2,1)S(1)}, bf16[256,512]{1,0:T(8,128)(2,1)}, u32[]{:S(2)}) copy-start(bf16[256,512]{1,0:T(8,128)(2,1)} %param.15) | copy-start | bytes 786436
  41.5 14.9 %copy-start.4 = (bf16[256,512]{1,0:T(8,128)(2,1)S(1)}, bf16[256,512]{1,0:T(8,128)(2,1)}, u32[]{:S(2)}) copy-start(bf16[256,512]{1,0:T(8,128)(2,1)} %param.14) | copy-start | bytes 786436
  47.7 69.9 %all-to-all-start.3 = ((bf16[8,2,16384]{2,1,0:T(2,128)(2,1)}), bf16[8,2,16384]{2,1,0:T(2,128)(2,1)}, u32[]{:S(2)}, u32[]{:S(2)}) async-start(bf16[8,2,16384]{2,1,0:T(2,128)(2,1)} %reshape.195), calls=%async_computation.3 | async-start | bytes 1048576 | tf_op jit(solution)/shard_map/all_to_all | solution.py:132
  53.3 18.6 %collective-permute-start.1 = (bf16[256,512]{0,1:T(8,128)(2,1)S(1)}, bf16[256,512]{0,1:T(8,128)(2,1)S(1)}, u32[]{:S(2)}, u32[]{:S(2)}) collective-permute-start(bf16[256,512]{0,1:T(8,128)(2,1)S(1)} %copy.56), channel_id=1, source_target_pairs={{0,2},{2,4},{4,6},{6,8},{8,10},{10,12},{12,14},{1,3},{3,5},{5,7},{... | collective-permute-start | bytes 786440 | tf_op jit(solution)/shard_map/ppermute | solution.py:17
  56.5 21.1 %collective-permute-start = (bf16[256,512]{1,0:T(8,128)(2,1)S(1)}, bf16[256,512]{1,0:T(8,128)(2,1)S(1)}, u32[]{:S(2)}, u32[]{:S(2)}) collective-permute-start(bf16[256,512]{1,0:T(8,128)(2,1)S(1)} %copy-done.4), channel_id=1, source_target_pairs={{0,2},{2,4},{4,6},{6,8},{8,10},{10,12},{12,14},{1,3},{3,5},{5,7},{... | collective-permute-start | bytes 786440 | tf_op jit(solution)/shard_map/ppermute | solution.py:17
  86.5 2.3 %copy-start.7 = (pred[256,256]{0,1:T(8,128)(4,1)S(1)}, pred[256,256]{0,1:T(8,128)(4,1)}, u32[]{:S(2)}) copy-start(pred[256,256]{0,1:T(8,128)(4,1)} %get-tuple-element.634) | copy-start | bytes 196612 | tf_op jit(solution)/shard_map/cond/branch_0_fun/while
  86.5 2.3 %copy-start.8 = (pred[256,256]{0,1:T(8,128)(4,1)S(1)}, pred[256,256]{0,1:T(8,128)(4,1)}, u32[]{:S(2)}) copy-start(pred[256,256]{0,1:T(8,128)(4,1)} %get-tuple-element.635) | copy-start | bytes 196612 | tf_op jit(solution)/shard_map/cond/branch_0_fun/while
  94.2 2.4 %copy-start.7 = (pred[256,256]{0,1:T(8,128)(4,1)S(1)}, pred[256,256]{0,1:T(8,128)(4,1)}, u32[]{:S(2)}) copy-start(pred[256,256]{0,1:T(8,128)(4,1)} %get-tuple-element.634) | copy-start | bytes 196612 | tf_op jit(solution)/shard_map/cond/branch_0_fun/while
  94.2 2.4 %copy-start.8 = (pred[256,256]{0,1:T(8,128)(4,1)S(1)}, pred[256,256]{0,1:T(8,128)(4,1)}, u32[]{:S(2)}) copy-start(pred[256,256]{0,1:T(8,128)(4,1)} %get-tuple-element.635) | copy-start | bytes 196612 | tf_op jit(solution)/shard_map/cond/branch_0_fun/while
  102.0 2.3 %copy-start.7 = (pred[256,256]{0,1:T(8,128)(4,1)S(1)}, pred[256,256]{0,1:T(8,128)(4,1)}, u32[]{:S(2)}) copy-start(pred[256,256]{0,1:T(8,128)(4,1)} %get-tuple-element.634) | copy-start | bytes 196612 | tf_op jit(solution)/shard_map/cond/branch_0_fun/while
  102.0 2.3 %copy-start.8 = (pred[256,256]{0,1:T(8,128)(4,1)S(1)}, pred[256,256]{0,1:T(8,128)(4,1)}, u32[]{:S(2)}) copy-start(pred[256,256]{0,1:T(8,128)(4,1)} %get-tuple-element.635) | copy-start | bytes 196612 | tf_op jit(solution)/shard_map/cond/branch_0_fun/while
  109.7 2.3 %copy-start.7 = (pred[256,256]{0,1:T(8,128)(4,1)S(1)}, pred[256,256]{0,1:T(8,128)(4,1)}, u32[]{:S(2)}) copy-start(pred[256,256]{0,1:T(8,128)(4,1)} %get-tuple-element.634) | copy-start | bytes 196612 | tf_op jit(solution)/shard_map/cond/branch_0_fun/while
  109.7 2.3 %copy-start.8 = (pred[256,256]{0,1:T(8,128)(4,1)S(1)}, pred[256,256]{0,1:T(8,128)(4,1)}, u32[]{:S(2)}) copy-start(pred[256,256]{0,1:T(8,128)(4,1)} %get-tuple-element.635) | copy-start | bytes 196612 | tf_op jit(solution)/shard_map/cond/branch_0_fun/while
  115.8 1.3 %copy-start.2 = (bf16[256,32,8,16]{0,3,2,1:T(8,128)(2,1)}, bf16[256,32,8,16]{0,3,2,1:T(8,128)(2,1)S(1)}, u32[]{:S(2)}) copy-start(bf16[256,32,8,16]{0,3,2,1:T(8,128)(2,1)S(1)} %get-tuple-element.647) | copy-start | bytes 6291460
  117.1 3.7 %copy-start.3 = (bf16[256,32,8,16]{0,3,2,1:T(8,128)(2,1)S(1)}, bf16[256,32,8,16]{0,3,2,1:T(8,128)(2,1)}, u32[]{:S(2)}) copy-start(bf16[256,32,8,16]{0,3,2,1:T(8,128)(2,1)} %copy-done.2) | copy-start | bytes 6291460
where the time goes:
time: 130 us; the launch traced here: 129 us
  local copies, waits for them, and re-layouts  36.8 us (28%)
  waiting for transfers between devices  36.3 us (28%)
  starting transfers between devices  28.7 us (22%)
  matrix products  18.4 us (14%)
  blocking collectives  4.46 us (3%)
  other arithmetic  3.8 us (3%)
    ppermute x2, waiting for transfers between devices, shifted(): return lax.ppermute(shard, axis, pairs)  17.9 us
    unnamed x25, local copies, waits for them, and re-layouts  13.6 us
    dot_general x4, matrix products, head_step(): jnp.einsum('tgs,sd->tgd', exp_terms.astype(jnp.bfloat16), value_head, pre...  10.8 us
    all_to_all x1, waiting for transfers between devices, body(): lax.all_to_all(down_cut, 'req', split_axis=1, concat_axis=0, tiled=True)  9.44 us
    dynamic_update_slice x4, local copies, waits for them, and re-layouts, head_step(): lax.dynamic_update_slice_in_dim(accum_out, head_out.reshape(row_count, qu...  9.28 us
    ppermute x2, starting transfers between devices, shifted(): return lax.ppermute(shard, axis, pairs)  6.18 us
    all_to_all x1, starting transfers between devices, body(): lax.all_to_all(up_rows, 'req', split_axis=0, concat_axis=0, tiled=True)  5.94 us
    all_to_all x1, starting transfers between devices, body(): lax.all_to_all(up_cut, 'req', split_axis=1, concat_axis=0, tiled=True)  5.58 us
  transfers between devices with their start and end apart: 6, of which 5 were waited for; matrix products, arithmetic and copies ran while one was open for 37% of the time, Pallas kernels for 0%

commit v1 on v0

v1 whole, which is shorter than its diff:
```python
import functools
import math

import jax
import jax.numpy as jnp
from jax import lax
from jax.experimental import pallas as pl
from jax.experimental.pallas import tpu as pltpu
from jax.sharding import PartitionSpec as P

QUERY_HEAD_COUNT = 64
KEY_VALUE_HEADS = 8
HEAD_SIZE = 128
ADAPTER_RANK = 64
GROUP = QUERY_HEAD_COUNT // KEY_VALUE_HEADS
EXP2_SCALE = math.log2(math.e) / math.sqrt(HEAD_SIZE)
VMEM_LIMIT = 32 << 20
MINOR_BOTH = (((1,), (1,)), ((), ()))
PLAIN = (((1,), (0,)), ((), ()))


def dot(lhs, rhs, dims=PLAIN):
    return lax.dot_general(lhs, rhs, dims, preferred_element_type=jnp.float32)


def swapped(shard, axis, mask):
    size = lax.axis_size(axis)
    return lax.ppermute(shard, axis, [(i, i ^ mask) for i in range(size)])


def attend_kernel(parity_ref, query_ref, key_ref, value_ref, far_key_ref, far_value_ref, context_ref):
    rows = key_ref.shape[0]
    ones = jnp.ones((rows, HEAD_SIZE), jnp.bfloat16)
    causal = lax.broadcasted_iota(jnp.int32, (rows, rows), 0) >= lax.broadcasted_iota(
        jnp.int32, (rows, rows), 1
    )

    def run(with_far):
        near_key = key_ref[...]
        near_value = jnp.concatenate([value_ref[...], ones], axis=1)
        if with_far:
            far_key = far_key_ref[...]
            far_value = jnp.concatenate([far_value_ref[...], ones], axis=1)
        for head in range(GROUP):
            columns = slice(head * HEAD_SIZE, (head + 1) * HEAD_SIZE)
            query = query_ref[:, columns]
            near = jnp.where(causal, dot(query, near_key, MINOR_BOTH), -1e30)
            peak = jnp.max(near, axis=1, keepdims=True)
            if with_far:
                far = dot(query, far_key, MINOR_BOTH)
                peak = jnp.maximum(peak, jnp.max(far, axis=1, keepdims=True))
            out = dot(jnp.exp2((near - peak) * EXP2_SCALE).astype(jnp.bfloat16), near_value)
            if with_far:
                out += dot(jnp.exp2((far - peak) * EXP2_SCALE).astype(jnp.bfloat16), far_value)
            context_ref[0, :, columns] = (out[:, :HEAD_SIZE] / out[:, HEAD_SIZE:]).astype(jnp.bfloat16)

    @pl.when(parity_ref[0] == 0)
    def _():
        run(False)

    @pl.when(parity_ref[0] != 0)
    def _():
        run(True)


def attend(parity, queries, keys, values, far_keys, far_values):
    rows, width = queries.shape
    kv_count = keys.shape[1] // HEAD_SIZE
    kv_spec = pl.BlockSpec((rows, HEAD_SIZE), lambda g: (0, g))
    pairs = 2 * rows * rows * width
    return pl.pallas_call(
        attend_kernel,
        grid=(kv_count,),
        in_specs=[
            pl.BlockSpec(memory_space=pltpu.SMEM),
            pl.BlockSpec((rows, GROUP * HEAD_SIZE), lambda g: (0, g)),
            kv_spec,
            kv_spec,
            kv_spec,
            kv_spec,
        ],
        out_specs=pl.BlockSpec((1, rows, GROUP * HEAD_SIZE), lambda g: (g, 0, 0)),
        out_shape=jax.ShapeDtypeStruct((kv_count, rows, GROUP * HEAD_SIZE), jnp.bfloat16),
        compiler_params=pltpu.CompilerParams(vmem_limit_bytes=VMEM_LIMIT),
        cost_estimate=pl.CostEstimate(
            flops=6 * pairs, bytes_accessed=4 * rows * width, transcendentals=pairs // HEAD_SIZE
        ),
        name="attend",
    )(parity, queries, keys, values, far_keys, far_values)


def rank_kernel(quarter_ref, context_ref, held_ref, got_ref, rank_ref):
    total = jnp.zeros(rank_ref.shape, jnp.float32)
    for part in range(4):
        panel_ref = held_ref if part < 2 else got_ref
        quarter = quarter_ref[part]
        for head in range(0, GROUP, 2):
            context = context_ref[quarter, :, head * HEAD_SIZE : (head + 2) * HEAD_SIZE]
            panel = jnp.concatenate(
                [panel_ref[part % 2, head], panel_ref[part % 2, head + 1]], axis=1
            )
            total += dot(context, panel, MINOR_BOTH)
    rank_ref[...] = total


def rank_of(quarters, context, held, got):
    rows = context.shape[1]
    whole = pl.BlockSpec(memory_space=pltpu.VMEM)
    return pl.pallas_call(
        rank_kernel,
        in_specs=[pl.BlockSpec(memory_space=pltpu.SMEM), whole, whole, whole],
        out_specs=whole,
        out_shape=jax.ShapeDtypeStruct((rows, ADAPTER_RANK), jnp.float32),
        compiler_params=pltpu.CompilerParams(vmem_limit_bytes=VMEM_LIMIT),
        name="rank_mix",
    )(quarters, context, held, got)


def delta_kernel(quarter_ref, near_ref, far_ref, held_ref, got_ref, out_ref):
    step = pl.program_id(0)
    rank = (near_ref[...] + far_ref[...]).astype(jnp.bfloat16)

    def emit(panel_ref):
        for at in range(2):

            @pl.when(step % 2 == at)
            def _():
                panel = jnp.concatenate([panel_ref[at, b] for b in range(panel_ref.shape[1])], axis=1)
                out_ref[...] = (2.0 * dot(rank, panel)).astype(jnp.bfloat16)

    @pl.when(step < 2)
    def _():
        emit(held_ref)

    @pl.when(step >= 2)
    def _():
        emit(got_ref)


def delta_of(quarters, near, far, held, got):
    rows = near.shape[0]
    wide = held.shape[1] * held.shape[3]
    whole = lambda shape: pl.BlockSpec(shape, lambda s, q: (0,) * len(shape))
    return pl.pallas_call(
        delta_kernel,
        grid_spec=pltpu.PrefetchScalarGridSpec(
            num_scalar_prefetch=1,
            grid=(4,),
            in_specs=[whole(near.shape), whole(far.shape), whole(held.shape), whole(got.shape)],
            out_specs=pl.BlockSpec((rows, wide), lambda s, q: (0, q[s])),
        ),
        out_shape=jax.ShapeDtypeStruct((rows, 4 * wide), jnp.bfloat16),
        compiler_params=pltpu.CompilerParams(vmem_limit_bytes=VMEM_LIMIT),
        name="delta",
    )(quarters, near, far, held, got)


def pick(index, cases):
    return lax.select_n(index.astype(jnp.int32), *cases)


def spread(blocks, me):
    count = blocks.shape[0] // 4
    cut = lambda quarter: lax.dynamic_slice_in_dim(blocks, quarter * count, count, 0)
    return [cut(me % 4)] + [swapped(cut((me ^ k) % 4), "req", k) for k in (1, 2, 3)]


def deliver(quarters, me, slots):
    chosen = lambda request: pick((slots[request] ^ me) & 3, quarters)
    request = me // 2
    near = chosen(request)
    came = [swapped(chosen(request ^ j), "req", 2 * j) for j in (1, 2, 3)]
    at_home = slots[request] // 4 == me // 4
    return jnp.stack([jnp.where(at_home, near, came[1]), jnp.where(at_home, came[0], came[2])])


def eight_way(context, me, down, up, slots):
    down_quarters = spread(down, me)
    up_quarters = spread(up, me)
    down_held = deliver(down_quarters, me, slots)
    up_held = deliver(up_quarters, me, slots)
    down_got = swapped(down_held, "req", 1)
    up_got = swapped(up_held, "req", 1)
    quarters = (me % 4) ^ jnp.array([0, 2, 1, 3], jnp.int32)
    rank = rank_of(quarters, context, down_held, down_got)
    return delta_of(quarters, rank, swapped(rank, "tp", 1), up_held, up_got)


def any_way(context, me, down, up, slots):
    partner_count = lax.axis_size("req")
    rows = context.shape[1]

    def exchanged(blocks):
        slot_count, block_count = blocks.shape[:2]
        tail = blocks.shape[2] // partner_count
        cut = blocks.reshape(slot_count, block_count, partner_count, tail, blocks.shape[3])
        cut = jnp.moveaxis(cut, 2, 1)
        library = lax.all_to_all(cut, "req", split_axis=1, concat_axis=0, tiled=True)[:, 0]
        wanted = jnp.take(library, slots[jnp.arange(partner_count) // 2], axis=0)
        return lax.all_to_all(wanted, "req", split_axis=0, concat_axis=0, tiled=True)

    down_all = exchanged(jnp.swapaxes(down, 2, 3))
    up_all = exchanged(jnp.swapaxes(up, 2, 3))
    flat = jnp.swapaxes(context, 0, 1).reshape(rows, down_all.shape[1], partner_count, down_all.shape[2])
    rank = jnp.einsum("thrp,rhpk->tk", flat, down_all, preferred_element_type=jnp.float32)
    rank = lax.psum(rank, "tp").astype(jnp.bfloat16)
    mixed = jnp.einsum("tk,rblk->tbrl", rank, up_all, preferred_element_type=jnp.float32)
    return (2.0 * mixed.reshape(rows, -1)).astype(jnp.bfloat16)


def body(
    projected_queries,
    projected_keys,
    projected_values,
    request_adapter,
    adapter_slot_table,
    adapter_down_factor,
    adapter_up_factor,
):
    me = lax.axis_index("req")
    far_keys = swapped(projected_keys, "req", 1)
    far_values = swapped(projected_values, "req", 1)
    context = attend(
        (me % 2).reshape(1), projected_queries, projected_keys, projected_values, far_keys, far_values
    )
    slots = adapter_slot_table[request_adapter]
    down = jnp.swapaxes(adapter_down_factor, 2, 3)
    up = jnp.swapaxes(adapter_up_factor, 1, 2)
    if lax.axis_size("req") == 8 and down.shape[0] == 1:
        return eight_way(context, me, down[0], up[0], slots)
    return any_way(context, me, down, up, slots)


def solution(mesh):
    placed = (
        P(("groups", "req"), "tp"),
        P(("groups", "req"), "tp"),
        P(("groups", "req"), "tp"),
        P("groups"),
        P("groups"),
        P(("groups", "req"), "tp", None, None),
        P(("groups", "req"), None, "tp", None),
    )
    return jax.shard_map(
        body, mesh=mesh, in_specs=placed, out_specs=P(("groups", "req"), "tp"), check_vma=False
    )
```

time: 130 us -> 60.3 us (0.46)
  the two profiles are of different devices: /device:TPU:17 before, /device:TPU:0 now
where the time goes in v1:
time: 60.3 us; the launch traced here: 60.1 us
  starting transfers between devices  29.3 us (49%)
  waiting for transfers between devices  12.1 us (20%)
  Pallas kernels  8.14 us (13%)
  between operations  5.59 us (9%)
  local copies, waits for them, and re-layouts  3.37 us (6%)
  other arithmetic  1.54 us (3%)
    ppermute x17, starting transfers between devices, swapped(): return lax.ppermute(shard, axis, [(i, i ^ mask) for i in range(size)])  29.3 us
    ppermute x17, waiting for transfers between devices, swapped(): return lax.ppermute(shard, axis, [(i, i ^ mask) for i in range(size)])  12.1 us
    pallas_call x1, Pallas kernels, attend(): pl.pallas_call(attend_kernel, grid=(kv_count,), in_specs=[pl.BlockSpec(me...  4.16 us
    pallas_call x1, Pallas kernels, delta_of(): pl.pallas_call(delta_kernel, grid_spec=pltpu.PrefetchScalarGridSpec(num_s...  2.77 us
    dynamic_slice x2, local copies, waits for them, and re-layouts, spread(): lax.dynamic_slice_in_dim(blocks, quarter * count, count, 0)  2.04 us
    pallas_call x1, Pallas kernels, rank_of(): pl.pallas_call(rank_kernel, in_specs=[pl.BlockSpec(memory_space=pltpu.SME...  1.22 us
  transfers between devices with their start and end apart: 17, of which 7 were waited for; matrix products, arithmetic and copies ran while one was open for 8% of the time, Pallas kernels for 9%

profile of v1, /device:TPU:0, one launch (start us, length us, event | category | flops | bytes accessed | tf_op | source)
XLA Modules:
  0.0 60.1 jit_solution(18286070758589877493)
XLA Ops:
  0.0 3.0 %collective-permute-start = (bf16[256,512]{1,0:T(8,128)(2,1)}, bf16[256,512]{1,0:T(8,128)(2,1)S(1)}, u32[]{:S(2)}, u32[]{:S(2)}) collective-permute-start(bf16[256,512]{1,0:T(8,128)(2,1)} %key_ref.1), channel_id=1, source_target_pairs={{0,2},{2,0},{4,6},{6,4},{8,10},{10,8},{12,14},{14,12},{1,3},{3,1},... | collective-permute-start | bytes 786440 | tf_op jit(solution)/shard_map/ppermute | solution.py:28
  3.0 0.1 collective-permute-start.1
  3.1 1.0 %dynamic-slice_bitcast_fusion.3 = (bf16[5,64,128]{2,1,0:T(8,128)(2,1)S(1)}, bf16[5,64,128]{2,1,0:T(8,128)(2,1)S(1)}, bf16[5,64,128]{2,1,0:T(8,128)(2,1)S(1)}) fusion(bf16[1,64,20,128]{3,1,2,0:T(8,128)(2,1)} %param.14, s32[]{:T(128)S(6)} %select_n.371, s32[]{:T(128)S(6)} %select_n.367, s32[]{:T(128)S(6)} %select_n.370), kind=kLoop, calls=%fused_computation.28 | loop fusion | bytes 491532 | tf_op jit(solution)/shard_map/dynamic_slice | solution.py:164
  4.1 2.0 %collective-permute-start.10 = (bf16[5,64,128]{2,1,0:T(8,128)(2,1)S(1)}, bf16[5,64,128]{2,1,0:T(8,128)(2,1)S(1)}, u32[]{:S(2)}, u32[]{:S(2)}) collective-permute-start(bf16[5,64,128]{2,1,0:T(8,128)(2,1)S(1)} %get-tuple-element.15), channel_id=1, source_target_pairs={{0,2},{2,0},{4,6},{6,4},{8,10},{10,8},{12,14},{14,12},{1,3},{3,1},... | collective-permute-start | bytes 245768 | tf_op jit(solution)/shard_map/ppermute | solution.py:28
  6.1 1.6 %collective-permute-start.11 = (bf16[5,64,128]{2,1,0:T(8,128)(2,1)S(1)}, bf16[5,64,128]{2,1,0:T(8,128)(2,1)S(1)}, u32[]{:S(2)}, u32[]{:S(2)}) collective-permute-start(bf16[5,64,128]{2,1,0:T(8,128)(2,1)S(1)} %get-tuple-element.16), channel_id=1, source_target_pairs={{0,4},{2,6},{4,0},{6,2},{8,12},{10,14},{12,8},{14,10},{1,5},{3,7},... | collective-permute-start | bytes 245768 | tf_op jit(solution)/shard_map/ppermute | solution.py:28
  7.7 0.7 %compare_select_fusion = s32[4]{0:T(128)S(1)} fusion(s32[4]{0:T(128)} %param.11), kind=kLoop, calls=%fused_computation.32 | loop fusion | flops 12 | bytes 32 | tf_op jit(solution)/shard_map/select_n | solution.py:226
  8.3 0.6 %gather_fusion = s32[4]{0:T(128)S(1)} fusion(s32[8]{0:T(128)S(1)} %copy-done, s32[1024]{0:T(1024)S(1)} %pad_clamp_fusion), kind=kCustom, calls=%fused_computation | custom fusion | bytes 48 | tf_op jit(solution)/shard_map/gather | solution.py:226
  9.0 0.7 %fusion.12 = (s32[1]{0:T(128)}, s32[1]{0:T(128)}, s32[1]{0:T(128)}, s32[1]{0:T(128)}) fusion(s32[4]{0:T(128)S(1)} %gather_fusion, s32[]{:T(128)S(6)} %select_n.331, s32[]{:T(128)S(6)} %select_n.342, s32[]{:T(128)S(6)} %select_n.311, s32[]{:T(128)S(6)} %select_n.352), kind=kLoop, calls=%fused_computation.34 | loop fusion | bytes 48 | tf_op jit(solution)/shard_map/dynamic_slice | solution.py:169
  15.1 0.7 %broadcast_xor_fusion.quarter_ref = s32[4]{0:T(128)S(1)} fusion(s32[4]{0:T(128)} %constant.106.clone, s32[]{:T(128)S(6)} %select_n.307), kind=kLoop, calls=%fused_computation.33 | loop fusion | flops 4 | bytes 36 | tf_op jit(solution)/shard_map/xor | solution.py:184
  15.8 1.1 %dynamic-slice_bitcast_fusion = (bf16[8,64,128]{2,1,0:T(8,128)(2,1)S(1)}, bf16[8,64,128]{2,1,0:T(8,128)(2,1)S(1)}, bf16[8,64,128]{2,1,0:T(8,128)(2,1)S(1)}) fusion(bf16[1,32,128,64]{2,3,1,0:T(8,128)(2,1)} %param.13, s32[]{:T(128)S(6)} %select_n.328, s32[]{:T(128)S(6)} %select_n.321, s32[]{:T(128)S(6)} %select_n.326), kind=kLoop, calls=%fused_computation.14 | loop fusion | bytes 786444 | tf_op jit(solution)/shard_map/dynamic_slice | solution.py:164
  16.8 1.8 %collective-permute-done.10 = bf16[5,64,128]{2,1,0:T(8,128)(2,1)S(1)} collective-permute-done((bf16[5,64,128]{2,1,0:T(8,128)(2,1)S(1)}, bf16[5,64,128]{2,1,0:T(8,128)(2,1)S(1)}, u32[]{:S(2)}, u32[]{:S(2)}) %collective-permute-start.10) | collective-permute-done | bytes 81952 | tf_op jit(solution)/shard_map/ppermute | solution.py:28
  18.7 1.7 %collective-permute-start.2 = (bf16[8,64,128]{2,1,0:T(8,128)(2,1)S(1)}, bf16[8,64,128]{2,1,0:T(8,128)(2,1)S(1)}, u32[]{:S(2)}, u32[]{:S(2)}) collective-permute-start(bf16[8,64,128]{2,1,0:T(8,128)(2,1)S(1)} %get-tuple-element.12), channel_id=1, source_target_pairs={{0,2},{2,0},{4,6},{6,4},{8,10},{10,8},{12,14},{14,12},{1,3},{3,1},... | collective-permute-start | bytes 393224 | tf_op jit(solution)/shard_map/ppermute | solution.py:28
  20.4 1.6 %collective-permute-start.3 = (bf16[8,64,128]{2,1,0:T(8,128)(2,1)S(1)}, bf16[8,64,128]{2,1,0:T(8,128)(2,1)S(1)}, u32[]{:S(2)}, u32[]{:S(2)}) collective-permute-start(bf16[8,64,128]{2,1,0:T(8,128)(2,1)S(1)} %get-tuple-element.13), channel_id=1, source_target_pairs={{0,4},{2,6},{4,0},{6,2},{8,12},{10,14},{12,8},{14,10},{1,5},{3,7},... | collective-permute-start | bytes 393224 | tf_op jit(solution)/shard_map/ppermute | solution.py:28
  22.0 0.2 collective-permute-start.4
  22.3 2.1 %collective-permute-done.2 = bf16[8,64,128]{2,1,0:T(8,128)(2,1)S(1)} collective-permute-done((bf16[8,64,128]{2,1,0:T(8,128)(2,1)S(1)}, bf16[8,64,128]{2,1,0:T(8,128)(2,1)S(1)}, u32[]{:S(2)}, u32[]{:S(2)}) %collective-permute-start.2) | collective-permute-done | bytes 131104 | tf_op jit(solution)/shard_map/ppermute | solution.py:28
  24.3 2.6 %collective-permute-start.13 = (bf16[5,64,128]{2,1,0:T(8,128)(2,1)S(1)}, bf16[5,64,128]{2,1,0:T(8,128)(2,1)S(1)}, u32[]{:S(2)}, u32[]{:S(2)}) collective-permute-start(bf16[5,64,128]{2,1,0:T(8,128)(2,1)S(1)} %fusion.9), channel_id=1, source_target_pairs={{0,8},{2,10},{4,12},{6,14},{8,0},{10,2},{12,4},{14,6},{1,9},{3,11}... | collective-permute-start | bytes 245768 | tf_op jit(solution)/shard_map/ppermute | solution.py:28
  26.9 1.9 %collective-permute-done.4 = bf16[8,64,128]{2,1,0:T(8,128)(2,1)S(1)} collective-permute-done((bf16[8,64,128]{2,1,0:T(8,128)(2,1)S(1)}, bf16[8,64,128]{2,1,0:T(8,128)(2,1)S(1)}, u32[]{:S(2)}, u32[]{:S(2)}) %collective-permute-start.4) | collective-permute-done | bytes 131104 | tf_op jit(solution)/shard_map/ppermute | solution.py:28
  28.8 3.4 %collective-permute-start.5 = (bf16[8,64,128]{2,1,0:T(8,128)(2,1)S(1)}, bf16[8,64,128]{2,1,0:T(8,128)(2,1)S(1)}, u32[]{:S(2)}, u32[]{:S(2)}) collective-permute-start(bf16[8,64,128]{2,1,0:T(8,128)(2,1)S(1)} %fusion.3), channel_id=1, source_target_pairs={{0,8},{2,10},{4,12},{6,14},{8,0},{10,2},{12,4},{14,6},{1,9},{3,11}... | collective-permute-start | bytes 393224 | tf_op jit(solution)/shard_map/ppermute | solution.py:28
  32.3 1.6 %collective-permute-start.14 = (bf16[5,64,128]{2,1,0:T(8,128)(2,1)S(1)}, bf16[5,64,128]{2,1,0:T(8,128)(2,1)S(1)}, u32[]{:S(2)}, u32[]{:S(2)}) collective-permute-start(bf16[5,64,128]{2,1,0:T(8,128)(2,1)S(1)} %get-tuple-element.10), channel_id=1, source_target_pairs={{0,4},{2,6},{4,0},{6,2},{8,12},{10,14},{12,8},{14,10},{1,5},{3,7},... | collective-permute-start | bytes 245768 | tf_op jit(solution)/shard_map/ppermute | solution.py:28
  33.9 3.8 %collective-permute-start.15 = (bf16[5,64,128]{2,1,0:T(8,128)(2,1)S(1)}, bf16[5,64,128]{2,1,0:T(8,128)(2,1)S(1)}, u32[]{:S(2)}, u32[]{:S(2)}) collective-permute-start(bf16[5,64,128]{2,1,0:T(8,128)(2,1)S(1)} %get-tuple-element.9), channel_id=1, source_target_pairs={{0,12},{2,14},{4,8},{6,10},{8,4},{10,6},{12,0},{14,2},{1,13},{3,15... | collective-permute-start | bytes 245768 | tf_op jit(solution)/shard_map/ppermute | solution.py:28
  37.6 0.9 %collective-permute-done.5 = bf16[8,64,128]{2,1,0:T(8,128)(2,1)S(1)} collective-permute-done((bf16[8,64,128]{2,1,0:T(8,128)(2,1)S(1)}, bf16[8,64,128]{2,1,0:T(8,128)(2,1)S(1)}, u32[]{:S(2)}, u32[]{:S(2)}) %collective-permute-start.5) | collective-permute-done | bytes 131104 | tf_op jit(solution)/shard_map/ppermute | solution.py:28
  38.6 0.2 collective-permute-start.6
  38.8 6.4 %collective-permute-start.7 = (bf16[8,64,128]{2,1,0:T(8,128)(2,1)S(1)}, bf16[8,64,128]{2,1,0:T(8,128)(2,1)S(1)}, u32[]{:S(2)}, u32[]{:S(2)}) collective-permute-start(bf16[8,64,128]{2,1,0:T(8,128)(2,1)S(1)} %get-tuple-element.6), channel_id=1, source_target_pairs={{0,12},{2,14},{4,8},{6,10},{8,4},{10,6},{12,0},{14,2},{1,13},{3,15... | collective-permute-start | bytes 393224 | tf_op jit(solution)/shard_map/ppermute | solution.py:28
  45.3 0.1 collective-permute-start.16
  45.4 2.8 %collective-permute-done.7 = bf16[8,64,128]{2,1,0:T(8,128)(2,1)S(1)} collective-permute-done((bf16[8,64,128]{2,1,0:T(8,128)(2,1)S(1)}, bf16[8,64,128]{2,1,0:T(8,128)(2,1)S(1)}, u32[]{:S(2)}, u32[]{:S(2)}) %collective-permute-start.7) | collective-permute-done | bytes 131104 | tf_op jit(solution)/shard_map/ppermute | solution.py:28
  48.2 1.0 %collective-permute-start.8 = (bf16[2,8,64,128]{3,2,1,0:T(8,128)(2,1)S(1)}, bf16[2,8,64,128]{3,2,1,0:T(8,128)(2,1)S(1)}, u32[]{:S(2)}, u32[]{:S(2)}) collective-permute-start(bf16[2,8,64,128]{3,2,1,0:T(8,128)(2,1)S(1)} %pad_maximum_fusion.held_ref), channel_id=1, source_target_pairs={{0,2},{2,0},{4,6},{6,4},{8,10},{10,8},{12,14},{14,12},{1,3},{3,1},... | collective-permute-start | bytes 786440 | tf_op jit(solution)/shard_map/ppermute | solution.py:28
  49.2 4.2 %attend.1.context_ref = bf16[4,256,1024]{2,1,0:T(8,128)(2,1)S(1)} custom-call(s32[1]{0:T(128)} %bitcast.parity_ref, bf16[256,4096]{1,0:T(8,128)(2,1)S(1)} %copy-done.1, bf16[256,512]{1,0:T(8,128)(2,1)S(1)} %copy-done.2, bf16[256,512]{1,0:T(8,128)(2,1)S(1)} %copy-done.3, bf16[256,512]{1,0:T(8,128)(2,1)S(1)} %collective-permute-done.far_key_ref, ...), custom_call_target="tpu_custom_call" | custom-call | flops 3221225472 | bytes 4194304 | tf_op jit(solution)/shard_map/attend/pallas_call | solution.py:71
  53.4 1.3 %collective-permute-done.8.got_ref = bf16[2,8,64,128]{3,2,1,0:T(8,128)(2,1)S(1)} collective-permute-done((bf16[2,8,64,128]{3,2,1,0:T(8,128)(2,1)S(1)}, bf16[2,8,64,128]{3,2,1,0:T(8,128)(2,1)S(1)}, u32[]{:S(2)}, u32[]{:S(2)}) %collective-permute-start.8) | collective-permute-done | bytes 262176 | tf_op jit(solution)/shard_map/ppermute | solution.py:28
  54.7 1.2 %rank_mix.1.near_ref = f32[256,64]{1,0:T(8,128)S(1)} custom-call(s32[4]{0:T(128)S(1)} %broadcast_xor_fusion.quarter_ref, bf16[4,256,1024]{2,1,0:T(8,128)(2,1)S(1)} %attend.1.context_ref, bf16[2,8,64,128]{3,2,1,0:T(8,128)(2,1)S(1)} %pad_maximum_fusion.held_ref, bf16[2,8,64,128]{3,2,1,0:T(8,128)(2,1)S(1)} %collective-permute-done.8.got_ref), custom_call_target="tpu_custom_call" | custom-call | tf_op jit(solution)/shard_map/rank_mix/pallas_call | solution.py:109
  55.9 0.1 collective-permute-start.9
  56.0 1.3 %collective-permute-done.9.far_ref = f32[256,64]{1,0:T(8,128)S(1)} collective-permute-done((f32[256,64]{1,0:T(8,128)S(1)}, f32[256,64]{1,0:T(8,128)S(1)}, u32[]{:S(2)}, u32[]{:S(2)}) %collective-permute-start.9) | collective-permute-done | bytes 65568 | tf_op jit(solution)/shard_map/ppermute | solution.py:28
  57.3 2.8 %delta.1 = bf16[256,2560]{1,0:T(8,128)(2,1)} custom-call(s32[4]{0:T(128)S(1)} %broadcast_xor_fusion.quarter_ref, f32[256,64]{1,0:T(8,128)S(1)} %rank_mix.1.near_ref, f32[256,64]{1,0:T(8,128)S(1)} %collective-permute-done.9.far_ref, bf16[2,5,64,128]{3,2,1,0:T(8,128)(2,1)S(1)} %pad_maximum_fusion.1.held_ref, ...), custom_call_target="tpu_custom_call" | custom-call | tf_op jit(solution)/shard_map/delta/pallas_call | solution.py:144
  (32 shorter events, 0.3 us)
Async XLA Ops:
  0.0 8.3 %copy-start = (s32[8]{0:T(128)S(1)}, s32[8]{0:T(128)}, u32[]{:S(2)}) copy-start(s32[8]{0:T(128)} %param.12) | copy-start | bytes 100
  0.0 22.2 %copy-start.5 = (bf16[1,64,20,128]{3,1,2,0:T(8,128)(2,1)S(1)}, bf16[1,64,20,128]{3,1,2,0:T(8,128)(2,1)}, u32[]{:S(2)}) copy-start(bf16[1,64,20,128]{3,1,2,0:T(8,128)(2,1)} %param.14) | copy-start | bytes 983044
  0.0 28.8 %copy-start.4 = (bf16[1,32,128,64]{2,3,1,0:T(8,128)(2,1)S(1)}, bf16[1,32,128,64]{2,3,1,0:T(8,128)(2,1)}, u32[]{:S(2)}) copy-start(bf16[1,32,128,64]{2,3,1,0:T(8,128)(2,1)} %param.13) | copy-start | bytes 1572868
  0.0 49.2 %collective-permute-start = (bf16[256,512]{1,0:T(8,128)(2,1)}, bf16[256,512]{1,0:T(8,128)(2,1)S(1)}, u32[]{:S(2)}, u32[]{:S(2)}) collective-permute-start(bf16[256,512]{1,0:T(8,128)(2,1)} %key_ref.1), channel_id=1, source_target_pairs={{0,2},{2,0},{4,6},{6,4},{8,10},{10,8},{12,14},{14,12},{1,3},{3,1},... | collective-permute-start | bytes 786440 | tf_op jit(solution)/shard_map/ppermute | solution.py:28
  3.0 46.2 %collective-permute-start.1 = (bf16[256,512]{1,0:T(8,128)(2,1)}, bf16[256,512]{1,0:T(8,128)(2,1)S(1)}, u32[]{:S(2)}, u32[]{:S(2)}) collective-permute-start(bf16[256,512]{1,0:T(8,128)(2,1)} %value_ref.1), channel_id=1, source_target_pairs={{0,2},{2,0},{4,6},{6,4},{8,10},{10,8},{12,14},{14,12},{1,3},{3,1},... | collective-permute-start | bytes 786440 | tf_op jit(solution)/shard_map/ppermute | solution.py:28
  4.1 14.6 %collective-permute-start.10 = (bf16[5,64,128]{2,1,0:T(8,128)(2,1)S(1)}, bf16[5,64,128]{2,1,0:T(8,128)(2,1)S(1)}, u32[]{:S(2)}, u32[]{:S(2)}) collective-permute-start(bf16[5,64,128]{2,1,0:T(8,128)(2,1)S(1)} %get-tuple-element.15), channel_id=1, source_target_pairs={{0,2},{2,0},{4,6},{6,4},{8,10},{10,8},{12,14},{14,12},{1,3},{3,1},... | collective-permute-start | bytes 245768 | tf_op jit(solution)/shard_map/ppermute | solution.py:28
  6.1 14.3 %collective-permute-start.11 = (bf16[5,64,128]{2,1,0:T(8,128)(2,1)S(1)}, bf16[5,64,128]{2,1,0:T(8,128)(2,1)S(1)}, u32[]{:S(2)}, u32[]{:S(2)}) collective-permute-start(bf16[5,64,128]{2,1,0:T(8,128)(2,1)S(1)} %get-tuple-element.16), channel_id=1, source_target_pairs={{0,4},{2,6},{4,0},{6,2},{8,12},{10,14},{12,8},{14,10},{1,5},{3,7},... | collective-permute-start | bytes 245768 | tf_op jit(solution)/shard_map/ppermute | solution.py:28
  7.7 14.3 %collective-permute-start.12 = (bf16[5,64,128]{2,1,0:T(8,128)(2,1)S(1)}, bf16[5,64,128]{2,1,0:T(8,128)(2,1)S(1)}, u32[]{:S(2)}, u32[]{:S(2)}) collective-permute-start(bf16[5,64,128]{2,1,0:T(8,128)(2,1)S(1)} %get-tuple-element.14), channel_id=1, source_target_pairs={{0,6},{2,4},{4,2},{6,0},{8,14},{10,12},{12,10},{14,8},{1,7},{3,5},... | collective-permute-start | bytes 245768 | tf_op jit(solution)/shard_map/ppermute | solution.py:28
  18.7 5.7 %collective-permute-start.2 = (bf16[8,64,128]{2,1,0:T(8,128)(2,1)S(1)}, bf16[8,64,128]{2,1,0:T(8,128)(2,1)S(1)}, u32[]{:S(2)}, u32[]{:S(2)}) collective-permute-start(bf16[8,64,128]{2,1,0:T(8,128)(2,1)S(1)} %get-tuple-element.12), channel_id=1, source_target_pairs={{0,2},{2,0},{4,6},{6,4},{8,10},{10,8},{12,14},{14,12},{1,3},{3,1},... | collective-permute-start | bytes 393224 | tf_op jit(solution)/shard_map/ppermute | solution.py:28
  20.4 6.5 %collective-permute-start.3 = (bf16[8,64,128]{2,1,0:T(8,128)(2,1)S(1)}, bf16[8,64,128]{2,1,0:T(8,128)(2,1)S(1)}, u32[]{:S(2)}, u32[]{:S(2)}) collective-permute-start(bf16[8,64,128]{2,1,0:T(8,128)(2,1)S(1)} %get-tuple-element.13), channel_id=1, source_target_pairs={{0,4},{2,6},{4,0},{6,2},{8,12},{10,14},{12,8},{14,10},{1,5},{3,7},... | collective-permute-start | bytes 393224 | tf_op jit(solution)/shard_map/ppermute | solution.py:28
  22.0 27.2 %copy-start.1 = (bf16[256,4096]{1,0:T(8,128)(2,1)S(1)}, bf16[256,4096]{1,0:T(8,128)(2,1)}, u32[]{:S(2)}) copy-start(bf16[256,4096]{1,0:T(8,128)(2,1)} %query_ref.1) | copy-start | bytes 6291460
  22.0 27.2 %copy-start.2 = (bf16[256,512]{1,0:T(8,128)(2,1)S(1)}, bf16[256,512]{1,0:T(8,128)(2,1)}, u32[]{:S(2)}) copy-start(bf16[256,512]{1,0:T(8,128)(2,1)} %key_ref.1) | copy-start | bytes 786436
  22.0 27.2 %copy-start.3 = (bf16[256,512]{1,0:T(8,128)(2,1)S(1)}, bf16[256,512]{1,0:T(8,128)(2,1)}, u32[]{:S(2)}) copy-start(bf16[256,512]{1,0:T(8,128)(2,1)} %value_ref.1) | copy-start | bytes 786436
  22.0 6.8 %collective-permute-start.4 = (bf16[8,64,128]{2,1,0:T(8,128)(2,1)S(1)}, bf16[8,64,128]{2,1,0:T(8,128)(2,1)S(1)}, u32[]{:S(2)}, u32[]{:S(2)}) collective-permute-start(bf16[8,64,128]{2,1,0:T(8,128)(2,1)S(1)} %get-tuple-element.11), channel_id=1, source_target_pairs={{0,6},{2,4},{4,2},{6,0},{8,14},{10,12},{12,10},{14,8},{1,7},{3,5},... | collective-permute-start | bytes 393224 | tf_op jit(solution)/shard_map/ppermute | solution.py:28
  24.3 7.9 %collective-permute-start.13 = (bf16[5,64,128]{2,1,0:T(8,128)(2,1)S(1)}, bf16[5,64,128]{2,1,0:T(8,128)(2,1)S(1)}, u32[]{:S(2)}, u32[]{:S(2)}) collective-permute-start(bf16[5,64,128]{2,1,0:T(8,128)(2,1)S(1)} %fusion.9), channel_id=1, source_target_pairs={{0,8},{2,10},{4,12},{6,14},{8,0},{10,2},{12,4},{14,6},{1,9},{3,11}... | collective-permute-start | bytes 245768 | tf_op jit(solution)/shard_map/ppermute | solution.py:28
  28.8 9.7 %collective-permute-start.5 = (bf16[8,64,128]{2,1,0:T(8,128)(2,1)S(1)}, bf16[8,64,128]{2,1,0:T(8,128)(2,1)S(1)}, u32[]{:S(2)}, u32[]{:S(2)}) collective-permute-start(bf16[8,64,128]{2,1,0:T(8,128)(2,1)S(1)} %fusion.3), channel_id=1, source_target_pairs={{0,8},{2,10},{4,12},{6,14},{8,0},{10,2},{12,4},{14,6},{1,9},{3,11}... | collective-permute-start | bytes 393224 | tf_op jit(solution)/shard_map/ppermute | solution.py:28
  32.3 6.5 %collective-permute-start.14 = (bf16[5,64,128]{2,1,0:T(8,128)(2,1)S(1)}, bf16[5,64,128]{2,1,0:T(8,128)(2,1)S(1)}, u32[]{:S(2)}, u32[]{:S(2)}) collective-permute-start(bf16[5,64,128]{2,1,0:T(8,128)(2,1)S(1)} %get-tuple-element.10), channel_id=1, source_target_pairs={{0,4},{2,6},{4,0},{6,2},{8,12},{10,14},{12,8},{14,10},{1,5},{3,7},... | collective-permute-start | bytes 245768 | tf_op jit(solution)/shard_map/ppermute | solution.py:28
  33.9 11.4 %collective-permute-start.15 = (bf16[5,64,128]{2,1,0:T(8,128)(2,1)S(1)}, bf16[5,64,128]{2,1,0:T(8,128)(2,1)S(1)}, u32[]{:S(2)}, u32[]{:S(2)}) collective-permute-start(bf16[5,64,128]{2,1,0:T(8,128)(2,1)S(1)} %get-tuple-element.9), channel_id=1, source_target_pairs={{0,12},{2,14},{4,8},{6,10},{8,4},{10,6},{12,0},{14,2},{1,13},{3,15... | collective-permute-start | bytes 245768 | tf_op jit(solution)/shard_map/ppermute | solution.py:28
  38.6 6.8 %collective-permute-start.6 = (bf16[8,64,128]{2,1,0:T(8,128)(2,1)S(1)}, bf16[8,64,128]{2,1,0:T(8,128)(2,1)S(1)}, u32[]{:S(2)}, u32[]{:S(2)}) collective-permute-start(bf16[8,64,128]{2,1,0:T(8,128)(2,1)S(1)} %get-tuple-element.7), channel_id=1, source_target_pairs={{0,4},{2,6},{4,0},{6,2},{8,12},{10,14},{12,8},{14,10},{1,5},{3,7},... | collective-permute-start | bytes 393224 | tf_op jit(solution)/shard_map/ppermute | solution.py:28
  38.8 9.4 %collective-permute-start.7 = (bf16[8,64,128]{2,1,0:T(8,128)(2,1)S(1)}, bf16[8,64,128]{2,1,0:T(8,128)(2,1)S(1)}, u32[]{:S(2)}, u32[]{:S(2)}) collective-permute-start(bf16[8,64,128]{2,1,0:T(8,128)(2,1)S(1)} %get-tuple-element.6), channel_id=1, source_target_pairs={{0,12},{2,14},{4,8},{6,10},{8,4},{10,6},{12,0},{14,2},{1,13},{3,15... | collective-permute-start | bytes 393224 | tf_op jit(solution)/shard_map/ppermute | solution.py:28
  45.3 10.7 %collective-permute-start.16 = (bf16[2,5,64,128]{3,2,1,0:T(8,128)(2,1)S(1)}, bf16[2,5,64,128]{3,2,1,0:T(8,128)(2,1)S(1)}, u32[]{:S(2)}, u32[]{:S(2)}) collective-permute-start(bf16[2,5,64,128]{3,2,1,0:T(8,128)(2,1)S(1)} %pad_maximum_fusion.1.held_ref), channel_id=1, source_target_pairs={{0,2},{2,0},{4,6},{6,4},{8,10},{10,8},{12,14},{14,12},{1,3},{3,1},... | collective-permute-start | bytes 491528 | tf_op jit(solution)/shard_map/ppermute | solution.py:28
  48.2 6.4 %collective-permute-start.8 = (bf16[2,8,64,128]{3,2,1,0:T(8,128)(2,1)S(1)}, bf16[2,8,64,128]{3,2,1,0:T(8,128)(2,1)S(1)}, u32[]{:S(2)}, u32[]{:S(2)}) collective-permute-start(bf16[2,8,64,128]{3,2,1,0:T(8,128)(2,1)S(1)} %pad_maximum_fusion.held_ref), channel_id=1, source_target_pairs={{0,2},{2,0},{4,6},{6,4},{8,10},{10,8},{12,14},{14,12},{1,3},{3,1},... | collective-permute-start | bytes 786440 | tf_op jit(solution)/shard_map/ppermute | solution.py:28
  55.9 1.4 %collective-permute-start.9 = (f32[256,64]{1,0:T(8,128)S(1)}, f32[256,64]{1,0:T(8,128)S(1)}, u32[]{:S(2)}, u32[]{:S(2)}) collective-permute-start(f32[256,64]{1,0:T(8,128)S(1)} %rank_mix.1.near_ref), channel_id=1, source_target_pairs={{0,1},{1,0},{2,3},{3,2},{4,5},{5,4},{6,7},{7,6},{8,9},{9,8},{10,11... | collective-permute-start | bytes 196616 | tf_op jit(solution)/shard_map/ppermute | solution.py:28

commit v2 on v1

v2 whole, which is shorter than its diff:
```python
import functools
import math

import jax
import jax.numpy as jnp
from jax import lax
from jax.experimental import pallas as pl
from jax.experimental.pallas import tpu as pltpu
from jax.sharding import PartitionSpec as P

QUERY_HEAD_COUNT = 64
KEY_VALUE_HEADS = 8
HEAD_SIZE = 128
ADAPTER_RANK = 64
GROUP = QUERY_HEAD_COUNT // KEY_VALUE_HEADS
EXP2_SCALE = math.log2(math.e) / math.sqrt(HEAD_SIZE)
VMEM_LIMIT = 32 << 20
MINOR_BOTH = (((1,), (1,)), ((), ()))
PLAIN = (((1,), (0,)), ((), ()))


def dot(lhs, rhs, dims=PLAIN):
    return lax.dot_general(lhs, rhs, dims, preferred_element_type=jnp.float32)


def swapped(shard, axis, mask):
    size = lax.axis_size(axis)
    return lax.ppermute(shard, axis, [(i, i ^ mask) for i in range(size)])


def attend_kernel(query_ref, key_ref, value_ref, far_key_ref, far_value_ref, context_ref):
    rows = key_ref.shape[0]
    ones = jnp.ones((rows, HEAD_SIZE), jnp.bfloat16)
    causal = lax.broadcasted_iota(jnp.int32, (rows, rows), 0) >= lax.broadcasted_iota(
        jnp.int32, (rows, rows), 1
    )

    def run(with_far):
        near_key = key_ref[...]
        near_value = jnp.concatenate([value_ref[...], ones], axis=1)
        if with_far:
            far_key = far_key_ref[...]
            far_value = jnp.concatenate([far_value_ref[...], ones], axis=1)
        for head in range(GROUP):
            columns = slice(head * HEAD_SIZE, (head + 1) * HEAD_SIZE)
            query = query_ref[:, columns]
            near = jnp.where(causal, dot(query, near_key, MINOR_BOTH), -1e30)
            peak = jnp.max(near, axis=1, keepdims=True)
            if with_far:
                far = dot(query, far_key, MINOR_BOTH)
                peak = jnp.maximum(peak, jnp.max(far, axis=1, keepdims=True))
            out = dot(jnp.exp2((near - peak) * EXP2_SCALE).astype(jnp.bfloat16), near_value)
            if with_far:
                out += dot(jnp.exp2((far - peak) * EXP2_SCALE).astype(jnp.bfloat16), far_value)
            context_ref[0, :, columns] = (out[:, :HEAD_SIZE] / out[:, HEAD_SIZE:]).astype(jnp.bfloat16)

    parity = lax.axis_index("req") & 1

    @pl.when(parity == 0)
    def _():
        run(False)

    @pl.when(parity != 0)
    def _():
        run(True)


def attend(queries, keys, values, far_keys, far_values):
    rows, width = queries.shape
    kv_count = keys.shape[1] // HEAD_SIZE
    kv_spec = pl.BlockSpec((rows, HEAD_SIZE), lambda g: (0, g))
    pairs = 2 * rows * rows * width
    return pl.pallas_call(
        attend_kernel,
        grid=(kv_count,),
        in_specs=[
            pl.BlockSpec((rows, GROUP * HEAD_SIZE), lambda g: (0, g)),
            kv_spec,
            kv_spec,
            kv_spec,
            kv_spec,
        ],
        out_specs=pl.BlockSpec((1, rows, GROUP * HEAD_SIZE), lambda g: (g, 0, 0)),
        out_shape=jax.ShapeDtypeStruct((kv_count, rows, GROUP * HEAD_SIZE), jnp.bfloat16),
        compiler_params=pltpu.CompilerParams(vmem_limit_bytes=VMEM_LIMIT),
        cost_estimate=pl.CostEstimate(
            flops=6 * pairs, bytes_accessed=4 * rows * width, transcendentals=pairs // HEAD_SIZE
        ),
        name="attend",
    )(queries, keys, values, far_keys, far_values)


def in_vmem(kernel, name, out_shape, index_args, *arrays):
    return pl.pallas_call(
        kernel,
        in_specs=[pl.BlockSpec(memory_space=pltpu.SMEM)] * len(index_args)
        + [pl.BlockSpec(memory_space=pltpu.VMEM)] * len(arrays),
        out_specs=jax.tree.map(lambda _: pl.BlockSpec(memory_space=pltpu.VMEM), out_shape),
        out_shape=out_shape,
        compiler_params=pltpu.CompilerParams(vmem_limit_bytes=VMEM_LIMIT),
        name=name,
    )(*index_args, *arrays)


def slot_of(request, adapter_ref, table_ref):
    return table_ref[adapter_ref[request]]


def choose_kernel(adapter_ref, table_ref, *refs):
    me = lax.axis_index("req")
    for out, out_ref in enumerate(refs[4:]):
        wanted = (slot_of((me >> 1) ^ out, adapter_ref, table_ref) ^ me) & 3
        for k in range(4):

            @pl.when(wanted == k)
            def _():
                out_ref[...] = refs[k][...]


def assemble_kernel(adapter_ref, table_ref, *refs):
    me = lax.axis_index("req")
    home = (slot_of(me >> 1, adapter_ref, table_ref) ^ me) < 4

    @pl.when(home)
    def _():
        refs[4][0] = refs[0][...]
        refs[4][1] = refs[1][...]

    @pl.when(jnp.logical_not(home))
    def _():
        refs[4][0] = refs[2][...]
        refs[4][1] = refs[3][...]


def rank_kernel(adapter_ref, table_ref, context_ref, held_ref, got_ref, rank_ref):
    me = lax.axis_index("req")
    first = (slot_of(me >> 1, adapter_ref, table_ref) ^ me) & 3
    total = jnp.zeros(rank_ref.shape, jnp.float32)
    for part, bits in enumerate((0, 2, 1, 3)):
        panel_ref = held_ref if part < 2 else got_ref
        for head in range(0, GROUP, 2):
            context = context_ref[first ^ bits, :, head * HEAD_SIZE : (head + 2) * HEAD_SIZE]
            panel = jnp.concatenate(
                [panel_ref[part % 2, head], panel_ref[part % 2, head + 1]], axis=1
            )
            total += dot(context, panel, MINOR_BOTH)
    rank_ref[...] = total


def delta_kernel(adapter_ref, table_ref, near_ref, far_ref, held_ref, got_ref, out_ref, stage_ref, sems):
    me = lax.axis_index("req")
    first = (slot_of(me >> 1, adapter_ref, table_ref) ^ me) & 3
    rank = (near_ref[...] + far_ref[...]).astype(jnp.bfloat16)
    wide = stage_ref.shape[2]
    copies = []
    for part, bits in enumerate((0, 2, 1, 3)):
        panel_ref = held_ref if part < 2 else got_ref
        panel = jnp.concatenate(
            [panel_ref[part % 2, b] for b in range(panel_ref.shape[1])], axis=1
        )
        stage_ref[part] = (2.0 * dot(rank, panel)).astype(jnp.bfloat16)
        columns = pl.ds(pl.multiple_of((first ^ bits) * wide, HEAD_SIZE), wide)
        copy = pltpu.make_async_copy(stage_ref.at[part], out_ref.at[:, columns], sems.at[part])
        copy.start()
        copies.append(copy)
    for copy in copies:
        copy.wait()


def delta_of(index_args, near, far, held, got):
    rows = near.shape[0]
    wide = held.shape[1] * held.shape[3]
    return pl.pallas_call(
        delta_kernel,
        in_specs=[pl.BlockSpec(memory_space=pltpu.SMEM)] * 2
        + [pl.BlockSpec(memory_space=pltpu.VMEM)] * 4,
        out_specs=pl.BlockSpec(memory_space=pl.ANY),
        out_shape=jax.ShapeDtypeStruct((rows, 4 * wide), jnp.bfloat16),
        scratch_shapes=[pltpu.VMEM((4, rows, wide), jnp.bfloat16), pltpu.SemaphoreType.DMA((4,))],
        compiler_params=pltpu.CompilerParams(vmem_limit_bytes=VMEM_LIMIT),
        name="delta",
    )(*index_args, near, far, held, got)


def spread(blocks):
    count = blocks.shape[0] // 4
    cut = [blocks[k * count : (k + 1) * count] for k in range(4)]
    return cut[:1] + [swapped(cut[k], "req", k) for k in (1, 2, 3)]


def deliver(index_args, quarters):
    shape = jax.ShapeDtypeStruct(quarters[0].shape, quarters[0].dtype)
    near, *sent = in_vmem(choose_kernel, "choose", [shape] * 4, index_args, *quarters)
    came = [swapped(panel, "req", 2 * j) for j, panel in enumerate(sent, 1)]
    both = jax.ShapeDtypeStruct((2, *shape.shape), shape.dtype)
    return in_vmem(assemble_kernel, "assemble", both, index_args, near, *came)


def eight_way(context, down, up, index_args):
    down_quarters = spread(down)
    up_quarters = spread(up)
    down_held = deliver(index_args, down_quarters)
    up_held = deliver(index_args, up_quarters)
    down_got = swapped(down_held, "req", 1)
    up_got = swapped(up_held, "req", 1)
    rank_shape = jax.ShapeDtypeStruct((context.shape[1], ADAPTER_RANK), jnp.float32)
    rank = in_vmem(rank_kernel, "rank_mix", rank_shape, index_args, context, down_held, down_got)
    return delta_of(index_args, rank, swapped(rank, "tp", 1), up_held, up_got)


def any_way(context, down, up, slots):
    partner_count = lax.axis_size("req")
    rows = context.shape[1]

    def exchanged(blocks):
        slot_count, block_count = blocks.shape[:2]
        tail = blocks.shape[2] // partner_count
        cut = blocks.reshape(slot_count, block_count, partner_count, tail, blocks.shape[3])
        cut = jnp.moveaxis(cut, 2, 1)
        library = lax.all_to_all(cut, "req", split_axis=1, concat_axis=0, tiled=True)[:, 0]
        wanted = jnp.take(library, slots[jnp.arange(partner_count) // 2], axis=0)
        return lax.all_to_all(wanted, "req", split_axis=0, concat_axis=0, tiled=True)

    down_all = exchanged(jnp.swapaxes(down, 2, 3))
    up_all = exchanged(jnp.swapaxes(up, 2, 3))
    flat = jnp.swapaxes(context, 0, 1).reshape(rows, down_all.shape[1], partner_count, down_all.shape[2])
    rank = jnp.einsum("thrp,rhpk->tk", flat, down_all, preferred_element_type=jnp.float32)
    rank = lax.psum(rank, "tp").astype(jnp.bfloat16)
    mixed = jnp.einsum("tk,rblk->tbrl", rank, up_all, preferred_element_type=jnp.float32)
    return (2.0 * mixed.reshape(rows, -1)).astype(jnp.bfloat16)


def body(
    projected_queries,
    projected_keys,
    projected_values,
    request_adapter,
    adapter_slot_table,
    adapter_down_factor,
    adapter_up_factor,
):
    far_keys = swapped(projected_keys, "req", 1)
    far_values = swapped(projected_values, "req", 1)
    context = attend(projected_queries, projected_keys, projected_values, far_keys, far_values)
    down = jnp.swapaxes(adapter_down_factor, 2, 3)
    up = jnp.swapaxes(adapter_up_factor, 1, 2)
    if lax.axis_size("req") == 8 and down.shape[0] == 1:
        return eight_way(context, down[0], up[0], (request_adapter, adapter_slot_table))
    return any_way(context, down, up, adapter_slot_table[request_adapter])


def solution(mesh):
    placed = (
        P(("groups", "req"), "tp"),
        P(("groups", "req"), "tp"),
        P(("groups", "req"), "tp"),
        P("groups"),
        P("groups"),
        P(("groups", "req"), "tp", None, None),
        P(("groups", "req"), None, "tp", None),
    )
    return jax.shard_map(
        body, mesh=mesh, in_specs=placed, out_specs=P(("groups", "req"), "tp"), check_vma=False
    )
```

time: 60.3 us -> 53 us (0.88); the launches traced: 60.1 us -> 52 us
  starting transfers between devices: 29.3 us -> 23.5 us
  between operations: 5.59 us -> 0.15 us
  waiting for transfers between devices: 12.1 us -> 15.1 us
  Pallas kernels: 8.14 us -> 9.73 us
  other arithmetic: 1.54 us -> 0 us
    ppermute x17, starting transfers between devices: 29.3 us -> 23.5 us  [swapped(): return lax.ppermute(shard, axis, [(i, i ^ mask) for i in range(size)])]
    ppermute x17, waiting for transfers between devices: 12.1 us -> 15.1 us  [swapped(): return lax.ppermute(shard, axis, [(i, i ^ mask) for i in range(size)])]
    dynamic_slice x3 -> x0, local copies, waits for them, and re-layouts: 2.71 us -> none  [the longest x2 2.04 us: spread(): lax.dynamic_slice_in_dim(blocks, quarter * count, count, 0)]
    slice x0 -> x2, local copies, waits for them, and re-layouts: none -> 2.21 us  [spread(): cut = [blocks[k * count:(k + 1) * count] for k in range(4)]]
    pallas_call x3 -> x7, Pallas kernels: 8.14 us -> 9.73 us  [the longest x1 4.13 us: attend(): pl.pallas_call(attend_kernel, grid=(kv_count,), in_specs=[pl.BlockSpec((r...]
    unnamed x12 -> x14, local copies, waits for them, and re-layouts: 0.02 us -> 1.33 us
    select_n x3 -> x0, other arithmetic: 0.7 us -> none  [the longest x1 0.66 us: body(): slots = adapter_slot_table[request_adapter]]
    xor x1 -> x0, other arithmetic: 0.66 us -> none  [eight_way(): quarters = me % 4 ^ jnp.array([0, 2, 1, 3], jnp.int32)]
  transfers between devices with their start and end apart: 17 -> 17, of which waited for: 7 -> 7; matrix products, arithmetic and copies ran while one was open for 8% -> 2% of each run, Pallas kernels for 9% -> 15%
where the time goes in v2:
time: 53 us; the launch traced here: 52 us
  starting transfers between devices  23.5 us (44%)
  waiting for transfers between devices  15.1 us (28%)
  Pallas kernels  9.73 us (18%)
  local copies, waits for them, and re-layouts  3.55 us (7%)
    ppermute x17, starting transfers between devices, swapped(): return lax.ppermute(shard, axis, [(i, i ^ mask) for i in range(size)])  23.5 us
    ppermute x17, waiting for transfers between devices, swapped(): return lax.ppermute(shard, axis, [(i, i ^ mask) for i in range(size)])  15.1 us
    pallas_call x1, Pallas kernels, attend(): pl.pallas_call(attend_kernel, grid=(kv_count,), in_specs=[pl.BlockSpec((r...  4.13 us
    pallas_call x5, Pallas kernels, in_vmem(): pl.pallas_call(kernel, in_specs=[pl.BlockSpec(memory_space=pltpu.SMEM)] *...  3.73 us
    slice x2, local copies, waits for them, and re-layouts, spread(): cut = [blocks[k * count:(k + 1) * count] for k in range(4)]  2.21 us
    pallas_call x1, Pallas kernels, delta_of(): pl.pallas_call(delta_kernel, in_specs=[pl.BlockSpec(memory_space=pltpu.SM...  1.87 us
    unnamed x14, local copies, waits for them, and re-layouts  1.33 us
  transfers between devices with their start and end apart: 17, of which 7 were waited for; matrix products, arithmetic and copies ran while one was open for 2% of the time, Pallas kernels for 15%

profile of v2, /device:TPU:0, one launch (start us, length us, event | category | flops | bytes accessed | tf_op | source)
XLA Modules:
  0.0 52.0 jit_solution(10462457390317095219)
XLA Ops:
  0.0 1.1 %slice_bitcast_fusion.4 = (bf16[5,64,128]{2,1,0:T(8,128)(2,1)S(1)}, bf16[5,64,128]{2,1,0:T(8,128)(2,1)S(1)}, bf16[5,64,128]{2,1,0:T(8,128)(2,1)S(1)}, bf16[5,64,128]{2,1,0:T(8,128)(2,1)S(1)}) fusion(bf16[1,20,64,128]{3,2,1,0:T(8,128)(2,1)} %bitcast.19), kind=kLoop, calls=%fused_computation.4 | loop fusion | bytes 655360 | tf_op jit(solution)/shard_map/slice | solution.py:187
  1.1 3.0 %collective-permute-start.10 = (bf16[5,64,128]{2,1,0:T(8,128)(2,1)S(1)}, bf16[5,64,128]{2,1,0:T(8,128)(2,1)S(1)}, u32[]{:S(2)}, u32[]{:S(2)}) collective-permute-start(bf16[5,64,128]{2,1,0:T(8,128)(2,1)S(1)} %get-tuple-element.27), channel_id=1, source_target_pairs={{0,2},{2,0},{4,6},{6,4},{8,10},{10,8},{12,14},{14,12},{1,3},{3,1},... | collective-permute-start | bytes 245768 | tf_op jit(solution)/shard_map/ppermute | solution.py:28
  4.1 1.1 %slice_bitcast_fusion = (bf16[8,64,128]{2,1,0:T(8,128)(2,1)S(1)}, bf16[8,64,128]{2,1,0:T(8,128)(2,1)S(1)}, bf16[8,64,128]{2,1,0:T(8,128)(2,1)S(1)}, bf16[8,64,128]{2,1,0:T(8,128)(2,1)S(1)}) fusion(bf16[1,32,64,128]{3,2,1,0:T(8,128)(2,1)} %bitcast.18), kind=kLoop, calls=%fused_computation | loop fusion | bytes 1048576 | tf_op jit(solution)/shard_map/slice | solution.py:187
  5.3 2.1 %collective-permute-start.3 = (bf16[8,64,128]{2,1,0:T(8,128)(2,1)S(1)}, bf16[8,64,128]{2,1,0:T(8,128)(2,1)S(1)}, u32[]{:S(2)}, u32[]{:S(2)}) collective-permute-start(bf16[8,64,128]{2,1,0:T(8,128)(2,1)S(1)} %get-tuple-element.22), channel_id=1, source_target_pairs={{0,4},{2,6},{4,0},{6,2},{8,12},{10,14},{12,8},{14,10},{1,5},{3,7},... | collective-permute-start | bytes 393224 | tf_op jit(solution)/shard_map/ppermute | solution.py:28
  7.4 1.4 %collective-permute-start.4 = (bf16[8,64,128]{2,1,0:T(8,128)(2,1)S(1)}, bf16[8,64,128]{2,1,0:T(8,128)(2,1)S(1)}, u32[]{:S(2)}, u32[]{:S(2)}) collective-permute-start(bf16[8,64,128]{2,1,0:T(8,128)(2,1)S(1)} %get-tuple-element.21), channel_id=1, source_target_pairs={{0,6},{2,4},{4,2},{6,0},{8,14},{10,12},{12,10},{14,8},{1,7},{3,5},... | collective-permute-start | bytes 393224 | tf_op jit(solution)/shard_map/ppermute | solution.py:28
  8.8 1.6 %collective-permute-start.11 = (bf16[5,64,128]{2,1,0:T(8,128)(2,1)S(1)}, bf16[5,64,128]{2,1,0:T(8,128)(2,1)S(1)}, u32[]{:S(2)}, u32[]{:S(2)}) collective-permute-start(bf16[5,64,128]{2,1,0:T(8,128)(2,1)S(1)} %get-tuple-element.26), channel_id=1, source_target_pairs={{0,4},{2,6},{4,0},{6,2},{8,12},{10,14},{12,8},{14,10},{1,5},{3,7},... | collective-permute-start | bytes 245768 | tf_op jit(solution)/shard_map/ppermute | solution.py:28
  10.4 5.4 %collective-permute-done.11.refs_2_ = bf16[5,64,128]{2,1,0:T(8,128)(2,1)S(1)} collective-permute-done((bf16[5,64,128]{2,1,0:T(8,128)(2,1)S(1)}, bf16[5,64,128]{2,1,0:T(8,128)(2,1)S(1)}, u32[]{:S(2)}, u32[]{:S(2)}) %collective-permute-start.11) | collective-permute-done | bytes 81952 | tf_op jit(solution)/shard_map/ppermute | solution.py:28
  15.8 1.6 %collective-permute-start = (bf16[256,512]{1,0:T(8,128)(2,1)}, bf16[256,512]{1,0:T(8,128)(2,1)S(1)}, u32[]{:S(2)}, u32[]{:S(2)}) collective-permute-start(bf16[256,512]{1,0:T(8,128)(2,1)} %key_ref.1), channel_id=1, source_target_pairs={{0,2},{2,0},{4,6},{6,4},{8,10},{10,8},{12,14},{14,12},{1,3},{3,1},... | collective-permute-start | bytes 786440 | tf_op jit(solution)/shard_map/ppermute | solution.py:28
  17.4 0.4 collective-permute-done.12.refs_3_
  17.9 0.3 collective-permute-start.1
  18.2 0.7 %copy-done = s32[4]{0:T(128)S(1)} copy-done((s32[4]{0:T(128)S(1)}, s32[4]{0:T(128)}, u32[]{:S(2)}) %copy-start) | copy-done | bytes 40
  18.8 0.7 %copy-done.2 = s32[8]{0:T(128)S(1)} copy-done((s32[8]{0:T(128)S(1)}, s32[8]{0:T(128)}, u32[]{:S(2)}) %copy-start.2) | copy-done | bytes 56
  19.5 0.7 %choose.3 = (bf16[5,64,128]{2,1,0:T(8,128)(2,1)S(1)}, bf16[5,64,128]{2,1,0:T(8,128)(2,1)S(1)}, bf16[5,64,128]{2,1,0:T(8,128)(2,1)S(1)}, bf16[5,64,128]{2,1,0:T(8,128)(2,1)S(1)}) custom-call(s32[4]{0:T(128)S(1)} %copy-done, s32[8]{0:T(128)S(1)} %copy-done.2, bf16[5,64,128]{2,1,0:T(8,128)(2,1)S(1)} %get-tuple-element.28.refs_0_, ...), custom_call_target="tpu_custom_call" | custom-call | tf_op jit(solution)/shard_map/choose/pallas_call | solution.py:94
  20.2 1.8 %collective-permute-start.13 = (bf16[5,64,128]{2,1,0:T(8,128)(2,1)S(1)}, bf16[5,64,128]{2,1,0:T(8,128)(2,1)S(1)}, u32[]{:S(2)}, u32[]{:S(2)}) collective-permute-start(bf16[5,64,128]{2,1,0:T(8,128)(2,1)S(1)} %get-tuple-element.18), channel_id=1, source_target_pairs={{0,4},{2,6},{4,0},{6,2},{8,12},{10,14},{12,8},{14,10},{1,5},{3,7},... | collective-permute-start | bytes 245768 | tf_op jit(solution)/shard_map/ppermute | solution.py:28
  22.0 2.6 %collective-permute-start.14 = (bf16[5,64,128]{2,1,0:T(8,128)(2,1)S(1)}, bf16[5,64,128]{2,1,0:T(8,128)(2,1)S(1)}, u32[]{:S(2)}, u32[]{:S(2)}) collective-permute-start(bf16[5,64,128]{2,1,0:T(8,128)(2,1)S(1)} %get-tuple-element.19), channel_id=1, source_target_pairs={{0,8},{2,10},{4,12},{6,14},{8,0},{10,2},{12,4},{14,6},{1,9},{3,11}... | collective-permute-start | bytes 245768 | tf_op jit(solution)/shard_map/ppermute | solution.py:28
  24.6 0.3 collective-permute-start.15
  24.9 0.7 %choose.2 = (bf16[8,64,128]{2,1,0:T(8,128)(2,1)S(1)}, bf16[8,64,128]{2,1,0:T(8,128)(2,1)S(1)}, bf16[8,64,128]{2,1,0:T(8,128)(2,1)S(1)}, bf16[8,64,128]{2,1,0:T(8,128)(2,1)S(1)}) custom-call(s32[4]{0:T(128)S(1)} %copy-done, s32[8]{0:T(128)S(1)} %copy-done.2, bf16[8,64,128]{2,1,0:T(8,128)(2,1)S(1)} %get-tuple-element.24.refs_0_, ...), custom_call_target="tpu_custom_call" | custom-call | tf_op jit(solution)/shard_map/choose/pallas_call | solution.py:94
  25.6 1.7 %collective-permute-start.5 = (bf16[8,64,128]{2,1,0:T(8,128)(2,1)S(1)}, bf16[8,64,128]{2,1,0:T(8,128)(2,1)S(1)}, u32[]{:S(2)}, u32[]{:S(2)}) collective-permute-start(bf16[8,64,128]{2,1,0:T(8,128)(2,1)S(1)} %get-tuple-element.14), channel_id=1, source_target_pairs={{0,4},{2,6},{4,0},{6,2},{8,12},{10,14},{12,8},{14,10},{1,5},{3,7},... | collective-permute-start | bytes 393224 | tf_op jit(solution)/shard_map/ppermute | solution.py:28
  27.3 1.8 %collective-permute-done.14.refs_2_ = bf16[5,64,128]{2,1,0:T(8,128)(2,1)S(1)} collective-permute-done((bf16[5,64,128]{2,1,0:T(8,128)(2,1)S(1)}, bf16[5,64,128]{2,1,0:T(8,128)(2,1)S(1)}, u32[]{:S(2)}, u32[]{:S(2)}) %collective-permute-start.14) | collective-permute-done | bytes 81952 | tf_op jit(solution)/shard_map/ppermute | solution.py:28
  29.1 1.9 %collective-permute-start.6 = (bf16[8,64,128]{2,1,0:T(8,128)(2,1)S(1)}, bf16[8,64,128]{2,1,0:T(8,128)(2,1)S(1)}, u32[]{:S(2)}, u32[]{:S(2)}) collective-permute-start(bf16[8,64,128]{2,1,0:T(8,128)(2,1)S(1)} %get-tuple-element.15), channel_id=1, source_target_pairs={{0,8},{2,10},{4,12},{6,14},{8,0},{10,2},{12,4},{14,6},{1,9},{3,11}... | collective-permute-start | bytes 393224 | tf_op jit(solution)/shard_map/ppermute | solution.py:28
  31.0 0.8 %collective-permute-done.15.refs_3_ = bf16[5,64,128]{2,1,0:T(8,128)(2,1)S(1)} collective-permute-done((bf16[5,64,128]{2,1,0:T(8,128)(2,1)S(1)}, bf16[5,64,128]{2,1,0:T(8,128)(2,1)S(1)}, u32[]{:S(2)}, u32[]{:S(2)}) %collective-permute-start.15) | collective-permute-done | bytes 81952 | tf_op jit(solution)/shard_map/ppermute | solution.py:28
  31.8 1.8 %collective-permute-start.7 = (bf16[8,64,128]{2,1,0:T(8,128)(2,1)S(1)}, bf16[8,64,128]{2,1,0:T(8,128)(2,1)S(1)}, u32[]{:S(2)}, u32[]{:S(2)}) collective-permute-start(bf16[8,64,128]{2,1,0:T(8,128)(2,1)S(1)} %get-tuple-element.16), channel_id=1, source_target_pairs={{0,12},{2,14},{4,8},{6,10},{8,4},{10,6},{12,0},{14,2},{1,13},{3,15... | collective-permute-start | bytes 393224 | tf_op jit(solution)/shard_map/ppermute | solution.py:28
  33.6 0.6 %assemble.3.held_ref = bf16[2,5,64,128]{3,2,1,0:T(8,128)(2,1)S(1)} custom-call(s32[4]{0:T(128)S(1)} %copy-done, s32[8]{0:T(128)S(1)} %copy-done.2, bf16[5,64,128]{2,1,0:T(8,128)(2,1)S(1)} %get-tuple-element.17.refs_0_, bf16[5,64,128]{2,1,0:T(8,128)(2,1)S(1)} %collective-permute-done.13.refs_1_, bf16[5,64,128]{2,1,0:T(8,128)(2,1)S(1)} %collective-permute-done.14.refs_2_, ...), custom_call_target="tpu_custom_call" | custom-call | tf_op jit(solution)/shard_map/assemble/pallas_call | solution.py:94
  34.2 1.6 %collective-permute-start.16 = (bf16[2,5,64,128]{3,2,1,0:T(8,128)(2,1)S(1)}, bf16[2,5,64,128]{3,2,1,0:T(8,128)(2,1)S(1)}, u32[]{:S(2)}, u32[]{:S(2)}) collective-permute-start(bf16[2,5,64,128]{3,2,1,0:T(8,128)(2,1)S(1)} %assemble.3.held_ref), channel_id=1, source_target_pairs={{0,2},{2,0},{4,6},{6,4},{8,10},{10,8},{12,14},{14,12},{1,3},{3,1},... | collective-permute-start | bytes 491528 | tf_op jit(solution)/shard_map/ppermute | solution.py:28
  35.8 4.6 %collective-permute-done.6.refs_2_ = bf16[8,64,128]{2,1,0:T(8,128)(2,1)S(1)} collective-permute-done((bf16[8,64,128]{2,1,0:T(8,128)(2,1)S(1)}, bf16[8,64,128]{2,1,0:T(8,128)(2,1)S(1)}, u32[]{:S(2)}, u32[]{:S(2)}) %collective-permute-start.6) | collective-permute-done | bytes 131104 | tf_op jit(solution)/shard_map/ppermute | solution.py:28
  40.5 0.6 %assemble.2.held_ref = bf16[2,8,64,128]{3,2,1,0:T(8,128)(2,1)S(1)} custom-call(s32[4]{0:T(128)S(1)} %copy-done, s32[8]{0:T(128)S(1)} %copy-done.2, bf16[8,64,128]{2,1,0:T(8,128)(2,1)S(1)} %get-tuple-element.13.refs_0_, bf16[8,64,128]{2,1,0:T(8,128)(2,1)S(1)} %collective-permute-done.5.refs_1_, bf16[8,64,128]{2,1,0:T(8,128)(2,1)S(1)} %collective-permute-done.6.refs_2_, ...), custom_call_target="tpu_custom_call" | custom-call | tf_op jit(solution)/shard_map/assemble/pallas_call | solution.py:94
  41.1 1.6 %collective-permute-start.8 = (bf16[2,8,64,128]{3,2,1,0:T(8,128)(2,1)S(1)}, bf16[2,8,64,128]{3,2,1,0:T(8,128)(2,1)S(1)}, u32[]{:S(2)}, u32[]{:S(2)}) collective-permute-start(bf16[2,8,64,128]{3,2,1,0:T(8,128)(2,1)S(1)} %assemble.2.held_ref), channel_id=1, source_target_pairs={{0,2},{2,0},{4,6},{6,4},{8,10},{10,8},{12,14},{14,12},{1,3},{3,1},... | collective-permute-start | bytes 786440 | tf_op jit(solution)/shard_map/ppermute | solution.py:28
  42.7 4.1 %attend.1.context_ref = bf16[4,256,1024]{2,1,0:T(8,128)(2,1)S(1)} custom-call(bf16[256,4096]{1,0:T(8,128)(2,1)S(1)} %copy-done.4, bf16[256,512]{1,0:T(8,128)(2,1)S(1)} %copy-done.5, bf16[256,512]{1,0:T(8,128)(2,1)S(1)} %copy-done.6, bf16[256,512]{1,0:T(8,128)(2,1)S(1)} %collective-permute-done.far_key_ref, ...), custom_call_target="tpu_custom_call" | custom-call | flops 3221225472 | bytes 4194304 | tf_op jit(solution)/shard_map/attend/pallas_call | solution.py:73
  46.8 0.7 %collective-permute-done.8.got_ref = bf16[2,8,64,128]{3,2,1,0:T(8,128)(2,1)S(1)} collective-permute-done((bf16[2,8,64,128]{3,2,1,0:T(8,128)(2,1)S(1)}, bf16[2,8,64,128]{3,2,1,0:T(8,128)(2,1)S(1)}, u32[]{:S(2)}, u32[]{:S(2)}) %collective-permute-start.8) | collective-permute-done | bytes 262176 | tf_op jit(solution)/shard_map/ppermute | solution.py:28
  47.5 1.2 %rank_mix.1.near_ref = f32[256,64]{1,0:T(8,128)S(1)} custom-call(s32[4]{0:T(128)S(1)} %copy-done.1, s32[8]{0:T(128)S(1)} %copy-done.3, bf16[4,256,1024]{2,1,0:T(8,128)(2,1)S(1)} %attend.1.context_ref, bf16[2,8,64,128]{3,2,1,0:T(8,128)(2,1)S(1)} %assemble.2.held_ref, bf16[2,8,64,128]{3,2,1,0:T(8,128)(2,1)S(1)} %collective-permute-done.8.got_ref), custom_call_target="tpu_custom_call" | custom-call | tf_op jit(solution)/shard_map/rank_mix/pallas_call | solution.py:94
  48.8 1.3 %collective-permute-done.9.far_ref = f32[256,64]{1,0:T(8,128)S(1)} collective-permute-done((f32[256,64]{1,0:T(8,128)S(1)}, f32[256,64]{1,0:T(8,128)S(1)}, u32[]{:S(2)}, u32[]{:S(2)}) %collective-permute-start.9) | collective-permute-done | bytes 65568 | tf_op jit(solution)/shard_map/ppermute | solution.py:28
  50.2 1.9 %delta.1 = bf16[256,2560]{1,0:T(8,128)(2,1)} custom-call(s32[4]{0:T(128)S(1)} %copy-done.1, s32[8]{0:T(128)S(1)} %copy-done.3, f32[256,64]{1,0:T(8,128)S(1)} %rank_mix.1.near_ref, f32[256,64]{1,0:T(8,128)S(1)} %collective-permute-done.9.far_ref, bf16[2,5,64,128]{3,2,1,0:T(8,128)(2,1)S(1)} %assemble.3.held_ref, ...), custom_call_target="tpu_custom_call" | custom-call | tf_op jit(solution)/shard_map/delta/pallas_call | solution.py:173
  (25 shorter events, 0.2 us)
Async XLA Ops:
  0.0 42.7 %copy-start.5 = (bf16[256,512]{1,0:T(8,128)(2,1)S(1)}, bf16[256,512]{1,0:T(8,128)(2,1)}, u32[]{:S(2)}) copy-start(bf16[256,512]{1,0:T(8,128)(2,1)} %key_ref.1) | copy-start | bytes 786436
  0.0 42.7 %copy-start.6 = (bf16[256,512]{1,0:T(8,128)(2,1)S(1)}, bf16[256,512]{1,0:T(8,128)(2,1)}, u32[]{:S(2)}) copy-start(bf16[256,512]{1,0:T(8,128)(2,1)} %value_ref.1) | copy-start | bytes 786436
  1.1 9.3 %collective-permute-start.10 = (bf16[5,64,128]{2,1,0:T(8,128)(2,1)S(1)}, bf16[5,64,128]{2,1,0:T(8,128)(2,1)S(1)}, u32[]{:S(2)}, u32[]{:S(2)}) collective-permute-start(bf16[5,64,128]{2,1,0:T(8,128)(2,1)S(1)} %get-tuple-element.27), channel_id=1, source_target_pairs={{0,2},{2,0},{4,6},{6,4},{8,10},{10,8},{12,14},{14,12},{1,3},{3,1},... | collective-permute-start | bytes 245768 | tf_op jit(solution)/shard_map/ppermute | solution.py:28
  5.2 14.9 %collective-permute-start.2 = (bf16[8,64,128]{2,1,0:T(8,128)(2,1)S(1)}, bf16[8,64,128]{2,1,0:T(8,128)(2,1)S(1)}, u32[]{:S(2)}, u32[]{:S(2)}) collective-permute-start(bf16[8,64,128]{2,1,0:T(8,128)(2,1)S(1)} %get-tuple-element.23), channel_id=1, source_target_pairs={{0,2},{2,0},{4,6},{6,4},{8,10},{10,8},{12,14},{14,12},{1,3},{3,1},... | collective-permute-start | bytes 393224 | tf_op jit(solution)/shard_map/ppermute | solution.py:28
  5.3 16.7 %collective-permute-start.3 = (bf16[8,64,128]{2,1,0:T(8,128)(2,1)S(1)}, bf16[8,64,128]{2,1,0:T(8,128)(2,1)S(1)}, u32[]{:S(2)}, u32[]{:S(2)}) collective-permute-start(bf16[8,64,128]{2,1,0:T(8,128)(2,1)S(1)} %get-tuple-element.22), channel_id=1, source_target_pairs={{0,4},{2,6},{4,0},{6,2},{8,12},{10,14},{12,8},{14,10},{1,5},{3,7},... | collective-permute-start | bytes 393224 | tf_op jit(solution)/shard_map/ppermute | solution.py:28
  7.4 17.2 %collective-permute-start.4 = (bf16[8,64,128]{2,1,0:T(8,128)(2,1)S(1)}, bf16[8,64,128]{2,1,0:T(8,128)(2,1)S(1)}, u32[]{:S(2)}, u32[]{:S(2)}) collective-permute-start(bf16[8,64,128]{2,1,0:T(8,128)(2,1)S(1)} %get-tuple-element.21), channel_id=1, source_target_pairs={{0,6},{2,4},{4,2},{6,0},{8,14},{10,12},{12,10},{14,8},{1,7},{3,5},... | collective-permute-start | bytes 393224 | tf_op jit(solution)/shard_map/ppermute | solution.py:28
  8.8 7.0 %collective-permute-start.11 = (bf16[5,64,128]{2,1,0:T(8,128)(2,1)S(1)}, bf16[5,64,128]{2,1,0:T(8,128)(2,1)S(1)}, u32[]{:S(2)}, u32[]{:S(2)}) collective-permute-start(bf16[5,64,128]{2,1,0:T(8,128)(2,1)S(1)} %get-tuple-element.26), channel_id=1, source_target_pairs={{0,4},{2,6},{4,0},{6,2},{8,12},{10,14},{12,8},{14,10},{1,5},{3,7},... | collective-permute-start | bytes 245768 | tf_op jit(solution)/shard_map/ppermute | solution.py:28
  10.4 7.5 %collective-permute-start.12 = (bf16[5,64,128]{2,1,0:T(8,128)(2,1)S(1)}, bf16[5,64,128]{2,1,0:T(8,128)(2,1)S(1)}, u32[]{:S(2)}, u32[]{:S(2)}) collective-permute-start(bf16[5,64,128]{2,1,0:T(8,128)(2,1)S(1)} %get-tuple-element.25), channel_id=1, source_target_pairs={{0,6},{2,4},{4,2},{6,0},{8,14},{10,12},{12,10},{14,8},{1,7},{3,5},... | collective-permute-start | bytes 245768 | tf_op jit(solution)/shard_map/ppermute | solution.py:28
  15.8 26.9 %collective-permute-start = (bf16[256,512]{1,0:T(8,128)(2,1)}, bf16[256,512]{1,0:T(8,128)(2,1)S(1)}, u32[]{:S(2)}, u32[]{:S(2)}) collective-permute-start(bf16[256,512]{1,0:T(8,128)(2,1)} %key_ref.1), channel_id=1, source_target_pairs={{0,2},{2,0},{4,6},{6,4},{8,10},{10,8},{12,14},{14,12},{1,3},{3,1},... | collective-permute-start | bytes 786440 | tf_op jit(solution)/shard_map/ppermute | solution.py:28
  17.9 24.8 %collective-permute-start.1 = (bf16[256,512]{1,0:T(8,128)(2,1)}, bf16[256,512]{1,0:T(8,128)(2,1)S(1)}, u32[]{:S(2)}, u32[]{:S(2)}) collective-permute-start(bf16[256,512]{1,0:T(8,128)(2,1)} %value_ref.1), channel_id=1, source_target_pairs={{0,2},{2,0},{4,6},{6,4},{8,10},{10,8},{12,14},{14,12},{1,3},{3,1},... | collective-permute-start | bytes 786440 | tf_op jit(solution)/shard_map/ppermute | solution.py:28
  18.2 0.7 %copy-start = (s32[4]{0:T(128)S(1)}, s32[4]{0:T(128)}, u32[]{:S(2)}) copy-start(s32[4]{0:T(128)} %adapter_ref.11) | copy-start | bytes 52
  18.8 0.7 %copy-start.2 = (s32[8]{0:T(128)S(1)}, s32[8]{0:T(128)}, u32[]{:S(2)}) copy-start(s32[8]{0:T(128)} %table_ref.11) | copy-start | bytes 100
  19.5 23.2 %copy-start.4 = (bf16[256,4096]{1,0:T(8,128)(2,1)S(1)}, bf16[256,4096]{1,0:T(8,128)(2,1)}, u32[]{:S(2)}) copy-start(bf16[256,4096]{1,0:T(8,128)(2,1)} %query_ref.1) | copy-start | bytes 6291460
  20.2 5.4 %collective-permute-start.13 = (bf16[5,64,128]{2,1,0:T(8,128)(2,1)S(1)}, bf16[5,64,128]{2,1,0:T(8,128)(2,1)S(1)}, u32[]{:S(2)}, u32[]{:S(2)}) collective-permute-start(bf16[5,64,128]{2,1,0:T(8,128)(2,1)S(1)} %get-tuple-element.18), channel_id=1, source_target_pairs={{0,4},{2,6},{4,0},{6,2},{8,12},{10,14},{12,8},{14,10},{1,5},{3,7},... | collective-permute-start | bytes 245768 | tf_op jit(solution)/shard_map/ppermute | solution.py:28
  22.0 7.1 %collective-permute-start.14 = (bf16[5,64,128]{2,1,0:T(8,128)(2,1)S(1)}, bf16[5,64,128]{2,1,0:T(8,128)(2,1)S(1)}, u32[]{:S(2)}, u32[]{:S(2)}) collective-permute-start(bf16[5,64,128]{2,1,0:T(8,128)(2,1)S(1)} %get-tuple-element.19), channel_id=1, source_target_pairs={{0,8},{2,10},{4,12},{6,14},{8,0},{10,2},{12,4},{14,6},{1,9},{3,11}... | collective-permute-start | bytes 245768 | tf_op jit(solution)/shard_map/ppermute | solution.py:28
  24.6 7.2 %collective-permute-start.15 = (bf16[5,64,128]{2,1,0:T(8,128)(2,1)S(1)}, bf16[5,64,128]{2,1,0:T(8,128)(2,1)S(1)}, u32[]{:S(2)}, u32[]{:S(2)}) collective-permute-start(bf16[5,64,128]{2,1,0:T(8,128)(2,1)S(1)} %get-tuple-element.20), channel_id=1, source_target_pairs={{0,12},{2,14},{4,8},{6,10},{8,4},{10,6},{12,0},{14,2},{1,13},{3,15... | collective-permute-start | bytes 245768 | tf_op jit(solution)/shard_map/ppermute | solution.py:28
  25.6 8.6 %collective-permute-start.5 = (bf16[8,64,128]{2,1,0:T(8,128)(2,1)S(1)}, bf16[8,64,128]{2,1,0:T(8,128)(2,1)S(1)}, u32[]{:S(2)}, u32[]{:S(2)}) collective-permute-start(bf16[8,64,128]{2,1,0:T(8,128)(2,1)S(1)} %get-tuple-element.14), channel_id=1, source_target_pairs={{0,4},{2,6},{4,0},{6,2},{8,12},{10,14},{12,8},{14,10},{1,5},{3,7},... | collective-permute-start | bytes 393224 | tf_op jit(solution)/shard_map/ppermute | solution.py:28
  29.1 11.4 %collective-permute-start.6 = (bf16[8,64,128]{2,1,0:T(8,128)(2,1)S(1)}, bf16[8,64,128]{2,1,0:T(8,128)(2,1)S(1)}, u32[]{:S(2)}, u32[]{:S(2)}) collective-permute-start(bf16[8,64,128]{2,1,0:T(8,128)(2,1)S(1)} %get-tuple-element.15), channel_id=1, source_target_pairs={{0,8},{2,10},{4,12},{6,14},{8,0},{10,2},{12,4},{14,6},{1,9},{3,11}... | collective-permute-start | bytes 393224 | tf_op jit(solution)/shard_map/ppermute | solution.py:28
  31.8 8.7 %collective-permute-start.7 = (bf16[8,64,128]{2,1,0:T(8,128)(2,1)S(1)}, bf16[8,64,128]{2,1,0:T(8,128)(2,1)S(1)}, u32[]{:S(2)}, u32[]{:S(2)}) collective-permute-start(bf16[8,64,128]{2,1,0:T(8,128)(2,1)S(1)} %get-tuple-element.16), channel_id=1, source_target_pairs={{0,12},{2,14},{4,8},{6,10},{8,4},{10,6},{12,0},{14,2},{1,13},{3,15... | collective-permute-start | bytes 393224 | tf_op jit(solution)/shard_map/ppermute | solution.py:28
  34.2 14.6 %collective-permute-start.16 = (bf16[2,5,64,128]{3,2,1,0:T(8,128)(2,1)S(1)}, bf16[2,5,64,128]{3,2,1,0:T(8,128)(2,1)S(1)}, u32[]{:S(2)}, u32[]{:S(2)}) collective-permute-start(bf16[2,5,64,128]{3,2,1,0:T(8,128)(2,1)S(1)} %assemble.3.held_ref), channel_id=1, source_target_pairs={{0,2},{2,0},{4,6},{6,4},{8,10},{10,8},{12,14},{14,12},{1,3},{3,1},... | collective-permute-start | bytes 491528 | tf_op jit(solution)/shard_map/ppermute | solution.py:28
  41.0 6.5 %copy-start.1 = (s32[4]{0:T(128)S(1)}, s32[4]{0:T(128)}, u32[]{:S(2)}) copy-start(s32[4]{0:T(128)} %adapter_ref.11) | copy-start | bytes 52
  41.1 6.5 %copy-start.3 = (s32[8]{0:T(128)S(1)}, s32[8]{0:T(128)}, u32[]{:S(2)}) copy-start(s32[8]{0:T(128)} %table_ref.11) | copy-start | bytes 100
  41.1 6.4 %collective-permute-start.8 = (bf16[2,8,64,128]{3,2,1,0:T(8,128)(2,1)S(1)}, bf16[2,8,64,128]{3,2,1,0:T(8,128)(2,1)S(1)}, u32[]{:S(2)}, u32[]{:S(2)}) collective-permute-start(bf16[2,8,64,128]{3,2,1,0:T(8,128)(2,1)S(1)} %assemble.2.held_ref), channel_id=1, source_target_pairs={{0,2},{2,0},{4,6},{6,4},{8,10},{10,8},{12,14},{14,12},{1,3},{3,1},... | collective-permute-start | bytes 786440 | tf_op jit(solution)/shard_map/ppermute | solution.py:28
  48.8 1.4 %collective-permute-start.9 = (f32[256,64]{1,0:T(8,128)S(1)}, f32[256,64]{1,0:T(8,128)S(1)}, u32[]{:S(2)}, u32[]{:S(2)}) collective-permute-start(f32[256,64]{1,0:T(8,128)S(1)} %rank_mix.1.near_ref), channel_id=1, source_target_pairs={{0,1},{1,0},{2,3},{3,2},{4,5},{5,4},{6,7},{7,6},{8,9},{9,8},{10,11... | collective-permute-start | bytes 196616 | tf_op jit(solution)/shard_map/ppermute | solution.py:28

commit v3 on v2

v3 whole, which is shorter than its diff:
```python
import functools
import math

import jax
import jax.numpy as jnp
from jax import lax
from jax.experimental import pallas as pl
from jax.experimental.pallas import tpu as pltpu
from jax.sharding import PartitionSpec as P

QUERY_HEAD_COUNT = 64
KEY_VALUE_HEADS = 8
HEAD_SIZE = 128
ADAPTER_RANK = 64
GROUP = QUERY_HEAD_COUNT // KEY_VALUE_HEADS
EXP2_SCALE = math.log2(math.e) / math.sqrt(HEAD_SIZE)
VMEM_LIMIT = 32 << 20
MINOR_BOTH = (((1,), (1,)), ((), ()))
PLAIN = (((1,), (0,)), ((), ()))


def dot(lhs, rhs, dims=PLAIN):
    return lax.dot_general(lhs, rhs, dims, preferred_element_type=jnp.float32)


def swapped(shard, axis, mask):
    size = lax.axis_size(axis)
    return lax.ppermute(shard, axis, [(i, i ^ mask) for i in range(size)])


def attend_kernel(query_ref, key_ref, value_ref, far_ref, context_ref):
    rows = key_ref.shape[0]
    ones = jnp.ones((rows, HEAD_SIZE), jnp.bfloat16)
    causal = lax.broadcasted_iota(jnp.int32, (rows, rows), 0) >= lax.broadcasted_iota(
        jnp.int32, (rows, rows), 1
    )

    def run(with_far):
        for group in range(context_ref.shape[0]):
            own = slice(group * HEAD_SIZE, (group + 1) * HEAD_SIZE)
            near_key = key_ref[:, own]
            near_value = jnp.concatenate([value_ref[:, own], ones], axis=1)
            if with_far:
                far_key = far_ref[:, own]
                far_value = jnp.concatenate([far_ref[:, key_ref.shape[1] + group * HEAD_SIZE : key_ref.shape[1] + (group + 1) * HEAD_SIZE], ones], axis=1)
            for head in range(GROUP):
                at = (group * GROUP + head) * HEAD_SIZE
                query = query_ref[:, at : at + HEAD_SIZE]
                near = jnp.where(causal, dot(query, near_key, MINOR_BOTH), -1e30)
                peak = jnp.max(near, axis=1, keepdims=True)
                if with_far:
                    far = dot(query, far_key, MINOR_BOTH)
                    peak = jnp.maximum(peak, jnp.max(far, axis=1, keepdims=True))
                out = dot(jnp.exp2((near - peak) * EXP2_SCALE).astype(jnp.bfloat16), near_value)
                if with_far:
                    out += dot(jnp.exp2((far - peak) * EXP2_SCALE).astype(jnp.bfloat16), far_value)
                context = (out[:, :HEAD_SIZE] / out[:, HEAD_SIZE:]).astype(jnp.bfloat16)
                context_ref[group, :, head * HEAD_SIZE : (head + 1) * HEAD_SIZE] = context

    parity = lax.axis_index("req") & 1

    @pl.when(parity == 0)
    def _():
        run(False)

    @pl.when(parity != 0)
    def _():
        run(True)


def attend(queries, keys, values, far):
    rows, width = queries.shape
    shape = (keys.shape[1] // HEAD_SIZE, rows, GROUP * HEAD_SIZE)
    whole = jax.ShapeDtypeStruct(shape, jnp.bfloat16)
    return in_vmem(attend_kernel, "attend", whole, None, queries, keys, values, far)


def in_vmem(kernel, name, out_shape, slots, *arrays, weight=0):
    scalars = [] if slots is None else [slots]
    return pl.pallas_call(
        kernel,
        in_specs=[pl.BlockSpec(memory_space=pltpu.SMEM)] * len(scalars)
        + [pl.BlockSpec(memory_space=pltpu.VMEM)] * len(arrays),
        out_specs=jax.tree.map(lambda _: pl.BlockSpec(memory_space=pltpu.VMEM), out_shape),
        out_shape=out_shape,
        compiler_params=pltpu.CompilerParams(vmem_limit_bytes=VMEM_LIMIT),
        cost_estimate=pl.CostEstimate(flops=weight, bytes_accessed=weight // 100, transcendentals=0),
        name=name,
    )(*scalars, *arrays)


def slots_kernel(adapter_ref, table_ref, slots_ref):
    for request in range(slots_ref.shape[0]):
        slots_ref[request] = table_ref[adapter_ref[request]]


def slots_of(request_adapter, adapter_slot_table):
    return pl.pallas_call(
        slots_kernel,
        in_specs=[pl.BlockSpec(memory_space=pltpu.SMEM)] * 2,
        out_specs=pl.BlockSpec(memory_space=pltpu.SMEM),
        out_shape=jax.ShapeDtypeStruct(request_adapter.shape, jnp.int32),
        cost_estimate=pl.CostEstimate(flops=0, bytes_accessed=0, transcendentals=0),
        name="slots",
    )(request_adapter, adapter_slot_table)


def take(request, me, slots_ref, quarter_refs, out_ref, at, other=None):
    where = slots_ref[request] ^ me
    for k in range(4):

        @pl.when((where if other is not None else where & 3) == k)
        def _():
            out_ref[at] = quarter_refs[k][...]

    if other is not None:

        @pl.when(where >= 4)
        def _():
            out_ref[at] = other[...]


def cross_kernel(slots_ref, *refs):
    me = lax.axis_index("req")
    for at in range(2):
        take((me >> 1) ^ (2 + at), me, slots_ref, refs[:4], refs[4], at)


def settle_kernel(slots_ref, *refs):
    me = lax.axis_index("req")
    for at in range(2):
        request = (me >> 1) ^ at
        take(request, me, slots_ref, refs[:4], refs[5 + at], ..., refs[4].at[at])


def rank_kernel(slots_ref, context_ref, *refs):
    me = lax.axis_index("req")
    first = (slots_ref[me >> 1] ^ me) & 3
    total = jnp.zeros(refs[4].shape, jnp.float32)
    for k in range(4):
        for head in range(0, GROUP, 2):
            context = context_ref[first ^ k, :, head * HEAD_SIZE : (head + 2) * HEAD_SIZE]
            panel = jnp.concatenate([refs[k][head], refs[k][head + 1]], axis=1)
            total += dot(context, panel, MINOR_BOTH)
    refs[4][...] = total


def delta_kernel(slots_ref, near_ref, far_ref, *refs):
    out_ref, stage_ref, sems = refs[4:]
    me = lax.axis_index("req")
    first = (slots_ref[me >> 1] ^ me) & 3
    rank = (near_ref[...] + far_ref[...]).astype(jnp.bfloat16)
    wide = stage_ref.shape[2]
    copies = []
    for k in range(4):
        panel = jnp.concatenate([refs[k][b] for b in range(refs[k].shape[0])], axis=1)
        stage_ref[k] = (2.0 * dot(rank, panel)).astype(jnp.bfloat16)
        columns = pl.ds(pl.multiple_of((first ^ k) * wide, HEAD_SIZE), wide)
        copy = pltpu.make_async_copy(stage_ref.at[k], out_ref.at[:, columns], sems.at[k])
        copy.start()
        copies.append(copy)
    for copy in copies:
        copy.wait()


def delta_of(slots, near, far, panels):
    rows = near.shape[0]
    wide = panels[0].shape[0] * panels[0].shape[2]
    return pl.pallas_call(
        delta_kernel,
        in_specs=[pl.BlockSpec(memory_space=pltpu.SMEM)]
        + [pl.BlockSpec(memory_space=pltpu.VMEM)] * 6,
        out_specs=pl.BlockSpec(memory_space=pl.ANY),
        out_shape=jax.ShapeDtypeStruct((rows, 4 * wide), jnp.bfloat16),
        scratch_shapes=[pltpu.VMEM((4, rows, wide), jnp.bfloat16), pltpu.SemaphoreType.DMA((4,))],
        compiler_params=pltpu.CompilerParams(vmem_limit_bytes=VMEM_LIMIT),
        name="delta",
    )(slots, near, far, *panels)


def quarter_cut(blocks):
    count = blocks.shape[0] // 4
    return [blocks[k * count : (k + 1) * count] for k in range(4)]


def spread(cut):
    return cut[:1] + [swapped(cut[k], "req", k) for k in (1, 2, 3)]


def cross(slots, quarters, weight=0):
    shape = jax.ShapeDtypeStruct((2, *quarters[0].shape), quarters[0].dtype)
    return in_vmem(cross_kernel, "cross", shape, slots, *quarters, weight=weight)


def gather(slots, quarters, came):
    shape = jax.ShapeDtypeStruct(quarters[0].shape, quarters[0].dtype)
    near, aside = in_vmem(settle_kernel, "settle", [shape] * 2, slots, *quarters, came)
    return [near] + [swapped(panel, "req", k) for k, panel in ((1, near), (2, aside), (3, aside))]


def after(earlier, value):
    return lax.optimization_barrier((earlier, value))[1]


def eight_way(queries, keys, values, down, up, request_adapter, adapter_slot_table):
    slots = slots_of(request_adapter, adapter_slot_table)
    down_quarters = spread(quarter_cut(down))
    up_cut = quarter_cut(after(slots, up))
    far = swapped(jnp.concatenate(after(up_cut, (keys, values)), axis=1), "req", 1)
    down_sent = cross(slots, down_quarters, 3000000000)
    down_came = swapped(down_sent, "req", 4)
    up_quarters = spread(after(down_sent, up_cut))
    context = attend(queries, keys, values, far)
    down_panels = gather(slots, down_quarters, down_came)
    up_came = swapped(cross(slots, after(context, up_quarters)), "req", 4)
    up_panels = gather(slots, up_quarters, up_came)
    rank_shape = jax.ShapeDtypeStruct((context.shape[1], ADAPTER_RANK), jnp.float32)
    rank = in_vmem(rank_kernel, "rank_mix", rank_shape, slots, context, *down_panels)
    return delta_of(slots, rank, swapped(rank, "tp", 1), up_panels)


def any_way(context, down, up, slots):
    partner_count = lax.axis_size("req")
    rows = context.shape[1]

    def exchanged(blocks):
        slot_count, block_count = blocks.shape[:2]
        tail = blocks.shape[2] // partner_count
        cut = blocks.reshape(slot_count, block_count, partner_count, tail, blocks.shape[3])
        cut = jnp.moveaxis(cut, 2, 1)
        library = lax.all_to_all(cut, "req", split_axis=1, concat_axis=0, tiled=True)[:, 0]
        wanted = jnp.take(library, slots[jnp.arange(partner_count) // 2], axis=0)
        return lax.all_to_all(wanted, "req", split_axis=0, concat_axis=0, tiled=True)

    down_all = exchanged(jnp.swapaxes(down, 2, 3))
    up_all = exchanged(jnp.swapaxes(up, 2, 3))
    flat = jnp.swapaxes(context, 0, 1).reshape(rows, down_all.shape[1], partner_count, down_all.shape[2])
    rank = jnp.einsum("thrp,rhpk->tk", flat, down_all, preferred_element_type=jnp.float32)
    rank = lax.psum(rank, "tp").astype(jnp.bfloat16)
    mixed = jnp.einsum("tk,rblk->tbrl", rank, up_all, preferred_element_type=jnp.float32)
    return (2.0 * mixed.reshape(rows, -1)).astype(jnp.bfloat16)


def body(
    projected_queries,
    projected_keys,
    projected_values,
    request_adapter,
    adapter_slot_table,
    adapter_down_factor,
    adapter_up_factor,
):
    down = jnp.swapaxes(adapter_down_factor, 2, 3)
    up = jnp.swapaxes(adapter_up_factor, 1, 2)
    spans = (projected_queries, projected_keys, projected_values)
    if lax.axis_size("req") == 8 and down.shape[0] == 1:
        return eight_way(*spans, down[0], up[0], request_adapter, adapter_slot_table)
    far = swapped(jnp.concatenate(spans[1:], axis=1), "req", 1)
    return any_way(attend(*spans, far), down, up, adapter_slot_table[request_adapter])


def solution(mesh):
    placed = (
        P(("groups", "req"), "tp"),
        P(("groups", "req"), "tp"),
        P(("groups", "req"), "tp"),
        P("groups"),
        P("groups"),
        P(("groups", "req"), "tp", None, None),
        P(("groups", "req"), None, "tp", None),
    )
    return jax.shard_map(
        body, mesh=mesh, in_specs=placed, out_specs=P(("groups", "req"), "tp"), check_vma=False
    )
```

time: 53 us -> 48.7 us (0.919); the launches traced: 52 us -> 48.5 us
  waiting for transfers between devices: 15.1 us -> 8.93 us
  starting transfers between devices: 23.5 us -> 26.2 us
  other arithmetic: 0 us -> 1.07 us
  local copies, waits for them, and re-layouts: 3.55 us -> 2.83 us
    ppermute x17 -> x16, waiting for transfers between devices: 15.1 us -> 8.93 us  [swapped(): return lax.ppermute(shard, axis, [(i, i ^ mask) for i in range(size)])]
    pallas_call x1, Pallas kernels: 4.13 us -> 1.2 us  [slots_of(): pl.pallas_call(slots_kernel, in_specs=[pl.BlockSpec(memory_space=pltpu.SM...]
    ppermute x17 -> x16, starting transfers between devices: 23.5 us -> 26.2 us  [swapped(): return lax.ppermute(shard, axis, [(i, i ^ mask) for i in range(size)])]
    pallas_call x5 -> x6, Pallas kernels: 3.73 us -> 6.33 us  [in_vmem(): pl.pallas_call(kernel, in_specs=[pl.BlockSpec(memory_space=pltpu.SMEM)] *...]
    concatenate x0 -> x1, other arithmetic: none -> 1.07 us  [eight_way(): jnp.concatenate(after(up_cut, (keys, values)), axis=1)]
    unnamed x14 -> x8, local copies, waits for them, and re-layouts: 1.33 us -> 0.67 us
  transfers between devices with their start and end apart: 17 -> 16, of which waited for: 7 -> 7; matrix products, arithmetic and copies ran while one was open for 2% -> 4% of each run, Pallas kernels for 15% -> 16%
where the time goes in v3:
time: 48.7 us; the launch traced here: 48.5 us
  starting transfers between devices  26.2 us (54%)
  Pallas kernels  9.39 us (19%)
  waiting for transfers between devices  8.93 us (18%)
  local copies, waits for them, and re-layouts  2.83 us (6%)
  other arithmetic  1.07 us (2%)
    ppermute x16, starting transfers between devices, swapped(): return lax.ppermute(shard, axis, [(i, i ^ mask) for i in range(size)])  26.2 us
    ppermute x16, waiting for transfers between devices, swapped(): return lax.ppermute(shard, axis, [(i, i ^ mask) for i in range(size)])  8.93 us
    pallas_call x6, Pallas kernels, in_vmem(): pl.pallas_call(kernel, in_specs=[pl.BlockSpec(memory_space=pltpu.SMEM)] *...  6.33 us
    slice x2, local copies, waits for them, and re-layouts, quarter_cut(): return [blocks[k * count:(k + 1) * count] for k in range(4)]  2.16 us
    pallas_call x1, Pallas kernels, delta_of(): pl.pallas_call(delta_kernel, in_specs=[pl.BlockSpec(memory_space=pltpu.SM...  1.86 us
    pallas_call x1, Pallas kernels, slots_of(): pl.pallas_call(slots_kernel, in_specs=[pl.BlockSpec(memory_space=pltpu.SM...  1.2 us
    concatenate x1, other arithmetic, eight_way(): jnp.concatenate(after(up_cut, (keys, values)), axis=1)  1.07 us
  transfers between devices with their start and end apart: 16, of which 7 were waited for; matrix products, arithmetic and copies ran while one was open for 4% of the time, Pallas kernels for 16%

profile of v3, /device:TPU:0, one launch (start us, length us, event | category | flops | bytes accessed | tf_op | source)
XLA Modules:
  0.0 48.5 jit_solution(8006162106321684263)
XLA Ops:
  0.0 1.1 %slice_bitcast_fusion = (bf16[8,64,128]{2,1,0:T(8,128)(2,1)S(1)}, bf16[8,64,128]{2,1,0:T(8,128)(2,1)S(1)}, bf16[8,64,128]{2,1,0:T(8,128)(2,1)S(1)}, bf16[8,64,128]{2,1,0:T(8,128)(2,1)S(1)}) fusion(bf16[1,32,64,128]{3,2,1,0:T(8,128)(2,1)} %bitcast.12), kind=kLoop, calls=%fused_computation.1 | loop fusion | bytes 1048576 | tf_op jit(solution)/shard_map/slice | solution.py:183
  1.1 4.0 %collective-permute-start.3 = (bf16[8,64,128]{2,1,0:T(8,128)(2,1)S(1)}, bf16[8,64,128]{2,1,0:T(8,128)(2,1)S(1)}, u32[]{:S(2)}, u32[]{:S(2)}) collective-permute-start(bf16[8,64,128]{2,1,0:T(8,128)(2,1)S(1)} %get-tuple-element.35), channel_id=1, source_target_pairs={{0,6},{2,4},{4,2},{6,0},{8,14},{10,12},{12,10},{14,8},{1,7},{3,5},... | collective-permute-start | bytes 393224 | tf_op jit(solution)/shard_map/ppermute | solution.py:28
  5.1 0.4 collective-permute-start.2
  5.6 0.2 collective-permute-start.1
  5.8 1.2 %slots.1.slots_ref = s32[4]{0:T(128)} custom-call(s32[4]{0:T(128)} %adapter_ref.1, s32[8]{0:T(128)} %table_ref.1), custom_call_target="tpu_custom_call" | custom-call | tf_op jit(solution)/shard_map/slots/pallas_call | solution.py:98
  7.0 1.0 %fusion = (bf16[5,64,128]{2,1,0:T(8,128)(2,1)S(1)}, bf16[5,64,128]{2,1,0:T(8,128)(2,1)S(1)}, bf16[5,64,128]{2,1,0:T(8,128)(2,1)S(1)}, bf16[5,64,128]{2,1,0:T(8,128)(2,1)S(1)}) fusion(bf16[20,64,128]{2,1,0:T(8,128)(2,1)} %bitcast.13), kind=kLoop, calls=%fused_computation.5 | loop fusion | bytes 655360 | tf_op jit(solution)/shard_map/slice | solution.py:183
  8.0 1.1 %pad_maximum_fusion = bf16[256,1024]{1,0:T(8,128)(2,1)S(1)} fusion(bf16[256,512]{1,0:T(8,128)(2,1)} %value_ref.1, bf16[256,512]{1,0:T(8,128)(2,1)} %key_ref.1), kind=kLoop, calls=%fused_computation | loop fusion | flops 1048576 | bytes 1048576 | tf_op jit(solution)/shard_map/concatenate | solution.py:209
  9.1 1.9 %collective-permute-start = (bf16[256,1024]{1,0:T(8,128)(2,1)S(1)}, bf16[256,1024]{1,0:T(8,128)(2,1)S(1)}, u32[]{:S(2)}, u32[]{:S(2)}) collective-permute-start(bf16[256,1024]{1,0:T(8,128)(2,1)S(1)} %pad_maximum_fusion), channel_id=1, source_target_pairs={{0,2},{2,0},{4,6},{6,4},{8,10},{10,8},{12,14},{14,12},{1,3},{3,1},... | collective-permute-start | bytes 1572872 | tf_op jit(solution)/shard_map/ppermute | solution.py:28
  11.0 0.6 %collective-permute-done.2.refs_2_ = bf16[8,64,128]{2,1,0:T(8,128)(2,1)S(1)} collective-permute-done((bf16[8,64,128]{2,1,0:T(8,128)(2,1)S(1)}, bf16[8,64,128]{2,1,0:T(8,128)(2,1)S(1)}, u32[]{:S(2)}, u32[]{:S(2)}) %collective-permute-start.2) | collective-permute-done | bytes 131104 | tf_op jit(solution)/shard_map/ppermute | solution.py:28
  11.8 0.7 %copy-done.3 = s32[4]{0:T(128)S(1)} copy-done((s32[4]{0:T(128)S(1)}, s32[4]{0:T(128)}, u32[]{:S(2)}) %copy-start.3) | copy-done | bytes 40
  12.5 0.6 %cross.2 = bf16[2,8,64,128]{3,2,1,0:T(8,128)(2,1)S(1)} custom-call(s32[4]{0:T(128)S(1)} %copy-done.3, bf16[8,64,128]{2,1,0:T(8,128)(2,1)S(1)} %get-tuple-element.38.refs_0_, bf16[8,64,128]{2,1,0:T(8,128)(2,1)S(1)} %collective-permute-done.1.refs_1_, bf16[8,64,128]{2,1,0:T(8,128)(2,1)S(1)} %collective-permute-done.2.refs_2_, ...), custom_call_target="tpu_custom_call" | custom-call | flops 3000000000 | bytes 30000000 | tf_op jit(solution)/shard_map/cross/pallas_call | solution.py:80
  13.1 2.9 %collective-permute-start.4 = (bf16[2,8,64,128]{3,2,1,0:T(8,128)(2,1)S(1)}, bf16[2,8,64,128]{3,2,1,0:T(8,128)(2,1)S(1)}, u32[]{:S(2)}, u32[]{:S(2)}) collective-permute-start(bf16[2,8,64,128]{3,2,1,0:T(8,128)(2,1)S(1)} %cross.2), channel_id=1, source_target_pairs={{0,8},{2,10},{4,12},{6,14},{8,0},{10,2},{12,4},{14,6},{1,9},{3,11}... | collective-permute-start | bytes 786440 | tf_op jit(solution)/shard_map/ppermute | solution.py:28
  15.9 1.4 %collective-permute-start.9 = (bf16[5,64,128]{2,1,0:T(8,128)(2,1)S(1)}, bf16[5,64,128]{2,1,0:T(8,128)(2,1)S(1)}, u32[]{:S(2)}, u32[]{:S(2)}) collective-permute-start(bf16[5,64,128]{2,1,0:T(8,128)(2,1)S(1)} %get-tuple-element.26), channel_id=1, source_target_pairs={{0,2},{2,0},{4,6},{6,4},{8,10},{10,8},{12,14},{14,12},{1,3},{3,1},... | collective-permute-start | bytes 245768 | tf_op jit(solution)/shard_map/ppermute | solution.py:28
  17.3 1.6 %collective-permute-start.10 = (bf16[5,64,128]{2,1,0:T(8,128)(2,1)S(1)}, bf16[5,64,128]{2,1,0:T(8,128)(2,1)S(1)}, u32[]{:S(2)}, u32[]{:S(2)}) collective-permute-start(bf16[5,64,128]{2,1,0:T(8,128)(2,1)S(1)} %get-tuple-element.27), channel_id=1, source_target_pairs={{0,4},{2,6},{4,0},{6,2},{8,12},{10,14},{12,8},{14,10},{1,5},{3,7},... | collective-permute-start | bytes 245768 | tf_op jit(solution)/shard_map/ppermute | solution.py:28
  18.9 0.5 %collective-permute-start.11 = (bf16[5,64,128]{2,1,0:T(8,128)(2,1)S(1)}, bf16[5,64,128]{2,1,0:T(8,128)(2,1)S(1)}, u32[]{:S(2)}, u32[]{:S(2)}) collective-permute-start(bf16[5,64,128]{2,1,0:T(8,128)(2,1)S(1)} %get-tuple-element.28), channel_id=1, source_target_pairs={{0,6},{2,4},{4,2},{6,0},{8,14},{10,12},{12,10},{14,8},{1,7},{3,5},... | collective-permute-start | bytes 245768 | tf_op jit(solution)/shard_map/ppermute | solution.py:28
  19.4 5.9 %collective-permute-done.far_ref = bf16[256,1024]{1,0:T(8,128)(2,1)S(1)} collective-permute-done((bf16[256,1024]{1,0:T(8,128)(2,1)S(1)}, bf16[256,1024]{1,0:T(8,128)(2,1)S(1)}, u32[]{:S(2)}, u32[]{:S(2)}) %collective-permute-start) | collective-permute-done | bytes 524320 | tf_op jit(solution)/shard_map/ppermute | solution.py:28
  25.3 2.7 %attend.1.context_ref = bf16[4,256,1024]{2,1,0:T(8,128)(2,1)S(1)} custom-call(bf16[256,4096]{1,0:T(8,128)(2,1)S(1)} %copy-done, bf16[256,512]{1,0:T(8,128)(2,1)S(1)} %copy-done.1, bf16[256,512]{1,0:T(8,128)(2,1)S(1)} %copy-done.2, bf16[256,1024]{1,0:T(8,128)(2,1)S(1)} %collective-permute-done.far_ref), custom_call_target="tpu_custom_call" | custom-call | tf_op jit(solution)/shard_map/attend/pallas_call | solution.py:80
  28.0 0.6 %cross.3 = bf16[2,5,64,128]{3,2,1,0:T(8,128)(2,1)S(1)} custom-call(s32[4]{0:T(128)S(1)} %copy-done.3, bf16[5,64,128]{2,1,0:T(8,128)(2,1)S(1)} %get-tuple-element.29.refs_0_, bf16[5,64,128]{2,1,0:T(8,128)(2,1)S(1)} %collective-permute-done.9.refs_1_, bf16[5,64,128]{2,1,0:T(8,128)(2,1)S(1)} %collective-permute-done.10.refs_2_, ...), custom_call_target="tpu_custom_call" | custom-call | tf_op jit(solution)/shard_map/cross/pallas_call | solution.py:80
  28.7 2.8 %collective-permute-start.12 = (bf16[2,5,64,128]{3,2,1,0:T(8,128)(2,1)S(1)}, bf16[2,5,64,128]{3,2,1,0:T(8,128)(2,1)S(1)}, u32[]{:S(2)}, u32[]{:S(2)}) collective-permute-start(bf16[2,5,64,128]{3,2,1,0:T(8,128)(2,1)S(1)} %cross.3), channel_id=1, source_target_pairs={{0,8},{2,10},{4,12},{6,14},{8,0},{10,2},{12,4},{14,6},{1,9},{3,11}... | collective-permute-start | bytes 491528 | tf_op jit(solution)/shard_map/ppermute | solution.py:28
  31.4 0.6 %settle.2 = (bf16[8,64,128]{2,1,0:T(8,128)(2,1)S(1)}, bf16[8,64,128]{2,1,0:T(8,128)(2,1)S(1)}) custom-call(s32[4]{0:T(128)S(1)} %copy-done.3, bf16[8,64,128]{2,1,0:T(8,128)(2,1)S(1)} %get-tuple-element.38.refs_0_, bf16[8,64,128]{2,1,0:T(8,128)(2,1)S(1)} %collective-permute-done.1.refs_1_, bf16[8,64,128]{2,1,0:T(8,128)(2,1)S(1)} %collective-permute-done.2.refs_2_, ...), custom_call_target="tpu_custom_call" | custom-call | tf_op jit(solution)/shard_map/settle/pallas_call | solution.py:80
  32.1 4.0 %collective-permute-start.5 = (bf16[8,64,128]{2,1,0:T(8,128)(2,1)S(1)}, bf16[8,64,128]{2,1,0:T(8,128)(2,1)S(1)}, u32[]{:S(2)}, u32[]{:S(2)}) collective-permute-start(bf16[8,64,128]{2,1,0:T(8,128)(2,1)S(1)} %get-tuple-element.23.refs_0_), channel_id=1, source_target_pairs={{0,2},{2,0},{4,6},{6,4},{8,10},{10,8},{12,14},{14,12},{1,3},{3,1},... | collective-permute-start | bytes 393224 | tf_op jit(solution)/shard_map/ppermute | solution.py:28
  36.1 1.1 %collective-permute-start.7 = (bf16[8,64,128]{2,1,0:T(8,128)(2,1)S(1)}, bf16[8,64,128]{2,1,0:T(8,128)(2,1)S(1)}, u32[]{:S(2)}, u32[]{:S(2)}) collective-permute-start(bf16[8,64,128]{2,1,0:T(8,128)(2,1)S(1)} %get-tuple-element.24), channel_id=1, source_target_pairs={{0,6},{2,4},{4,2},{6,0},{8,14},{10,12},{12,10},{14,8},{1,7},{3,5},... | collective-permute-start | bytes 393224 | tf_op jit(solution)/shard_map/ppermute | solution.py:28
  37.2 0.5 %collective-permute-start.6 = (bf16[8,64,128]{2,1,0:T(8,128)(2,1)S(1)}, bf16[8,64,128]{2,1,0:T(8,128)(2,1)S(1)}, u32[]{:S(2)}, u32[]{:S(2)}) collective-permute-start(bf16[8,64,128]{2,1,0:T(8,128)(2,1)S(1)} %get-tuple-element.24), channel_id=1, source_target_pairs={{0,4},{2,6},{4,0},{6,2},{8,12},{10,14},{12,8},{14,10},{1,5},{3,7},... | collective-permute-start | bytes 393224 | tf_op jit(solution)/shard_map/ppermute | solution.py:28
  37.7 0.6 %settle.3 = (bf16[5,64,128]{2,1,0:T(8,128)(2,1)S(1)}, bf16[5,64,128]{2,1,0:T(8,128)(2,1)S(1)}) custom-call(s32[4]{0:T(128)S(1)} %copy-done.3, bf16[5,64,128]{2,1,0:T(8,128)(2,1)S(1)} %get-tuple-element.29.refs_0_, bf16[5,64,128]{2,1,0:T(8,128)(2,1)S(1)} %collective-permute-done.9.refs_1_, bf16[5,64,128]{2,1,0:T(8,128)(2,1)S(1)} %collective-permute-done.10.refs_2_, ...), custom_call_target="tpu_custom_call" | custom-call | tf_op jit(solution)/shard_map/settle/pallas_call | solution.py:80
  38.3 2.4 %collective-permute-start.13 = (bf16[5,64,128]{2,1,0:T(8,128)(2,1)S(1)}, bf16[5,64,128]{2,1,0:T(8,128)(2,1)S(1)}, u32[]{:S(2)}, u32[]{:S(2)}) collective-permute-start(bf16[5,64,128]{2,1,0:T(8,128)(2,1)S(1)} %get-tuple-element.33.refs_0_), channel_id=1, source_target_pairs={{0,2},{2,0},{4,6},{6,4},{8,10},{10,8},{12,14},{14,12},{1,3},{3,1},... | collective-permute-start | bytes 245768 | tf_op jit(solution)/shard_map/ppermute | solution.py:28
  40.7 1.5 %collective-permute-start.15 = (bf16[5,64,128]{2,1,0:T(8,128)(2,1)S(1)}, bf16[5,64,128]{2,1,0:T(8,128)(2,1)S(1)}, u32[]{:S(2)}, u32[]{:S(2)}) collective-permute-start(bf16[5,64,128]{2,1,0:T(8,128)(2,1)S(1)} %get-tuple-element.34), channel_id=1, source_target_pairs={{0,6},{2,4},{4,2},{6,0},{8,14},{10,12},{12,10},{14,8},{1,7},{3,5},... | collective-permute-start | bytes 245768 | tf_op jit(solution)/shard_map/ppermute | solution.py:28
  42.2 0.9 %collective-permute-start.14 = (bf16[5,64,128]{2,1,0:T(8,128)(2,1)S(1)}, bf16[5,64,128]{2,1,0:T(8,128)(2,1)S(1)}, u32[]{:S(2)}, u32[]{:S(2)}) collective-permute-start(bf16[5,64,128]{2,1,0:T(8,128)(2,1)S(1)} %get-tuple-element.34), channel_id=1, source_target_pairs={{0,4},{2,6},{4,0},{6,2},{8,12},{10,14},{12,8},{14,10},{1,5},{3,7},... | collective-permute-start | bytes 245768 | tf_op jit(solution)/shard_map/ppermute | solution.py:28
  43.1 0.3 collective-permute-done.7.refs_3_
  43.4 0.4 collective-permute-done.6.refs_2_
  43.8 1.2 %rank_mix.1.near_ref = f32[256,64]{1,0:T(8,128)S(1)} custom-call(s32[4]{0:T(128)S(1)} %copy-done.3, bf16[4,256,1024]{2,1,0:T(8,128)(2,1)S(1)} %attend.1.context_ref, bf16[8,64,128]{2,1,0:T(8,128)(2,1)S(1)} %get-tuple-element.23.refs_0_, bf16[8,64,128]{2,1,0:T(8,128)(2,1)S(1)} %collective-permute-done.5.refs_1_, ...), custom_call_target="tpu_custom_call" | custom-call | tf_op jit(solution)/shard_map/rank_mix/pallas_call | solution.py:80
  45.1 1.3 %collective-permute-done.8.far_ref = f32[256,64]{1,0:T(8,128)S(1)} collective-permute-done((f32[256,64]{1,0:T(8,128)S(1)}, f32[256,64]{1,0:T(8,128)S(1)}, u32[]{:S(2)}, u32[]{:S(2)}) %collective-permute-start.8) | collective-permute-done | bytes 65568 | tf_op jit(solution)/shard_map/ppermute | solution.py:28
  46.7 1.9 %delta.1 = bf16[256,2560]{1,0:T(8,128)(2,1)} custom-call(s32[4]{0:T(128)S(1)} %copy-done.3, f32[256,64]{1,0:T(8,128)S(1)} %rank_mix.1.near_ref, f32[256,64]{1,0:T(8,128)S(1)} %collective-permute-done.8.far_ref, bf16[5,64,128]{2,1,0:T(8,128)(2,1)S(1)} %get-tuple-element.33.refs_0_, bf16[5,64,128]{2,1,0:T(8,128)(2,1)S(1)} %collective-permute-done.13.refs_1_, ...), custom_call_target="tpu_custom_call" | custom-call | tf_op jit(solution)/shard_map/delta/pallas_call | solution.py:169
  (19 shorter events, 0.4 us)
Async XLA Ops:
  1.1 9.9 %collective-permute-start.3 = (bf16[8,64,128]{2,1,0:T(8,128)(2,1)S(1)}, bf16[8,64,128]{2,1,0:T(8,128)(2,1)S(1)}, u32[]{:S(2)}, u32[]{:S(2)}) collective-permute-start(bf16[8,64,128]{2,1,0:T(8,128)(2,1)S(1)} %get-tuple-element.35), channel_id=1, source_target_pairs={{0,6},{2,4},{4,2},{6,0},{8,14},{10,12},{12,10},{14,8},{1,7},{3,5},... | collective-permute-start | bytes 393224 | tf_op jit(solution)/shard_map/ppermute | solution.py:28
  5.1 6.5 %collective-permute-start.2 = (bf16[8,64,128]{2,1,0:T(8,128)(2,1)S(1)}, bf16[8,64,128]{2,1,0:T(8,128)(2,1)S(1)}, u32[]{:S(2)}, u32[]{:S(2)}) collective-permute-start(bf16[8,64,128]{2,1,0:T(8,128)(2,1)S(1)} %get-tuple-element.36), channel_id=1, source_target_pairs={{0,4},{2,6},{4,0},{6,2},{8,12},{10,14},{12,8},{14,10},{1,5},{3,7},... | collective-permute-start | bytes 393224 | tf_op jit(solution)/shard_map/ppermute | solution.py:28
  5.6 6.2 %collective-permute-start.1 = (bf16[8,64,128]{2,1,0:T(8,128)(2,1)S(1)}, bf16[8,64,128]{2,1,0:T(8,128)(2,1)S(1)}, u32[]{:S(2)}, u32[]{:S(2)}) collective-permute-start(bf16[8,64,128]{2,1,0:T(8,128)(2,1)S(1)} %get-tuple-element.37), channel_id=1, source_target_pairs={{0,2},{2,0},{4,6},{6,4},{8,10},{10,8},{12,14},{14,12},{1,3},{3,1},... | collective-permute-start | bytes 393224 | tf_op jit(solution)/shard_map/ppermute | solution.py:28
  9.1 16.2 %collective-permute-start = (bf16[256,1024]{1,0:T(8,128)(2,1)S(1)}, bf16[256,1024]{1,0:T(8,128)(2,1)S(1)}, u32[]{:S(2)}, u32[]{:S(2)}) collective-permute-start(bf16[256,1024]{1,0:T(8,128)(2,1)S(1)} %pad_maximum_fusion), channel_id=1, source_target_pairs={{0,2},{2,0},{4,6},{6,4},{8,10},{10,8},{12,14},{14,12},{1,3},{3,1},... | collective-permute-start | bytes 1572872 | tf_op jit(solution)/shard_map/ppermute | solution.py:28
  11.8 0.7 %copy-start.3 = (s32[4]{0:T(128)S(1)}, s32[4]{0:T(128)}, u32[]{:S(2)}) copy-start(s32[4]{0:T(128)} %slots.1.slots_ref) | copy-start | bytes 52
  12.5 12.9 %copy-start = (bf16[256,4096]{1,0:T(8,128)(2,1)S(1)}, bf16[256,4096]{1,0:T(8,128)(2,1)}, u32[]{:S(2)}) copy-start(bf16[256,4096]{1,0:T(8,128)(2,1)} %query_ref.1) | copy-start | bytes 6291460
  12.5 12.9 %copy-start.1 = (bf16[256,512]{1,0:T(8,128)(2,1)S(1)}, bf16[256,512]{1,0:T(8,128)(2,1)}, u32[]{:S(2)}) copy-start(bf16[256,512]{1,0:T(8,128)(2,1)} %key_ref.1) | copy-start | bytes 786436
  12.5 12.9 %copy-start.2 = (bf16[256,512]{1,0:T(8,128)(2,1)S(1)}, bf16[256,512]{1,0:T(8,128)(2,1)}, u32[]{:S(2)}) copy-start(bf16[256,512]{1,0:T(8,128)(2,1)} %value_ref.1) | copy-start | bytes 786436
  13.1 18.4 %collective-permute-start.4 = (bf16[2,8,64,128]{3,2,1,0:T(8,128)(2,1)S(1)}, bf16[2,8,64,128]{3,2,1,0:T(8,128)(2,1)S(1)}, u32[]{:S(2)}, u32[]{:S(2)}) collective-permute-start(bf16[2,8,64,128]{3,2,1,0:T(8,128)(2,1)S(1)} %cross.2), channel_id=1, source_target_pairs={{0,8},{2,10},{4,12},{6,14},{8,0},{10,2},{12,4},{14,6},{1,9},{3,11}... | collective-permute-start | bytes 786440 | tf_op jit(solution)/shard_map/ppermute | solution.py:28
  15.9 12.1 %collective-permute-start.9 = (bf16[5,64,128]{2,1,0:T(8,128)(2,1)S(1)}, bf16[5,64,128]{2,1,0:T(8,128)(2,1)S(1)}, u32[]{:S(2)}, u32[]{:S(2)}) collective-permute-start(bf16[5,64,128]{2,1,0:T(8,128)(2,1)S(1)} %get-tuple-element.26), channel_id=1, source_target_pairs={{0,2},{2,0},{4,6},{6,4},{8,10},{10,8},{12,14},{14,12},{1,3},{3,1},... | collective-permute-start | bytes 245768 | tf_op jit(solution)/shard_map/ppermute | solution.py:28
  17.3 10.7 %collective-permute-start.10 = (bf16[5,64,128]{2,1,0:T(8,128)(2,1)S(1)}, bf16[5,64,128]{2,1,0:T(8,128)(2,1)S(1)}, u32[]{:S(2)}, u32[]{:S(2)}) collective-permute-start(bf16[5,64,128]{2,1,0:T(8,128)(2,1)S(1)} %get-tuple-element.27), channel_id=1, source_target_pairs={{0,4},{2,6},{4,0},{6,2},{8,12},{10,14},{12,8},{14,10},{1,5},{3,7},... | collective-permute-start | bytes 245768 | tf_op jit(solution)/shard_map/ppermute | solution.py:28
  18.9 9.2 %collective-permute-start.11 = (bf16[5,64,128]{2,1,0:T(8,128)(2,1)S(1)}, bf16[5,64,128]{2,1,0:T(8,128)(2,1)S(1)}, u32[]{:S(2)}, u32[]{:S(2)}) collective-permute-start(bf16[5,64,128]{2,1,0:T(8,128)(2,1)S(1)} %get-tuple-element.28), channel_id=1, source_target_pairs={{0,6},{2,4},{4,2},{6,0},{8,14},{10,12},{12,10},{14,8},{1,7},{3,5},... | collective-permute-start | bytes 245768 | tf_op jit(solution)/shard_map/ppermute | solution.py:28
  28.7 9.0 %collective-permute-start.12 = (bf16[2,5,64,128]{3,2,1,0:T(8,128)(2,1)S(1)}, bf16[2,5,64,128]{3,2,1,0:T(8,128)(2,1)S(1)}, u32[]{:S(2)}, u32[]{:S(2)}) collective-permute-start(bf16[2,5,64,128]{3,2,1,0:T(8,128)(2,1)S(1)} %cross.3), channel_id=1, source_target_pairs={{0,8},{2,10},{4,12},{6,14},{8,0},{10,2},{12,4},{14,6},{1,9},{3,11}... | collective-permute-start | bytes 491528 | tf_op jit(solution)/shard_map/ppermute | solution.py:28
  32.1 10.1 %collective-permute-start.5 = (bf16[8,64,128]{2,1,0:T(8,128)(2,1)S(1)}, bf16[8,64,128]{2,1,0:T(8,128)(2,1)S(1)}, u32[]{:S(2)}, u32[]{:S(2)}) collective-permute-start(bf16[8,64,128]{2,1,0:T(8,128)(2,1)S(1)} %get-tuple-element.23.refs_0_), channel_id=1, source_target_pairs={{0,2},{2,0},{4,6},{6,4},{8,10},{10,8},{12,14},{14,12},{1,3},{3,1},... | collective-permute-start | bytes 393224 | tf_op jit(solution)/shard_map/ppermute | solution.py:28
  36.1 7.3 %collective-permute-start.7 = (bf16[8,64,128]{2,1,0:T(8,128)(2,1)S(1)}, bf16[8,64,128]{2,1,0:T(8,128)(2,1)S(1)}, u32[]{:S(2)}, u32[]{:S(2)}) collective-permute-start(bf16[8,64,128]{2,1,0:T(8,128)(2,1)S(1)} %get-tuple-element.24), channel_id=1, source_target_pairs={{0,6},{2,4},{4,2},{6,0},{8,14},{10,12},{12,10},{14,8},{1,7},{3,5},... | collective-permute-start | bytes 393224 | tf_op jit(solution)/shard_map/ppermute | solution.py:28
  37.2 6.7 %collective-permute-start.6 = (bf16[8,64,128]{2,1,0:T(8,128)(2,1)S(1)}, bf16[8,64,128]{2,1,0:T(8,128)(2,1)S(1)}, u32[]{:S(2)}, u32[]{:S(2)}) collective-permute-start(bf16[8,64,128]{2,1,0:T(8,128)(2,1)S(1)} %get-tuple-element.24), channel_id=1, source_target_pairs={{0,4},{2,6},{4,0},{6,2},{8,12},{10,14},{12,8},{14,10},{1,5},{3,7},... | collective-permute-start | bytes 393224 | tf_op jit(solution)/shard_map/ppermute | solution.py:28
  38.3 8.2 %collective-permute-start.13 = (bf16[5,64,128]{2,1,0:T(8,128)(2,1)S(1)}, bf16[5,64,128]{2,1,0:T(8,128)(2,1)S(1)}, u32[]{:S(2)}, u32[]{:S(2)}) collective-permute-start(bf16[5,64,128]{2,1,0:T(8,128)(2,1)S(1)} %get-tuple-element.33.refs_0_), channel_id=1, source_target_pairs={{0,2},{2,0},{4,6},{6,4},{8,10},{10,8},{12,14},{14,12},{1,3},{3,1},... | collective-permute-start | bytes 245768 | tf_op jit(solution)/shard_map/ppermute | solution.py:28
  40.7 5.8 %collective-permute-start.15 = (bf16[5,64,128]{2,1,0:T(8,128)(2,1)S(1)}, bf16[5,64,128]{2,1,0:T(8,128)(2,1)S(1)}, u32[]{:S(2)}, u32[]{:S(2)}) collective-permute-start(bf16[5,64,128]{2,1,0:T(8,128)(2,1)S(1)} %get-tuple-element.34), channel_id=1, source_target_pairs={{0,6},{2,4},{4,2},{6,0},{8,14},{10,12},{12,10},{14,8},{1,7},{3,5},... | collective-permute-start | bytes 245768 | tf_op jit(solution)/shard_map/ppermute | solution.py:28
  42.2 4.4 %collective-permute-start.14 = (bf16[5,64,128]{2,1,0:T(8,128)(2,1)S(1)}, bf16[5,64,128]{2,1,0:T(8,128)(2,1)S(1)}, u32[]{:S(2)}, u32[]{:S(2)}) collective-permute-start(bf16[5,64,128]{2,1,0:T(8,128)(2,1)S(1)} %get-tuple-element.34), channel_id=1, source_target_pairs={{0,4},{2,6},{4,0},{6,2},{8,12},{10,14},{12,8},{14,10},{1,5},{3,7},... | collective-permute-start | bytes 245768 | tf_op jit(solution)/shard_map/ppermute | solution.py:28
  45.1 1.4 %collective-permute-start.8 = (f32[256,64]{1,0:T(8,128)S(1)}, f32[256,64]{1,0:T(8,128)S(1)}, u32[]{:S(2)}, u32[]{:S(2)}) collective-permute-start(f32[256,64]{1,0:T(8,128)S(1)} %rank_mix.1.near_ref), channel_id=1, source_target_pairs={{0,1},{1,0},{2,3},{3,2},{4,5},{5,4},{6,7},{7,6},{8,9},{9,8},{10,11... | collective-permute-start | bytes 196616 | tf_op jit(solution)/shard_map/ppermute | solution.py:28

commit v4 on v3

--- a/solution.py
+++ b/solution.py
@@ -15,6 +15,7 @@
 GROUP = QUERY_HEAD_COUNT // KEY_VALUE_HEADS
 EXP2_SCALE = math.log2(math.e) / math.sqrt(HEAD_SIZE)
 VMEM_LIMIT = 32 << 20
+WEIGHT = 3_000_000_000
 MINOR_BOTH = (((1,), (1,)), ((), ()))
 PLAIN = (((1,), (0,)), ((), ()))
 
@@ -120,6 +121,28 @@
             out_ref[at] = other[...]
 
 
+def choose_kernel(slots_ref, *refs):
+    me = lax.axis_index("req")
+    for apart in (1, 2, 3):
+        take((me >> 1) ^ apart, me, slots_ref, refs[:4], refs[3 + apart], ...)
+
+
+def assemble_kernel(slots_ref, *refs):
+    me = lax.axis_index("req")
+    where = slots_ref[me >> 1] ^ me
+    for k in range(4):
+
+        @pl.when(where == k)
+        def _():
+            refs[7][0] = refs[k][...]
+            refs[7][1] = refs[4][...]
+
+    @pl.when(where >= 4)
+    def _():
+        refs[7][0] = refs[5][...]
+        refs[7][1] = refs[6][...]
+
+
 def cross_kernel(slots_ref, *refs):
     me = lax.axis_index("req")
     for at in range(2):
@@ -133,29 +156,31 @@
         take(request, me, slots_ref, refs[:4], refs[5 + at], ..., refs[4].at[at])
 
 
-def rank_kernel(slots_ref, context_ref, *refs):
+def rank_kernel(slots_ref, context_ref, held_ref, got_ref, rank_ref):
     me = lax.axis_index("req")
     first = (slots_ref[me >> 1] ^ me) & 3
-    total = jnp.zeros(refs[4].shape, jnp.float32)
+    total = jnp.zeros(rank_ref.shape, jnp.float32)
     for k in range(4):
+        panel_ref = (held_ref, got_ref)[k & 1].at[k >> 1]
         for head in range(0, GROUP, 2):
             context = context_ref[first ^ k, :, head * HEAD_SIZE : (head + 2) * HEAD_SIZE]
-            panel = jnp.concatenate([refs[k][head], refs[k][head + 1]], axis=1)
+            panel = jnp.concatenate([panel_ref[head], panel_ref[head + 1]], axis=1)
             total += dot(context, panel, MINOR_BOTH)
-    refs[4][...] = total
+    rank_ref[...] = total
 
 
 def delta_kernel(slots_ref, near_ref, far_ref, *refs):
     out_ref, stage_ref, sems = refs[4:]
     me = lax.axis_index("req")
     first = (slots_ref[me >> 1] ^ me) & 3
+    first = (first >> 1) | ((first & 1) << 1)
     rank = (near_ref[...] + far_ref[...]).astype(jnp.bfloat16)
     wide = stage_ref.shape[2]
     copies = []
     for k in range(4):
         panel = jnp.concatenate([refs[k][b] for b in range(refs[k].shape[0])], axis=1)
         stage_ref[k] = (2.0 * dot(rank, panel)).astype(jnp.bfloat16)
-        columns = pl.ds(pl.multiple_of((first ^ k) * wide, HEAD_SIZE), wide)
+        columns = pl.ds(pl.multiple_of((first ^ (k >> 1) ^ ((k & 1) << 1)) * wide, HEAD_SIZE), wide)
         copy = pltpu.make_async_copy(stage_ref.at[k], out_ref.at[:, columns], sems.at[k])
         copy.start()
         copies.append(copy)
@@ -192,9 +217,9 @@
     return in_vmem(cross_kernel, "cross", shape, slots, *quarters, weight=weight)
 
 
-def gather(slots, quarters, came):
+def gather(slots, quarters, came, weight=0):
     shape = jax.ShapeDtypeStruct(quarters[0].shape, quarters[0].dtype)
-    near, aside = in_vmem(settle_kernel, "settle", [shape] * 2, slots, *quarters, came)
+    near, aside = in_vmem(settle_kernel, "settle", [shape] * 2, slots, *quarters, came, weight=weight)
     return [near] + [swapped(panel, "req", k) for k, panel in ((1, near), (2, aside), (3, aside))]
 
 
@@ -202,20 +227,44 @@
     return lax.optimization_barrier((earlier, value))[1]
 
 
+def spread_in_turn(over_x, own, earlier):
+    count = own.shape[0] // 2
+    over_x = after(earlier, over_x)
+    over_z = swapped(jnp.concatenate([own[count:], over_x[count:]]), "req", 2)
+    return [own[:count], over_x[:count], over_z[:count], over_z[count:]]
+
+
+def deliver(slots, quarters):
+    shape = jax.ShapeDtypeStruct(quarters[0].shape, quarters[0].dtype)
+    sent = in_vmem(choose_kernel, "choose", [shape] * 3, slots, *quarters, weight=WEIGHT)
+    return sent, [swapped(panel, "req", 2 * apart) for apart, panel in enumerate(sent, 1)]
+
+
+def assemble(slots, quarters, came):
+    both = jax.ShapeDtypeStruct((2, *came[0].shape), came[0].dtype)
+    return in_vmem(assemble_kernel, "assemble", both, slots, *quarters, *came)
+
+
 def eight_way(queries, keys, values, down, up, request_adapter, adapter_slot_table):
     slots = slots_of(request_adapter, adapter_slot_table)
-    down_quarters = spread(quarter_cut(down))
-    up_cut = quarter_cut(after(slots, up))
-    far = swapped(jnp.concatenate(after(up_cut, (keys, values)), axis=1), "req", 1)
-    down_sent = cross(slots, down_quarters, 3000000000)
-    down_came = swapped(down_sent, "req", 4)
-    up_quarters = spread(after(down_sent, up_cut))
-    context = attend(queries, keys, values, far)
-    down_panels = gather(slots, down_quarters, down_came)
-    up_came = swapped(cross(slots, after(context, up_quarters)), "req", 4)
-    up_panels = gather(slots, up_quarters, up_came)
+    down_cut = quarter_cut(down)
+    down_quarters = spread(down_cut)
+    half = up.shape[0] // 2
+    up = after(down_cut, up)
+    up_half, up_own = up[half:], up[:half]
+    up_over_x = swapped(up_half, "req", 1)
+    far = jnp.concatenate(after(up_half, (keys, values)), axis=1)
+    far = swapped(far, "req", 1)
+    down_sent, down_came = deliver(slots, down_quarters)
+    up_quarters = spread_in_turn(up_over_x, up_own, down_sent)
+    down_held = assemble(slots, down_quarters, down_came)
+    down_got = swapped(down_held, "req", 1)
+    up_sent = cross(slots, after(down_held, up_quarters))
+    up_came = swapped(up_sent, "req", 4)
+    context = attend(queries, keys, values, after(up_sent, far))
+    up_panels = gather(slots, up_quarters, after(context, up_came), 1000_000_000)
     rank_shape = jax.ShapeDtypeStruct((context.shape[1], ADAPTER_RANK), jnp.float32)
-    rank = in_vmem(rank_kernel, "rank_mix", rank_shape, slots, context, *down_panels)
+    rank = in_vmem(rank_kernel, "rank_mix", rank_shape, slots, context, down_held, down_got)
     return delta_of(slots, rank, swapped(rank, "tp", 1), up_panels)
 
 

time: 48.7 us -> 47.5 us (0.975)
  starting transfers between devices: 26.2 us -> 20.8 us
  waiting for transfers between devices: 8.93 us -> 13.1 us
  other arithmetic: 1.07 us -> 0.07 us
  local copies, waits for them, and re-layouts: 2.83 us -> 3.7 us
    ppermute x16 -> x15, starting transfers between devices: 26.2 us -> 20.8 us  [swapped(): return lax.ppermute(shard, axis, [(i, i ^ mask) for i in range(size)])]
    ppermute x16 -> x15, waiting for transfers between devices: 8.93 us -> 13.1 us  [swapped(): return lax.ppermute(shard, axis, [(i, i ^ mask) for i in range(size)])]
    slice x0 -> x4, local copies, waits for them, and re-layouts: none -> 1.9 us  [the longest x2 0.96 us: spread_in_turn(): over_z = swapped(jnp.concatenate([own[count:], over_x[count:]]), 'req', 2)]
    slice x2 -> x1, local copies, waits for them, and re-layouts: 2.16 us -> 1.13 us  [quarter_cut(): return [blocks[k * count:(k + 1) * count] for k in range(4)]]
    concatenate x1 -> x2, other arithmetic: 1.07 us -> 0.07 us  [the longest x1 0.06 us: eight_way(): far = jnp.concatenate(after(up_half, (keys, values)), axis=1)]
  transfers between devices with their start and end apart: 16 -> 15, of which waited for: 7 -> 6; matrix products, arithmetic and copies ran while one was open for 4% -> 4% of each run, Pallas kernels for 16% -> 16%
where the time goes in v4:
time: 47.5 us; the launch traced here: 47.3 us
  starting transfers between devices  20.8 us (44%)
  waiting for transfers between devices  13.1 us (28%)
  Pallas kernels  9.39 us (20%)
  local copies, waits for them, and re-layouts  3.7 us (8%)
    ppermute x15, starting transfers between devices, swapped(): return lax.ppermute(shard, axis, [(i, i ^ mask) for i in range(size)])  20.8 us
    ppermute x15, waiting for transfers between devices, swapped(): return lax.ppermute(shard, axis, [(i, i ^ mask) for i in range(size)])  13.1 us
    pallas_call x6, Pallas kernels, in_vmem(): pl.pallas_call(kernel, in_specs=[pl.BlockSpec(memory_space=pltpu.SMEM)] *...  6.33 us
    pallas_call x1, Pallas kernels, delta_of(): pl.pallas_call(delta_kernel, in_specs=[pl.BlockSpec(memory_space=pltpu.SM...  1.86 us
    pallas_call x1, Pallas kernels, slots_of(): pl.pallas_call(slots_kernel, in_specs=[pl.BlockSpec(memory_space=pltpu.SM...  1.2 us
    slice x1, local copies, waits for them, and re-layouts, quarter_cut(): return [blocks[k * count:(k + 1) * count] for k in range(4)]  1.13 us
    slice x2, local copies, waits for them, and re-layouts, spread_in_turn(): over_z = swapped(jnp.concatenate([own[count:], over_x[count:]]), 'req', 2)  0.96 us
  transfers between devices with their start and end apart: 15, of which 6 were waited for; matrix products, arithmetic and copies ran while one was open for 4% of the time, Pallas kernels for 16%

profile of v4, /device:TPU:0, one launch (start us, length us, event | category | flops | bytes accessed | tf_op | source)
XLA Modules:
  0.0 47.3 jit_solution(16965970569242808741)
XLA Ops:
  0.0 1.1 %slice_bitcast_fusion = (bf16[8,64,128]{2,1,0:T(8,128)(2,1)S(1)}, bf16[8,64,128]{2,1,0:T(8,128)(2,1)S(1)}, bf16[8,64,128]{2,1,0:T(8,128)(2,1)S(1)}, bf16[8,64,128]{2,1,0:T(8,128)(2,1)S(1)}) fusion(bf16[1,32,64,128]{3,2,1,0:T(8,128)(2,1)} %bitcast.12), kind=kLoop, calls=%fused_computation.2 | loop fusion | bytes 1048576 | tf_op jit(solution)/shard_map/slice | solution.py:208
  1.1 3.0 %collective-permute-start = (bf16[8,64,128]{2,1,0:T(8,128)(2,1)S(1)}, bf16[8,64,128]{2,1,0:T(8,128)(2,1)S(1)}, u32[]{:S(2)}, u32[]{:S(2)}) collective-permute-start(bf16[8,64,128]{2,1,0:T(8,128)(2,1)S(1)} %get-tuple-element.37), channel_id=1, source_target_pairs={{0,2},{2,0},{4,6},{6,4},{8,10},{10,8},{12,14},{14,12},{1,3},{3,1},... | collective-permute-start | bytes 393224 | tf_op jit(solution)/shard_map/ppermute | solution.py:29
  4.1 1.6 %collective-permute-start.1 = (bf16[8,64,128]{2,1,0:T(8,128)(2,1)S(1)}, bf16[8,64,128]{2,1,0:T(8,128)(2,1)S(1)}, u32[]{:S(2)}, u32[]{:S(2)}) collective-permute-start(bf16[8,64,128]{2,1,0:T(8,128)(2,1)S(1)} %get-tuple-element.36), channel_id=1, source_target_pairs={{0,4},{2,6},{4,0},{6,2},{8,12},{10,14},{12,8},{14,10},{1,5},{3,7},... | collective-permute-start | bytes 393224 | tf_op jit(solution)/shard_map/ppermute | solution.py:29
  5.7 0.9 %slice.57 = bf16[10,64,128]{2,1,0:T(8,128)(2,1)S(1)} slice(bf16[20,64,128]{2,1,0:T(8,128)(2,1)} %bitcast.13), slice={[10:20], [0:64], [0:128]} | slice | bytes 327680 | tf_op jit(solution)/shard_map/slice | solution.py:254
  6.6 2.0 %collective-permute-start.6 = (bf16[10,64,128]{2,1,0:T(8,128)(2,1)S(1)}, bf16[10,64,128]{2,1,0:T(8,128)(2,1)S(1)}, u32[]{:S(2)}, u32[]{:S(2)}) collective-permute-start(bf16[10,64,128]{2,1,0:T(8,128)(2,1)S(1)} %slice.57), channel_id=1, source_target_pairs={{0,2},{2,0},{4,6},{6,4},{8,10},{10,8},{12,14},{14,12},{1,3},{3,1},... | collective-permute-start | bytes 491528 | tf_op jit(solution)/shard_map/ppermute | solution.py:29
  8.6 1.2 %slots.1.slots_ref = s32[4]{0:T(128)} custom-call(s32[4]{0:T(128)} %adapter_ref.1, s32[8]{0:T(128)} %table_ref.1), custom_call_target="tpu_custom_call" | custom-call | tf_op jit(solution)/shard_map/slots/pallas_call | solution.py:99
  9.8 0.9 %fusion = (bf16[5,64,128]{2,1,0:T(8,128)(2,1)S(1)}, bf16[5,64,128]{2,1,0:T(8,128)(2,1)S(1)}) fusion(bf16[20,64,128]{2,1,0:T(8,128)(2,1)} %bitcast.14), kind=kLoop, calls=%fused_computation.6 | loop fusion | bytes 327680 | tf_op jit(solution)/shard_map/slice | solution.py:233
  10.8 1.0 %collective-permute-done.2.refs_3_ = bf16[8,64,128]{2,1,0:T(8,128)(2,1)S(1)} collective-permute-done((bf16[8,64,128]{2,1,0:T(8,128)(2,1)S(1)}, bf16[8,64,128]{2,1,0:T(8,128)(2,1)S(1)}, u32[]{:S(2)}, u32[]{:S(2)}) %collective-permute-start.2) | collective-permute-done | bytes 131104 | tf_op jit(solution)/shard_map/ppermute | solution.py:29
  11.8 0.7 %copy-done.3 = s32[4]{0:T(128)S(1)} copy-done((s32[4]{0:T(128)S(1)}, s32[4]{0:T(128)}, u32[]{:S(2)}) %copy-start.3) | copy-done | bytes 40
  12.5 0.6 %choose.1 = (bf16[8,64,128]{2,1,0:T(8,128)(2,1)S(1)}, bf16[8,64,128]{2,1,0:T(8,128)(2,1)S(1)}, bf16[8,64,128]{2,1,0:T(8,128)(2,1)S(1)}) custom-call(s32[4]{0:T(128)S(1)} %copy-done.3, bf16[8,64,128]{2,1,0:T(8,128)(2,1)S(1)} %get-tuple-element.38.refs_0_, bf16[8,64,128]{2,1,0:T(8,128)(2,1)S(1)} %collective-permute-done.refs_1_, ...), custom_call_target="tpu_custom_call" | custom-call | flops 3000000000 | bytes 30000000 | tf_op jit(solution)/shard_map/choose/pallas_call | solution.py:81
  13.1 1.8 %collective-permute-start.3 = (bf16[8,64,128]{2,1,0:T(8,128)(2,1)S(1)}, bf16[8,64,128]{2,1,0:T(8,128)(2,1)S(1)}, u32[]{:S(2)}, u32[]{:S(2)}) collective-permute-start(bf16[8,64,128]{2,1,0:T(8,128)(2,1)S(1)} %get-tuple-element.20), channel_id=1, source_target_pairs={{0,4},{2,6},{4,0},{6,2},{8,12},{10,14},{12,8},{14,10},{1,5},{3,7},... | collective-permute-start | bytes 393224 | tf_op jit(solution)/shard_map/ppermute | solution.py:29
  14.9 2.6 %collective-permute-start.4 = (bf16[8,64,128]{2,1,0:T(8,128)(2,1)S(1)}, bf16[8,64,128]{2,1,0:T(8,128)(2,1)S(1)}, u32[]{:S(2)}, u32[]{:S(2)}) collective-permute-start(bf16[8,64,128]{2,1,0:T(8,128)(2,1)S(1)} %get-tuple-element.21), channel_id=1, source_target_pairs={{0,8},{2,10},{4,12},{6,14},{8,0},{10,2},{12,4},{14,6},{1,9},{3,11}... | collective-permute-start | bytes 393224 | tf_op jit(solution)/shard_map/ppermute | solution.py:29
  17.5 0.1 collective-permute-start.5
  17.6 0.9 %collective-permute-start.7 = (bf16[10,64,128]{2,1,0:T(8,128)(2,1)S(1)}, bf16[10,64,128]{2,1,0:T(8,128)(2,1)S(1)}, u32[]{:S(2)}, u32[]{:S(2)}) collective-permute-start(bf16[10,64,128]{2,1,0:T(8,128)(2,1)S(1)} %pad_maximum_fusion.1), channel_id=1, source_target_pairs={{0,4},{2,6},{4,0},{6,2},{8,12},{10,14},{12,8},{14,10},{1,5},{3,7},... | collective-permute-start | bytes 491528 | tf_op jit(solution)/shard_map/ppermute | solution.py:29
  18.6 1.6 %collective-permute-start.8 = (bf16[256,1024]{1,0:T(8,128)(2,1)S(1)}, bf16[256,1024]{1,0:T(8,128)(2,1)S(1)}, u32[]{:S(2)}, u32[]{:S(2)}) collective-permute-start(bf16[256,1024]{1,0:T(8,128)(2,1)S(1)} %pad_maximum_fusion), channel_id=1, source_target_pairs={{0,2},{2,0},{4,6},{6,4},{8,10},{10,8},{12,14},{14,12},{1,3},{3,1},... | collective-permute-start | bytes 1572872 | tf_op jit(solution)/shard_map/ppermute | solution.py:29
  20.1 5.9 %collective-permute-done.4.refs_5_ = bf16[8,64,128]{2,1,0:T(8,128)(2,1)S(1)} collective-permute-done((bf16[8,64,128]{2,1,0:T(8,128)(2,1)S(1)}, bf16[8,64,128]{2,1,0:T(8,128)(2,1)S(1)}, u32[]{:S(2)}, u32[]{:S(2)}) %collective-permute-start.4) | collective-permute-done | bytes 131104 | tf_op jit(solution)/shard_map/ppermute | solution.py:29
  26.0 1.1 %collective-permute-done.5.refs_6_ = bf16[8,64,128]{2,1,0:T(8,128)(2,1)S(1)} collective-permute-done((bf16[8,64,128]{2,1,0:T(8,128)(2,1)S(1)}, bf16[8,64,128]{2,1,0:T(8,128)(2,1)S(1)}, u32[]{:S(2)}, u32[]{:S(2)}) %collective-permute-start.5) | collective-permute-done | bytes 131104 | tf_op jit(solution)/shard_map/ppermute | solution.py:29
  27.1 0.6 %assemble.1.held_ref = bf16[2,8,64,128]{3,2,1,0:T(8,128)(2,1)S(1)} custom-call(s32[4]{0:T(128)S(1)} %copy-done.4, bf16[8,64,128]{2,1,0:T(8,128)(2,1)S(1)} %get-tuple-element.38.refs_0_, bf16[8,64,128]{2,1,0:T(8,128)(2,1)S(1)} %collective-permute-done.refs_1_, bf16[8,64,128]{2,1,0:T(8,128)(2,1)S(1)} %collective-permute-done.1.refs_2_, ...), custom_call_target="tpu_custom_call" | custom-call | tf_op jit(solution)/shard_map/assemble/pallas_call | solution.py:81
  27.7 0.6 %cross.1 = bf16[2,5,64,128]{3,2,1,0:T(8,128)(2,1)S(1)} custom-call(s32[4]{0:T(128)S(1)} %copy-done.4, bf16[5,64,128]{2,1,0:T(8,128)(2,1)S(1)} %get-tuple-element.25.refs_0_, bf16[5,64,128]{2,1,0:T(8,128)(2,1)S(1)} %get-tuple-element.26.refs_1_, bf16[5,64,128]{2,1,0:T(8,128)(2,1)S(1)} %get-tuple-element.27.refs_2_, ...), custom_call_target="tpu_custom_call" | custom-call | tf_op jit(solution)/shard_map/cross/pallas_call | solution.py:81
  28.3 2.8 %collective-permute-start.11 = (bf16[2,5,64,128]{3,2,1,0:T(8,128)(2,1)S(1)}, bf16[2,5,64,128]{3,2,1,0:T(8,128)(2,1)S(1)}, u32[]{:S(2)}, u32[]{:S(2)}) collective-permute-start(bf16[2,5,64,128]{3,2,1,0:T(8,128)(2,1)S(1)} %cross.1), channel_id=1, source_target_pairs={{0,8},{2,10},{4,12},{6,14},{8,0},{10,2},{12,4},{14,6},{1,9},{3,11}... | collective-permute-start | bytes 491528 | tf_op jit(solution)/shard_map/ppermute | solution.py:29
  31.2 0.9 %collective-permute-start.9 = (bf16[2,8,64,128]{3,2,1,0:T(8,128)(2,1)S(1)}, bf16[2,8,64,128]{3,2,1,0:T(8,128)(2,1)S(1)}, u32[]{:S(2)}, u32[]{:S(2)}) collective-permute-start(bf16[2,8,64,128]{3,2,1,0:T(8,128)(2,1)S(1)} %assemble.1.held_ref), channel_id=1, source_target_pairs={{0,2},{2,0},{4,6},{6,4},{8,10},{10,8},{12,14},{14,12},{1,3},{3,1},... | collective-permute-start | bytes 786440 | tf_op jit(solution)/shard_map/ppermute | solution.py:29
  32.1 2.7 %attend.1.context_ref = bf16[4,256,1024]{2,1,0:T(8,128)(2,1)S(1)} custom-call(bf16[256,4096]{1,0:T(8,128)(2,1)S(1)} %copy-done, bf16[256,512]{1,0:T(8,128)(2,1)S(1)} %copy-done.1, bf16[256,512]{1,0:T(8,128)(2,1)S(1)} %copy-done.2, bf16[256,1024]{1,0:T(8,128)(2,1)S(1)} %collective-permute-done.8.far_ref), custom_call_target="tpu_custom_call" | custom-call | tf_op jit(solution)/shard_map/attend/pallas_call | solution.py:81
  34.7 3.1 %collective-permute-done.11.refs_4_ = bf16[2,5,64,128]{3,2,1,0:T(8,128)(2,1)S(1)} collective-permute-done((bf16[2,5,64,128]{3,2,1,0:T(8,128)(2,1)S(1)}, bf16[2,5,64,128]{3,2,1,0:T(8,128)(2,1)S(1)}, u32[]{:S(2)}, u32[]{:S(2)}) %collective-permute-start.11) | collective-permute-done | bytes 163872 | tf_op jit(solution)/shard_map/ppermute | solution.py:29
  37.9 0.6 %settle.1 = (bf16[5,64,128]{2,1,0:T(8,128)(2,1)S(1)}, bf16[5,64,128]{2,1,0:T(8,128)(2,1)S(1)}) custom-call(s32[4]{0:T(128)S(1)} %copy-done.4, bf16[5,64,128]{2,1,0:T(8,128)(2,1)S(1)} %get-tuple-element.25.refs_0_, bf16[5,64,128]{2,1,0:T(8,128)(2,1)S(1)} %get-tuple-element.26.refs_1_, bf16[5,64,128]{2,1,0:T(8,128)(2,1)S(1)} %get-tuple-element.27.refs_2_, ...), custom_call_target="tpu_custom_call" | custom-call | flops 1000000000 | bytes 10000000 | tf_op jit(solution)/shard_map/settle/pallas_call | solution.py:81
  38.5 0.6 %collective-permute-start.12 = (bf16[5,64,128]{2,1,0:T(8,128)(2,1)S(1)}, bf16[5,64,128]{2,1,0:T(8,128)(2,1)S(1)}, u32[]{:S(2)}, u32[]{:S(2)}) collective-permute-start(bf16[5,64,128]{2,1,0:T(8,128)(2,1)S(1)} %get-tuple-element.33.refs_0_), channel_id=1, source_target_pairs={{0,2},{2,0},{4,6},{6,4},{8,10},{10,8},{12,14},{14,12},{1,3},{3,1},... | collective-permute-start | bytes 245768 | tf_op jit(solution)/shard_map/ppermute | solution.py:29
  39.0 0.6 %collective-permute-start.13 = (bf16[5,64,128]{2,1,0:T(8,128)(2,1)S(1)}, bf16[5,64,128]{2,1,0:T(8,128)(2,1)S(1)}, u32[]{:S(2)}, u32[]{:S(2)}) collective-permute-start(bf16[5,64,128]{2,1,0:T(8,128)(2,1)S(1)} %get-tuple-element.34), channel_id=1, source_target_pairs={{0,4},{2,6},{4,0},{6,2},{8,12},{10,14},{12,8},{14,10},{1,5},{3,7},... | collective-permute-start | bytes 245768 | tf_op jit(solution)/shard_map/ppermute | solution.py:29
  39.6 2.4 %collective-permute-start.14 = (bf16[5,64,128]{2,1,0:T(8,128)(2,1)S(1)}, bf16[5,64,128]{2,1,0:T(8,128)(2,1)S(1)}, u32[]{:S(2)}, u32[]{:S(2)}) collective-permute-start(bf16[5,64,128]{2,1,0:T(8,128)(2,1)S(1)} %get-tuple-element.34), channel_id=1, source_target_pairs={{0,6},{2,4},{4,2},{6,0},{8,14},{10,12},{12,10},{14,8},{1,7},{3,5},... | collective-permute-start | bytes 245768 | tf_op jit(solution)/shard_map/ppermute | solution.py:29
  42.0 1.2 %rank_mix.1.near_ref = f32[256,64]{1,0:T(8,128)S(1)} custom-call(s32[4]{0:T(128)S(1)} %copy-done.4, bf16[4,256,1024]{2,1,0:T(8,128)(2,1)S(1)} %attend.1.context_ref, bf16[2,8,64,128]{3,2,1,0:T(8,128)(2,1)S(1)} %assemble.1.held_ref, bf16[2,8,64,128]{3,2,1,0:T(8,128)(2,1)S(1)} %collective-permute-done.9.got_ref), custom_call_target="tpu_custom_call" | custom-call | tf_op jit(solution)/shard_map/rank_mix/pallas_call | solution.py:81
  43.3 0.1 collective-permute-start.10
  43.3 1.3 %collective-permute-done.10.far_ref = f32[256,64]{1,0:T(8,128)S(1)} collective-permute-done((f32[256,64]{1,0:T(8,128)S(1)}, f32[256,64]{1,0:T(8,128)S(1)}, u32[]{:S(2)}, u32[]{:S(2)}) %collective-permute-start.10) | collective-permute-done | bytes 65568 | tf_op jit(solution)/shard_map/ppermute | solution.py:29
  44.7 0.7 %collective-permute-done.14.refs_3_ = bf16[5,64,128]{2,1,0:T(8,128)(2,1)S(1)} collective-permute-done((bf16[5,64,128]{2,1,0:T(8,128)(2,1)S(1)}, bf16[5,64,128]{2,1,0:T(8,128)(2,1)S(1)}, u32[]{:S(2)}, u32[]{:S(2)}) %collective-permute-start.14) | collective-permute-done | bytes 81952 | tf_op jit(solution)/shard_map/ppermute | solution.py:29
  45.4 1.9 %delta.1 = bf16[256,2560]{1,0:T(8,128)(2,1)} custom-call(s32[4]{0:T(128)S(1)} %copy-done.4, f32[256,64]{1,0:T(8,128)S(1)} %rank_mix.1.near_ref, f32[256,64]{1,0:T(8,128)S(1)} %collective-permute-done.10.far_ref, bf16[5,64,128]{2,1,0:T(8,128)(2,1)S(1)} %get-tuple-element.33.refs_0_, bf16[5,64,128]{2,1,0:T(8,128)(2,1)S(1)} %collective-permute-done.12.refs_1_, ...), custom_call_target="tpu_custom_call" | custom-call | tf_op jit(solution)/shard_map/delta/pallas_call | solution.py:194
  (23 shorter events, 0.2 us)
Async XLA Ops:
  1.1 9.7 %collective-permute-start = (bf16[8,64,128]{2,1,0:T(8,128)(2,1)S(1)}, bf16[8,64,128]{2,1,0:T(8,128)(2,1)S(1)}, u32[]{:S(2)}, u32[]{:S(2)}) collective-permute-start(bf16[8,64,128]{2,1,0:T(8,128)(2,1)S(1)} %get-tuple-element.37), channel_id=1, source_target_pairs={{0,2},{2,0},{4,6},{6,4},{8,10},{10,8},{12,14},{14,12},{1,3},{3,1},... | collective-permute-start | bytes 393224 | tf_op jit(solution)/shard_map/ppermute | solution.py:29
  4.1 6.7 %collective-permute-start.1 = (bf16[8,64,128]{2,1,0:T(8,128)(2,1)S(1)}, bf16[8,64,128]{2,1,0:T(8,128)(2,1)S(1)}, u32[]{:S(2)}, u32[]{:S(2)}) collective-permute-start(bf16[8,64,128]{2,1,0:T(8,128)(2,1)S(1)} %get-tuple-element.36), channel_id=1, source_target_pairs={{0,4},{2,6},{4,0},{6,2},{8,12},{10,14},{12,8},{14,10},{1,5},{3,7},... | collective-permute-start | bytes 393224 | tf_op jit(solution)/shard_map/ppermute | solution.py:29
  5.7 6.1 %collective-permute-start.2 = (bf16[8,64,128]{2,1,0:T(8,128)(2,1)S(1)}, bf16[8,64,128]{2,1,0:T(8,128)(2,1)S(1)}, u32[]{:S(2)}, u32[]{:S(2)}) collective-permute-start(bf16[8,64,128]{2,1,0:T(8,128)(2,1)S(1)} %get-tuple-element.35), channel_id=1, source_target_pairs={{0,6},{2,4},{4,2},{6,0},{8,14},{10,12},{12,10},{14,8},{1,7},{3,5},... | collective-permute-start | bytes 393224 | tf_op jit(solution)/shard_map/ppermute | solution.py:29
  6.6 10.9 %collective-permute-start.6 = (bf16[10,64,128]{2,1,0:T(8,128)(2,1)S(1)}, bf16[10,64,128]{2,1,0:T(8,128)(2,1)S(1)}, u32[]{:S(2)}, u32[]{:S(2)}) collective-permute-start(bf16[10,64,128]{2,1,0:T(8,128)(2,1)S(1)} %slice.57), channel_id=1, source_target_pairs={{0,2},{2,0},{4,6},{6,4},{8,10},{10,8},{12,14},{14,12},{1,3},{3,1},... | collective-permute-start | bytes 491528 | tf_op jit(solution)/shard_map/ppermute | solution.py:29
  9.8 17.3 %copy-start.4 = (s32[4]{0:T(128)S(1)}, s32[4]{0:T(128)}, u32[]{:S(2)}) copy-start(s32[4]{0:T(128)} %slots.1.slots_ref) | copy-start | bytes 52
  10.8 7.7 %copy-start.1 = (bf16[256,512]{1,0:T(8,128)(2,1)S(1)}, bf16[256,512]{1,0:T(8,128)(2,1)}, u32[]{:S(2)}) copy-start(bf16[256,512]{1,0:T(8,128)(2,1)} %key_ref.1) | copy-start | bytes 786436
  10.8 7.7 %copy-start.2 = (bf16[256,512]{1,0:T(8,128)(2,1)S(1)}, bf16[256,512]{1,0:T(8,128)(2,1)}, u32[]{:S(2)}) copy-start(bf16[256,512]{1,0:T(8,128)(2,1)} %value_ref.1) | copy-start | bytes 786436
  11.8 0.7 %copy-start.3 = (s32[4]{0:T(128)S(1)}, s32[4]{0:T(128)}, u32[]{:S(2)}) copy-start(s32[4]{0:T(128)} %slots.1.slots_ref) | copy-start | bytes 52
  13.1 18.9 %copy-start = (bf16[256,4096]{1,0:T(8,128)(2,1)S(1)}, bf16[256,4096]{1,0:T(8,128)(2,1)}, u32[]{:S(2)}) copy-start(bf16[256,4096]{1,0:T(8,128)(2,1)} %query_ref.1) | copy-start | bytes 6291460
  13.1 7.0 %collective-permute-start.3 = (bf16[8,64,128]{2,1,0:T(8,128)(2,1)S(1)}, bf16[8,64,128]{2,1,0:T(8,128)(2,1)S(1)}, u32[]{:S(2)}, u32[]{:S(2)}) collective-permute-start(bf16[8,64,128]{2,1,0:T(8,128)(2,1)S(1)} %get-tuple-element.20), channel_id=1, source_target_pairs={{0,4},{2,6},{4,0},{6,2},{8,12},{10,14},{12,8},{14,10},{1,5},{3,7},... | collective-permute-start | bytes 393224 | tf_op jit(solution)/shard_map/ppermute | solution.py:29
  14.9 11.1 %collective-permute-start.4 = (bf16[8,64,128]{2,1,0:T(8,128)(2,1)S(1)}, bf16[8,64,128]{2,1,0:T(8,128)(2,1)S(1)}, u32[]{:S(2)}, u32[]{:S(2)}) collective-permute-start(bf16[8,64,128]{2,1,0:T(8,128)(2,1)S(1)} %get-tuple-element.21), channel_id=1, source_target_pairs={{0,8},{2,10},{4,12},{6,14},{8,0},{10,2},{12,4},{14,6},{1,9},{3,11}... | collective-permute-start | bytes 393224 | tf_op jit(solution)/shard_map/ppermute | solution.py:29
  17.5 9.6 %collective-permute-start.5 = (bf16[8,64,128]{2,1,0:T(8,128)(2,1)S(1)}, bf16[8,64,128]{2,1,0:T(8,128)(2,1)S(1)}, u32[]{:S(2)}, u32[]{:S(2)}) collective-permute-start(bf16[8,64,128]{2,1,0:T(8,128)(2,1)S(1)} %get-tuple-element.22), channel_id=1, source_target_pairs={{0,12},{2,14},{4,8},{6,10},{8,4},{10,6},{12,0},{14,2},{1,13},{3,15... | collective-permute-start | bytes 393224 | tf_op jit(solution)/shard_map/ppermute | solution.py:29
  17.6 10.1 %collective-permute-start.7 = (bf16[10,64,128]{2,1,0:T(8,128)(2,1)S(1)}, bf16[10,64,128]{2,1,0:T(8,128)(2,1)S(1)}, u32[]{:S(2)}, u32[]{:S(2)}) collective-permute-start(bf16[10,64,128]{2,1,0:T(8,128)(2,1)S(1)} %pad_maximum_fusion.1), channel_id=1, source_target_pairs={{0,4},{2,6},{4,0},{6,2},{8,12},{10,14},{12,8},{14,10},{1,5},{3,7},... | collective-permute-start | bytes 491528 | tf_op jit(solution)/shard_map/ppermute | solution.py:29
  18.6 13.5 %collective-permute-start.8 = (bf16[256,1024]{1,0:T(8,128)(2,1)S(1)}, bf16[256,1024]{1,0:T(8,128)(2,1)S(1)}, u32[]{:S(2)}, u32[]{:S(2)}) collective-permute-start(bf16[256,1024]{1,0:T(8,128)(2,1)S(1)} %pad_maximum_fusion), channel_id=1, source_target_pairs={{0,2},{2,0},{4,6},{6,4},{8,10},{10,8},{12,14},{14,12},{1,3},{3,1},... | collective-permute-start | bytes 1572872 | tf_op jit(solution)/shard_map/ppermute | solution.py:29
  28.3 9.5 %collective-permute-start.11 = (bf16[2,5,64,128]{3,2,1,0:T(8,128)(2,1)S(1)}, bf16[2,5,64,128]{3,2,1,0:T(8,128)(2,1)S(1)}, u32[]{:S(2)}, u32[]{:S(2)}) collective-permute-start(bf16[2,5,64,128]{3,2,1,0:T(8,128)(2,1)S(1)} %cross.1), channel_id=1, source_target_pairs={{0,8},{2,10},{4,12},{6,14},{8,0},{10,2},{12,4},{14,6},{1,9},{3,11}... | collective-permute-start | bytes 491528 | tf_op jit(solution)/shard_map/ppermute | solution.py:29
  31.2 10.9 %collective-permute-start.9 = (bf16[2,8,64,128]{3,2,1,0:T(8,128)(2,1)S(1)}, bf16[2,8,64,128]{3,2,1,0:T(8,128)(2,1)S(1)}, u32[]{:S(2)}, u32[]{:S(2)}) collective-permute-start(bf16[2,8,64,128]{3,2,1,0:T(8,128)(2,1)S(1)} %assemble.1.held_ref), channel_id=1, source_target_pairs={{0,2},{2,0},{4,6},{6,4},{8,10},{10,8},{12,14},{14,12},{1,3},{3,1},... | collective-permute-start | bytes 786440 | tf_op jit(solution)/shard_map/ppermute | solution.py:29
  38.5 6.2 %collective-permute-start.12 = (bf16[5,64,128]{2,1,0:T(8,128)(2,1)S(1)}, bf16[5,64,128]{2,1,0:T(8,128)(2,1)S(1)}, u32[]{:S(2)}, u32[]{:S(2)}) collective-permute-start(bf16[5,64,128]{2,1,0:T(8,128)(2,1)S(1)} %get-tuple-element.33.refs_0_), channel_id=1, source_target_pairs={{0,2},{2,0},{4,6},{6,4},{8,10},{10,8},{12,14},{14,12},{1,3},{3,1},... | collective-permute-start | bytes 245768 | tf_op jit(solution)/shard_map/ppermute | solution.py:29
  39.0 5.7 %collective-permute-start.13 = (bf16[5,64,128]{2,1,0:T(8,128)(2,1)S(1)}, bf16[5,64,128]{2,1,0:T(8,128)(2,1)S(1)}, u32[]{:S(2)}, u32[]{:S(2)}) collective-permute-start(bf16[5,64,128]{2,1,0:T(8,128)(2,1)S(1)} %get-tuple-element.34), channel_id=1, source_target_pairs={{0,4},{2,6},{4,0},{6,2},{8,12},{10,14},{12,8},{14,10},{1,5},{3,7},... | collective-permute-start | bytes 245768 | tf_op jit(solution)/shard_map/ppermute | solution.py:29
  39.6 5.8 %collective-permute-start.14 = (bf16[5,64,128]{2,1,0:T(8,128)(2,1)S(1)}, bf16[5,64,128]{2,1,0:T(8,128)(2,1)S(1)}, u32[]{:S(2)}, u32[]{:S(2)}) collective-permute-start(bf16[5,64,128]{2,1,0:T(8,128)(2,1)S(1)} %get-tuple-element.34), channel_id=1, source_target_pairs={{0,6},{2,4},{4,2},{6,0},{8,14},{10,12},{12,10},{14,8},{1,7},{3,5},... | collective-permute-start | bytes 245768 | tf_op jit(solution)/shard_map/ppermute | solution.py:29
  43.3 1.4 %collective-permute-start.10 = (f32[256,64]{1,0:T(8,128)S(1)}, f32[256,64]{1,0:T(8,128)S(1)}, u32[]{:S(2)}, u32[]{:S(2)}) collective-permute-start(f32[256,64]{1,0:T(8,128)S(1)} %rank_mix.1.near_ref), channel_id=1, source_target_pairs={{0,1},{1,0},{2,3},{3,2},{4,5},{5,4},{6,7},{7,6},{8,9},{9,8},{10,11... | collective-permute-start | bytes 196616 | tf_op jit(solution)/shard_map/ppermute | solution.py:29

commit v5 on v4

--- a/solution.py
+++ b/solution.py
@@ -143,19 +143,6 @@
         refs[7][1] = refs[6][...]
 
 
-def cross_kernel(slots_ref, *refs):
-    me = lax.axis_index("req")
-    for at in range(2):
-        take((me >> 1) ^ (2 + at), me, slots_ref, refs[:4], refs[4], at)
-
-
-def settle_kernel(slots_ref, *refs):
-    me = lax.axis_index("req")
-    for at in range(2):
-        request = (me >> 1) ^ at
-        take(request, me, slots_ref, refs[:4], refs[5 + at], ..., refs[4].at[at])
-
-
 def rank_kernel(slots_ref, context_ref, held_ref, got_ref, rank_ref):
     me = lax.axis_index("req")
     first = (slots_ref[me >> 1] ^ me) & 3
@@ -170,15 +157,16 @@
 
 
 def delta_kernel(slots_ref, near_ref, far_ref, *refs):
-    out_ref, stage_ref, sems = refs[4:]
+    out_ref, stage_ref, sems = refs[2:]
     me = lax.axis_index("req")
     first = (slots_ref[me >> 1] ^ me) & 3
     first = (first >> 1) | ((first & 1) << 1)
     rank = (near_ref[...] + far_ref[...]).astype(jnp.bfloat16)
     wide = stage_ref.shape[2]
     copies = []
-    for k in range(4):
-        panel = jnp.concatenate([refs[k][b] for b in range(refs[k].shape[0])], axis=1)
+    for k in (0, 2, 1, 3):
+        panel_ref = refs[k & 1].at[k >> 1]
+        panel = jnp.concatenate([panel_ref[b] for b in range(panel_ref.shape[0])], axis=1)
         stage_ref[k] = (2.0 * dot(rank, panel)).astype(jnp.bfloat16)
         columns = pl.ds(pl.multiple_of((first ^ (k >> 1) ^ ((k & 1) << 1)) * wide, HEAD_SIZE), wide)
         copy = pltpu.make_async_copy(stage_ref.at[k], out_ref.at[:, columns], sems.at[k])
@@ -188,19 +176,19 @@
         copy.wait()
 
 
-def delta_of(slots, near, far, panels):
+def delta_of(slots, near, far, held, got):
     rows = near.shape[0]
-    wide = panels[0].shape[0] * panels[0].shape[2]
+    wide = held.shape[1] * held.shape[3]
     return pl.pallas_call(
         delta_kernel,
         in_specs=[pl.BlockSpec(memory_space=pltpu.SMEM)]
-        + [pl.BlockSpec(memory_space=pltpu.VMEM)] * 6,
+        + [pl.BlockSpec(memory_space=pltpu.VMEM)] * 4,
         out_specs=pl.BlockSpec(memory_space=pl.ANY),
         out_shape=jax.ShapeDtypeStruct((rows, 4 * wide), jnp.bfloat16),
         scratch_shapes=[pltpu.VMEM((4, rows, wide), jnp.bfloat16), pltpu.SemaphoreType.DMA((4,))],
         compiler_params=pltpu.CompilerParams(vmem_limit_bytes=VMEM_LIMIT),
         name="delta",
-    )(slots, near, far, *panels)
+    )(slots, near, far, held, got)
 
 
 def quarter_cut(blocks):
@@ -210,17 +198,6 @@
 
 def spread(cut):
     return cut[:1] + [swapped(cut[k], "req", k) for k in (1, 2, 3)]
-
-
-def cross(slots, quarters, weight=0):
-    shape = jax.ShapeDtypeStruct((2, *quarters[0].shape), quarters[0].dtype)
-    return in_vmem(cross_kernel, "cross", shape, slots, *quarters, weight=weight)
-
-
-def gather(slots, quarters, came, weight=0):
-    shape = jax.ShapeDtypeStruct(quarters[0].shape, quarters[0].dtype)
-    near, aside = in_vmem(settle_kernel, "settle", [shape] * 2, slots, *quarters, came, weight=weight)
-    return [near] + [swapped(panel, "req", k) for k, panel in ((1, near), (2, aside), (3, aside))]
 
 
 def after(earlier, value):
@@ -234,15 +211,15 @@
     return [own[:count], over_x[:count], over_z[:count], over_z[count:]]
 
 
-def deliver(slots, quarters):
+def deliver(slots, quarters, weight=0):
     shape = jax.ShapeDtypeStruct(quarters[0].shape, quarters[0].dtype)
-    sent = in_vmem(choose_kernel, "choose", [shape] * 3, slots, *quarters, weight=WEIGHT)
+    sent = in_vmem(choose_kernel, "choose", [shape] * 3, slots, *quarters, weight=weight)
     return sent, [swapped(panel, "req", 2 * apart) for apart, panel in enumerate(sent, 1)]
 
 
-def assemble(slots, quarters, came):
+def assemble(slots, quarters, came, weight=0):
     both = jax.ShapeDtypeStruct((2, *came[0].shape), came[0].dtype)
-    return in_vmem(assemble_kernel, "assemble", both, slots, *quarters, *came)
+    return in_vmem(assemble_kernel, "assemble", both, slots, *quarters, *came, weight=weight)
 
 
 def eight_way(queries, keys, values, down, up, request_adapter, adapter_slot_table):
@@ -253,19 +230,18 @@
     up = after(down_cut, up)
     up_half, up_own = up[half:], up[:half]
     up_over_x = swapped(up_half, "req", 1)
-    far = jnp.concatenate(after(up_half, (keys, values)), axis=1)
-    far = swapped(far, "req", 1)
-    down_sent, down_came = deliver(slots, down_quarters)
+    down_sent, down_came = deliver(slots, down_quarters, WEIGHT)
+    far = swapped(jnp.concatenate(after(down_sent, (keys, values)), axis=1), "req", 1)
     up_quarters = spread_in_turn(up_over_x, up_own, down_sent)
-    down_held = assemble(slots, down_quarters, down_came)
+    down_held = assemble(slots, down_quarters, down_came, 3000_000_000)
     down_got = swapped(down_held, "req", 1)
-    up_sent = cross(slots, after(down_held, up_quarters))
-    up_came = swapped(up_sent, "req", 4)
+    up_sent, up_came = deliver(slots, after(down_held, up_quarters))
     context = attend(queries, keys, values, after(up_sent, far))
-    up_panels = gather(slots, up_quarters, after(context, up_came), 1000_000_000)
+    up_held = assemble(slots, up_quarters, after(context, up_came), 1000_000_000)
+    up_got = swapped(up_held, "req", 1)
     rank_shape = jax.ShapeDtypeStruct((context.shape[1], ADAPTER_RANK), jnp.float32)
     rank = in_vmem(rank_kernel, "rank_mix", rank_shape, slots, context, down_held, down_got)
-    return delta_of(slots, rank, swapped(rank, "tp", 1), up_panels)
+    return delta_of(slots, rank, swapped(rank, "tp", 1), up_held, up_got)
 
 
 def any_way(context, down, up, slots):

time: 47.5 us -> 46.2 us (0.973)
  waiting for transfers between devices: 13.1 us -> 11.9 us
    ppermute x15, waiting for transfers between devices: 13.1 us -> 11.9 us  [swapped(): return lax.ppermute(shard, axis, [(i, i ^ mask) for i in range(size)])]
where the time goes in v5:
time: 46.2 us; the launch traced here: 46 us
  starting transfers between devices  20.8 us (45%)
  waiting for transfers between devices  11.9 us (26%)
  Pallas kernels  9.39 us (20%)
  local copies, waits for them, and re-layouts  3.69 us (8%)
    ppermute x15, starting transfers between devices, swapped(): return lax.ppermute(shard, axis, [(i, i ^ mask) for i in range(size)])  20.8 us
    ppermute x15, waiting for transfers between devices, swapped(): return lax.ppermute(shard, axis, [(i, i ^ mask) for i in range(size)])  11.9 us
    pallas_call x6, Pallas kernels, in_vmem(): pl.pallas_call(kernel, in_specs=[pl.BlockSpec(memory_space=pltpu.SMEM)] *...  6.34 us
    pallas_call x1, Pallas kernels, delta_of(): pl.pallas_call(delta_kernel, in_specs=[pl.BlockSpec(memory_space=pltpu.SM...  1.86 us
    pallas_call x1, Pallas kernels, slots_of(): pl.pallas_call(slots_kernel, in_specs=[pl.BlockSpec(memory_space=pltpu.SM...  1.2 us
    slice x1, local copies, waits for them, and re-layouts, quarter_cut(): return [blocks[k * count:(k + 1) * count] for k in range(4)]  1.13 us
    slice x2, local copies, waits for them, and re-layouts, spread_in_turn(): over_z = swapped(jnp.concatenate([own[count:], over_x[count:]]), 'req', 2)  0.95 us
    slice x1, local copies, waits for them, and re-layouts, eight_way(): up_half, up_own = (up[half:], up[:half])  0.93 us
  transfers between devices with their start and end apart: 15, of which 6 were waited for; matrix products, arithmetic and copies ran while one was open for 4% of the time, Pallas kernels for 16%

profile of v5, /device:TPU:0, one launch (start us, length us, event | category | flops | bytes accessed | tf_op | source)
XLA Modules:
  0.0 46.0 jit_solution(18382005296746385432)
XLA Ops:
  0.0 1.1 %slice_bitcast_fusion = (bf16[8,64,128]{2,1,0:T(8,128)(2,1)S(1)}, bf16[8,64,128]{2,1,0:T(8,128)(2,1)S(1)}, bf16[8,64,128]{2,1,0:T(8,128)(2,1)S(1)}, bf16[8,64,128]{2,1,0:T(8,128)(2,1)S(1)}) fusion(bf16[1,32,64,128]{3,2,1,0:T(8,128)(2,1)} %bitcast.12), kind=kLoop, calls=%fused_computation.2 | loop fusion | bytes 1048576 | tf_op jit(solution)/shard_map/slice | solution.py:196
  1.1 3.0 %collective-permute-start = (bf16[8,64,128]{2,1,0:T(8,128)(2,1)S(1)}, bf16[8,64,128]{2,1,0:T(8,128)(2,1)S(1)}, u32[]{:S(2)}, u32[]{:S(2)}) collective-permute-start(bf16[8,64,128]{2,1,0:T(8,128)(2,1)S(1)} %get-tuple-element.43), channel_id=1, source_target_pairs={{0,2},{2,0},{4,6},{6,4},{8,10},{10,8},{12,14},{14,12},{1,3},{3,1},... | collective-permute-start | bytes 393224 | tf_op jit(solution)/shard_map/ppermute | solution.py:29
  4.1 1.6 %collective-permute-start.1 = (bf16[8,64,128]{2,1,0:T(8,128)(2,1)S(1)}, bf16[8,64,128]{2,1,0:T(8,128)(2,1)S(1)}, u32[]{:S(2)}, u32[]{:S(2)}) collective-permute-start(bf16[8,64,128]{2,1,0:T(8,128)(2,1)S(1)} %get-tuple-element.42), channel_id=1, source_target_pairs={{0,4},{2,6},{4,0},{6,2},{8,12},{10,14},{12,8},{14,10},{1,5},{3,7},... | collective-permute-start | bytes 393224 | tf_op jit(solution)/shard_map/ppermute | solution.py:29
  5.7 0.9 %slice.57 = bf16[10,64,128]{2,1,0:T(8,128)(2,1)S(1)} slice(bf16[20,64,128]{2,1,0:T(8,128)(2,1)} %bitcast.13), slice={[10:20], [0:64], [0:128]} | slice | bytes 327680 | tf_op jit(solution)/shard_map/slice | solution.py:231
  6.6 2.0 %collective-permute-start.6 = (bf16[10,64,128]{2,1,0:T(8,128)(2,1)S(1)}, bf16[10,64,128]{2,1,0:T(8,128)(2,1)S(1)}, u32[]{:S(2)}, u32[]{:S(2)}) collective-permute-start(bf16[10,64,128]{2,1,0:T(8,128)(2,1)S(1)} %slice.57), channel_id=1, source_target_pairs={{0,2},{2,0},{4,6},{6,4},{8,10},{10,8},{12,14},{14,12},{1,3},{3,1},... | collective-permute-start | bytes 491528 | tf_op jit(solution)/shard_map/ppermute | solution.py:29
  8.6 1.2 %slots.1.slots_ref = s32[4]{0:T(128)} custom-call(s32[4]{0:T(128)} %adapter_ref.1, s32[8]{0:T(128)} %table_ref.1), custom_call_target="tpu_custom_call" | custom-call | tf_op jit(solution)/shard_map/slots/pallas_call | solution.py:99
  9.8 0.9 %fusion = (bf16[5,64,128]{2,1,0:T(8,128)(2,1)S(1)}, bf16[5,64,128]{2,1,0:T(8,128)(2,1)S(1)}) fusion(bf16[20,64,128]{2,1,0:T(8,128)(2,1)} %bitcast.14), kind=kLoop, calls=%fused_computation.6 | loop fusion | bytes 327680 | tf_op jit(solution)/shard_map/slice | solution.py:210
  10.8 1.0 %collective-permute-done.2.refs_3_ = bf16[8,64,128]{2,1,0:T(8,128)(2,1)S(1)} collective-permute-done((bf16[8,64,128]{2,1,0:T(8,128)(2,1)S(1)}, bf16[8,64,128]{2,1,0:T(8,128)(2,1)S(1)}, u32[]{:S(2)}, u32[]{:S(2)}) %collective-permute-start.2) | collective-permute-done | bytes 131104 | tf_op jit(solution)/shard_map/ppermute | solution.py:29
  11.8 0.7 %copy-done.3 = s32[4]{0:T(128)S(1)} copy-done((s32[4]{0:T(128)S(1)}, s32[4]{0:T(128)}, u32[]{:S(2)}) %copy-start.3) | copy-done | bytes 40
  12.5 0.6 %choose.2 = (bf16[8,64,128]{2,1,0:T(8,128)(2,1)S(1)}, bf16[8,64,128]{2,1,0:T(8,128)(2,1)S(1)}, bf16[8,64,128]{2,1,0:T(8,128)(2,1)S(1)}) custom-call(s32[4]{0:T(128)S(1)} %copy-done.3, bf16[8,64,128]{2,1,0:T(8,128)(2,1)S(1)} %get-tuple-element.44.refs_0_, bf16[8,64,128]{2,1,0:T(8,128)(2,1)S(1)} %collective-permute-done.refs_1_, ...), custom_call_target="tpu_custom_call" | custom-call | flops 3000000000 | bytes 30000000 | tf_op jit(solution)/shard_map/choose/pallas_call | solution.py:81
  13.1 1.8 %collective-permute-start.3 = (bf16[8,64,128]{2,1,0:T(8,128)(2,1)S(1)}, bf16[8,64,128]{2,1,0:T(8,128)(2,1)S(1)}, u32[]{:S(2)}, u32[]{:S(2)}) collective-permute-start(bf16[8,64,128]{2,1,0:T(8,128)(2,1)S(1)} %get-tuple-element.23), channel_id=1, source_target_pairs={{0,4},{2,6},{4,0},{6,2},{8,12},{10,14},{12,8},{14,10},{1,5},{3,7},... | collective-permute-start | bytes 393224 | tf_op jit(solution)/shard_map/ppermute | solution.py:29
  14.9 2.6 %collective-permute-start.4 = (bf16[8,64,128]{2,1,0:T(8,128)(2,1)S(1)}, bf16[8,64,128]{2,1,0:T(8,128)(2,1)S(1)}, u32[]{:S(2)}, u32[]{:S(2)}) collective-permute-start(bf16[8,64,128]{2,1,0:T(8,128)(2,1)S(1)} %get-tuple-element.24), channel_id=1, source_target_pairs={{0,8},{2,10},{4,12},{6,14},{8,0},{10,2},{12,4},{14,6},{1,9},{3,11}... | collective-permute-start | bytes 393224 | tf_op jit(solution)/shard_map/ppermute | solution.py:29
  17.5 0.1 collective-permute-start.5
  17.6 1.7 %collective-permute-start.8 = (bf16[256,1024]{1,0:T(8,128)(2,1)S(1)}, bf16[256,1024]{1,0:T(8,128)(2,1)S(1)}, u32[]{:S(2)}, u32[]{:S(2)}) collective-permute-start(bf16[256,1024]{1,0:T(8,128)(2,1)S(1)} %pad_maximum_fusion), channel_id=1, source_target_pairs={{0,2},{2,0},{4,6},{6,4},{8,10},{10,8},{12,14},{14,12},{1,3},{3,1},... | collective-permute-start | bytes 1572872 | tf_op jit(solution)/shard_map/ppermute | solution.py:29
  19.4 0.7 %collective-permute-start.7 = (bf16[10,64,128]{2,1,0:T(8,128)(2,1)S(1)}, bf16[10,64,128]{2,1,0:T(8,128)(2,1)S(1)}, u32[]{:S(2)}, u32[]{:S(2)}) collective-permute-start(bf16[10,64,128]{2,1,0:T(8,128)(2,1)S(1)} %pad_maximum_fusion.1), channel_id=1, source_target_pairs={{0,4},{2,6},{4,0},{6,2},{8,12},{10,14},{12,8},{14,10},{1,5},{3,7},... | collective-permute-start | bytes 491528 | tf_op jit(solution)/shard_map/ppermute | solution.py:29
  20.1 5.9 %collective-permute-done.4.refs_5_ = bf16[8,64,128]{2,1,0:T(8,128)(2,1)S(1)} collective-permute-done((bf16[8,64,128]{2,1,0:T(8,128)(2,1)S(1)}, bf16[8,64,128]{2,1,0:T(8,128)(2,1)S(1)}, u32[]{:S(2)}, u32[]{:S(2)}) %collective-permute-start.4) | collective-permute-done | bytes 131104 | tf_op jit(solution)/shard_map/ppermute | solution.py:29
  26.0 1.1 %collective-permute-done.5.refs_6_ = bf16[8,64,128]{2,1,0:T(8,128)(2,1)S(1)} collective-permute-done((bf16[8,64,128]{2,1,0:T(8,128)(2,1)S(1)}, bf16[8,64,128]{2,1,0:T(8,128)(2,1)S(1)}, u32[]{:S(2)}, u32[]{:S(2)}) %collective-permute-start.5) | collective-permute-done | bytes 131104 | tf_op jit(solution)/shard_map/ppermute | solution.py:29
  27.1 0.6 %assemble.2.held_ref = bf16[2,8,64,128]{3,2,1,0:T(8,128)(2,1)S(1)} custom-call(s32[4]{0:T(128)S(1)} %copy-done.3, bf16[8,64,128]{2,1,0:T(8,128)(2,1)S(1)} %get-tuple-element.44.refs_0_, bf16[8,64,128]{2,1,0:T(8,128)(2,1)S(1)} %collective-permute-done.refs_1_, bf16[8,64,128]{2,1,0:T(8,128)(2,1)S(1)} %collective-permute-done.1.refs_2_, ...), custom_call_target="tpu_custom_call" | custom-call | flops 3000000000 | bytes 30000000 | tf_op jit(solution)/shard_map/assemble/pallas_call | solution.py:81
  27.7 0.6 %choose.3 = (bf16[5,64,128]{2,1,0:T(8,128)(2,1)S(1)}, bf16[5,64,128]{2,1,0:T(8,128)(2,1)S(1)}, bf16[5,64,128]{2,1,0:T(8,128)(2,1)S(1)}) custom-call(s32[4]{0:T(128)S(1)} %copy-done.3, bf16[5,64,128]{2,1,0:T(8,128)(2,1)S(1)} %get-tuple-element.28.refs_0_, bf16[5,64,128]{2,1,0:T(8,128)(2,1)S(1)} %get-tuple-element.29.refs_1_, ...), custom_call_target="tpu_custom_call" | custom-call | tf_op jit(solution)/shard_map/choose/pallas_call | solution.py:81
  28.4 1.6 %collective-permute-start.11 = (bf16[5,64,128]{2,1,0:T(8,128)(2,1)S(1)}, bf16[5,64,128]{2,1,0:T(8,128)(2,1)S(1)}, u32[]{:S(2)}, u32[]{:S(2)}) collective-permute-start(bf16[5,64,128]{2,1,0:T(8,128)(2,1)S(1)} %get-tuple-element.32), channel_id=1, source_target_pairs={{0,4},{2,6},{4,0},{6,2},{8,12},{10,14},{12,8},{14,10},{1,5},{3,7},... | collective-permute-start | bytes 245768 | tf_op jit(solution)/shard_map/ppermute | solution.py:29
  30.0 1.8 %collective-permute-start.12 = (bf16[5,64,128]{2,1,0:T(8,128)(2,1)S(1)}, bf16[5,64,128]{2,1,0:T(8,128)(2,1)S(1)}, u32[]{:S(2)}, u32[]{:S(2)}) collective-permute-start(bf16[5,64,128]{2,1,0:T(8,128)(2,1)S(1)} %get-tuple-element.33), channel_id=1, source_target_pairs={{0,8},{2,10},{4,12},{6,14},{8,0},{10,2},{12,4},{14,6},{1,9},{3,11}... | collective-permute-start | bytes 245768 | tf_op jit(solution)/shard_map/ppermute | solution.py:29
  31.8 1.1 %collective-permute-start.13 = (bf16[5,64,128]{2,1,0:T(8,128)(2,1)S(1)}, bf16[5,64,128]{2,1,0:T(8,128)(2,1)S(1)}, u32[]{:S(2)}, u32[]{:S(2)}) collective-permute-start(bf16[5,64,128]{2,1,0:T(8,128)(2,1)S(1)} %get-tuple-element.34), channel_id=1, source_target_pairs={{0,12},{2,14},{4,8},{6,10},{8,4},{10,6},{12,0},{14,2},{1,13},{3,15... | collective-permute-start | bytes 245768 | tf_op jit(solution)/shard_map/ppermute | solution.py:29
  32.8 0.9 %collective-permute-start.9 = (bf16[2,8,64,128]{3,2,1,0:T(8,128)(2,1)S(1)}, bf16[2,8,64,128]{3,2,1,0:T(8,128)(2,1)S(1)}, u32[]{:S(2)}, u32[]{:S(2)}) collective-permute-start(bf16[2,8,64,128]{3,2,1,0:T(8,128)(2,1)S(1)} %assemble.2.held_ref), channel_id=1, source_target_pairs={{0,2},{2,0},{4,6},{6,4},{8,10},{10,8},{12,14},{14,12},{1,3},{3,1},... | collective-permute-start | bytes 786440 | tf_op jit(solution)/shard_map/ppermute | solution.py:29
  33.7 2.7 %attend.1.context_ref = bf16[4,256,1024]{2,1,0:T(8,128)(2,1)S(1)} custom-call(bf16[256,4096]{1,0:T(8,128)(2,1)S(1)} %copy-done, bf16[256,512]{1,0:T(8,128)(2,1)S(1)} %copy-done.1, bf16[256,512]{1,0:T(8,128)(2,1)S(1)} %copy-done.2, bf16[256,1024]{1,0:T(8,128)(2,1)S(1)} %collective-permute-done.8.far_ref), custom_call_target="tpu_custom_call" | custom-call | tf_op jit(solution)/shard_map/attend/pallas_call | solution.py:81
  36.4 1.8 %collective-permute-done.12.refs_5_ = bf16[5,64,128]{2,1,0:T(8,128)(2,1)S(1)} collective-permute-done((bf16[5,64,128]{2,1,0:T(8,128)(2,1)S(1)}, bf16[5,64,128]{2,1,0:T(8,128)(2,1)S(1)}, u32[]{:S(2)}, u32[]{:S(2)}) %collective-permute-start.12) | collective-permute-done | bytes 81952 | tf_op jit(solution)/shard_map/ppermute | solution.py:29
  38.2 0.6 %assemble.3.refs_0_ = bf16[2,5,64,128]{3,2,1,0:T(8,128)(2,1)S(1)} custom-call(s32[4]{0:T(128)S(1)} %copy-done.3, bf16[5,64,128]{2,1,0:T(8,128)(2,1)S(1)} %get-tuple-element.28.refs_0_, bf16[5,64,128]{2,1,0:T(8,128)(2,1)S(1)} %get-tuple-element.29.refs_1_, bf16[5,64,128]{2,1,0:T(8,128)(2,1)S(1)} %get-tuple-element.30.refs_2_, ...), custom_call_target="tpu_custom_call" | custom-call | flops 1000000000 | bytes 10000000 | tf_op jit(solution)/shard_map/assemble/pallas_call | solution.py:81
  38.8 1.9 %collective-permute-start.14 = (bf16[2,5,64,128]{3,2,1,0:T(8,128)(2,1)S(1)}, bf16[2,5,64,128]{3,2,1,0:T(8,128)(2,1)S(1)}, u32[]{:S(2)}, u32[]{:S(2)}) collective-permute-start(bf16[2,5,64,128]{3,2,1,0:T(8,128)(2,1)S(1)} %assemble.3.refs_0_), channel_id=1, source_target_pairs={{0,2},{2,0},{4,6},{6,4},{8,10},{10,8},{12,14},{14,12},{1,3},{3,1},... | collective-permute-start | bytes 491528 | tf_op jit(solution)/shard_map/ppermute | solution.py:29
  40.7 1.2 %rank_mix.1.near_ref = f32[256,64]{1,0:T(8,128)S(1)} custom-call(s32[4]{0:T(128)S(1)} %copy-done.3, bf16[4,256,1024]{2,1,0:T(8,128)(2,1)S(1)} %attend.1.context_ref, bf16[2,8,64,128]{3,2,1,0:T(8,128)(2,1)S(1)} %assemble.2.held_ref, bf16[2,8,64,128]{3,2,1,0:T(8,128)(2,1)S(1)} %collective-permute-done.9.got_ref), custom_call_target="tpu_custom_call" | custom-call | tf_op jit(solution)/shard_map/rank_mix/pallas_call | solution.py:81
  41.9 0.1 collective-permute-start.10
  42.0 1.3 %collective-permute-done.10.far_ref = f32[256,64]{1,0:T(8,128)S(1)} collective-permute-done((f32[256,64]{1,0:T(8,128)S(1)}, f32[256,64]{1,0:T(8,128)S(1)}, u32[]{:S(2)}, u32[]{:S(2)}) %collective-permute-start.10) | collective-permute-done | bytes 65568 | tf_op jit(solution)/shard_map/ppermute | solution.py:29
  43.3 0.8 %collective-permute-done.14.refs_1_ = bf16[2,5,64,128]{3,2,1,0:T(8,128)(2,1)S(1)} collective-permute-done((bf16[2,5,64,128]{3,2,1,0:T(8,128)(2,1)S(1)}, bf16[2,5,64,128]{3,2,1,0:T(8,128)(2,1)S(1)}, u32[]{:S(2)}, u32[]{:S(2)}) %collective-permute-start.14) | collective-permute-done | bytes 163872 | tf_op jit(solution)/shard_map/ppermute | solution.py:29
  44.2 1.9 %delta.1 = bf16[256,2560]{1,0:T(8,128)(2,1)} custom-call(s32[4]{0:T(128)S(1)} %copy-done.3, f32[256,64]{1,0:T(8,128)S(1)} %rank_mix.1.near_ref, f32[256,64]{1,0:T(8,128)S(1)} %collective-permute-done.10.far_ref, bf16[2,5,64,128]{3,2,1,0:T(8,128)(2,1)S(1)} %assemble.3.refs_0_, bf16[2,5,64,128]{3,2,1,0:T(8,128)(2,1)S(1)} %collective-permute-done.14.refs_1_), custom_call_target="tpu_custom_call" | custom-call | tf_op jit(solution)/shard_map/delta/pallas_call | solution.py:182
  (21 shorter events, 0.1 us)
Async XLA Ops:
  1.1 9.7 %collective-permute-start = (bf16[8,64,128]{2,1,0:T(8,128)(2,1)S(1)}, bf16[8,64,128]{2,1,0:T(8,128)(2,1)S(1)}, u32[]{:S(2)}, u32[]{:S(2)}) collective-permute-start(bf16[8,64,128]{2,1,0:T(8,128)(2,1)S(1)} %get-tuple-element.43), channel_id=1, source_target_pairs={{0,2},{2,0},{4,6},{6,4},{8,10},{10,8},{12,14},{14,12},{1,3},{3,1},... | collective-permute-start | bytes 393224 | tf_op jit(solution)/shard_map/ppermute | solution.py:29
  4.1 6.7 %collective-permute-start.1 = (bf16[8,64,128]{2,1,0:T(8,128)(2,1)S(1)}, bf16[8,64,128]{2,1,0:T(8,128)(2,1)S(1)}, u32[]{:S(2)}, u32[]{:S(2)}) collective-permute-start(bf16[8,64,128]{2,1,0:T(8,128)(2,1)S(1)} %get-tuple-element.42), channel_id=1, source_target_pairs={{0,4},{2,6},{4,0},{6,2},{8,12},{10,14},{12,8},{14,10},{1,5},{3,7},... | collective-permute-start | bytes 393224 | tf_op jit(solution)/shard_map/ppermute | solution.py:29
  5.7 6.1 %collective-permute-start.2 = (bf16[8,64,128]{2,1,0:T(8,128)(2,1)S(1)}, bf16[8,64,128]{2,1,0:T(8,128)(2,1)S(1)}, u32[]{:S(2)}, u32[]{:S(2)}) collective-permute-start(bf16[8,64,128]{2,1,0:T(8,128)(2,1)S(1)} %get-tuple-element.41), channel_id=1, source_target_pairs={{0,6},{2,4},{4,2},{6,0},{8,14},{10,12},{12,10},{14,8},{1,7},{3,5},... | collective-permute-start | bytes 393224 | tf_op jit(solution)/shard_map/ppermute | solution.py:29
  6.6 12.7 %collective-permute-start.6 = (bf16[10,64,128]{2,1,0:T(8,128)(2,1)S(1)}, bf16[10,64,128]{2,1,0:T(8,128)(2,1)S(1)}, u32[]{:S(2)}, u32[]{:S(2)}) collective-permute-start(bf16[10,64,128]{2,1,0:T(8,128)(2,1)S(1)} %slice.57), channel_id=1, source_target_pairs={{0,2},{2,0},{4,6},{6,4},{8,10},{10,8},{12,14},{14,12},{1,3},{3,1},... | collective-permute-start | bytes 491528 | tf_op jit(solution)/shard_map/ppermute | solution.py:29
  10.8 6.8 %copy-start.1 = (bf16[256,512]{1,0:T(8,128)(2,1)S(1)}, bf16[256,512]{1,0:T(8,128)(2,1)}, u32[]{:S(2)}) copy-start(bf16[256,512]{1,0:T(8,128)(2,1)} %key_ref.1) | copy-start | bytes 786436
  10.8 6.8 %copy-start.2 = (bf16[256,512]{1,0:T(8,128)(2,1)S(1)}, bf16[256,512]{1,0:T(8,128)(2,1)}, u32[]{:S(2)}) copy-start(bf16[256,512]{1,0:T(8,128)(2,1)} %value_ref.1) | copy-start | bytes 786436
  11.8 0.7 %copy-start.3 = (s32[4]{0:T(128)S(1)}, s32[4]{0:T(128)}, u32[]{:S(2)}) copy-start(s32[4]{0:T(128)} %slots.1.slots_ref) | copy-start | bytes 52
  13.1 7.0 %collective-permute-start.3 = (bf16[8,64,128]{2,1,0:T(8,128)(2,1)S(1)}, bf16[8,64,128]{2,1,0:T(8,128)(2,1)S(1)}, u32[]{:S(2)}, u32[]{:S(2)}) collective-permute-start(bf16[8,64,128]{2,1,0:T(8,128)(2,1)S(1)} %get-tuple-element.23), channel_id=1, source_target_pairs={{0,4},{2,6},{4,0},{6,2},{8,12},{10,14},{12,8},{14,10},{1,5},{3,7},... | collective-permute-start | bytes 393224 | tf_op jit(solution)/shard_map/ppermute | solution.py:29
  14.9 11.1 %collective-permute-start.4 = (bf16[8,64,128]{2,1,0:T(8,128)(2,1)S(1)}, bf16[8,64,128]{2,1,0:T(8,128)(2,1)S(1)}, u32[]{:S(2)}, u32[]{:S(2)}) collective-permute-start(bf16[8,64,128]{2,1,0:T(8,128)(2,1)S(1)} %get-tuple-element.24), channel_id=1, source_target_pairs={{0,8},{2,10},{4,12},{6,14},{8,0},{10,2},{12,4},{14,6},{1,9},{3,11}... | collective-permute-start | bytes 393224 | tf_op jit(solution)/shard_map/ppermute | solution.py:29
  17.5 9.6 %collective-permute-start.5 = (bf16[8,64,128]{2,1,0:T(8,128)(2,1)S(1)}, bf16[8,64,128]{2,1,0:T(8,128)(2,1)S(1)}, u32[]{:S(2)}, u32[]{:S(2)}) collective-permute-start(bf16[8,64,128]{2,1,0:T(8,128)(2,1)S(1)} %get-tuple-element.25), channel_id=1, source_target_pairs={{0,12},{2,14},{4,8},{6,10},{8,4},{10,6},{12,0},{14,2},{1,13},{3,15... | collective-permute-start | bytes 393224 | tf_op jit(solution)/shard_map/ppermute | solution.py:29
  17.6 16.1 %collective-permute-start.8 = (bf16[256,1024]{1,0:T(8,128)(2,1)S(1)}, bf16[256,1024]{1,0:T(8,128)(2,1)S(1)}, u32[]{:S(2)}, u32[]{:S(2)}) collective-permute-start(bf16[256,1024]{1,0:T(8,128)(2,1)S(1)} %pad_maximum_fusion), channel_id=1, source_target_pairs={{0,2},{2,0},{4,6},{6,4},{8,10},{10,8},{12,14},{14,12},{1,3},{3,1},... | collective-permute-start | bytes 1572872 | tf_op jit(solution)/shard_map/ppermute | solution.py:29
  19.4 8.3 %collective-permute-start.7 = (bf16[10,64,128]{2,1,0:T(8,128)(2,1)S(1)}, bf16[10,64,128]{2,1,0:T(8,128)(2,1)S(1)}, u32[]{:S(2)}, u32[]{:S(2)}) collective-permute-start(bf16[10,64,128]{2,1,0:T(8,128)(2,1)S(1)} %pad_maximum_fusion.1), channel_id=1, source_target_pairs={{0,4},{2,6},{4,0},{6,2},{8,12},{10,14},{12,8},{14,10},{1,5},{3,7},... | collective-permute-start | bytes 491528 | tf_op jit(solution)/shard_map/ppermute | solution.py:29
  27.1 6.6 %copy-start = (bf16[256,4096]{1,0:T(8,128)(2,1)S(1)}, bf16[256,4096]{1,0:T(8,128)(2,1)}, u32[]{:S(2)}) copy-start(bf16[256,4096]{1,0:T(8,128)(2,1)} %query_ref.1) | copy-start | bytes 6291460
  28.4 8.1 %collective-permute-start.11 = (bf16[5,64,128]{2,1,0:T(8,128)(2,1)S(1)}, bf16[5,64,128]{2,1,0:T(8,128)(2,1)S(1)}, u32[]{:S(2)}, u32[]{:S(2)}) collective-permute-start(bf16[5,64,128]{2,1,0:T(8,128)(2,1)S(1)} %get-tuple-element.32), channel_id=1, source_target_pairs={{0,4},{2,6},{4,0},{6,2},{8,12},{10,14},{12,8},{14,10},{1,5},{3,7},... | collective-permute-start | bytes 245768 | tf_op jit(solution)/shard_map/ppermute | solution.py:29
  30.0 8.2 %collective-permute-start.12 = (bf16[5,64,128]{2,1,0:T(8,128)(2,1)S(1)}, bf16[5,64,128]{2,1,0:T(8,128)(2,1)S(1)}, u32[]{:S(2)}, u32[]{:S(2)}) collective-permute-start(bf16[5,64,128]{2,1,0:T(8,128)(2,1)S(1)} %get-tuple-element.33), channel_id=1, source_target_pairs={{0,8},{2,10},{4,12},{6,14},{8,0},{10,2},{12,4},{14,6},{1,9},{3,11}... | collective-permute-start | bytes 245768 | tf_op jit(solution)/shard_map/ppermute | solution.py:29
  31.8 6.4 %collective-permute-start.13 = (bf16[5,64,128]{2,1,0:T(8,128)(2,1)S(1)}, bf16[5,64,128]{2,1,0:T(8,128)(2,1)S(1)}, u32[]{:S(2)}, u32[]{:S(2)}) collective-permute-start(bf16[5,64,128]{2,1,0:T(8,128)(2,1)S(1)} %get-tuple-element.34), channel_id=1, source_target_pairs={{0,12},{2,14},{4,8},{6,10},{8,4},{10,6},{12,0},{14,2},{1,13},{3,15... | collective-permute-start | bytes 245768 | tf_op jit(solution)/shard_map/ppermute | solution.py:29
  32.8 7.9 %collective-permute-start.9 = (bf16[2,8,64,128]{3,2,1,0:T(8,128)(2,1)S(1)}, bf16[2,8,64,128]{3,2,1,0:T(8,128)(2,1)S(1)}, u32[]{:S(2)}, u32[]{:S(2)}) collective-permute-start(bf16[2,8,64,128]{3,2,1,0:T(8,128)(2,1)S(1)} %assemble.2.held_ref), channel_id=1, source_target_pairs={{0,2},{2,0},{4,6},{6,4},{8,10},{10,8},{12,14},{14,12},{1,3},{3,1},... | collective-permute-start | bytes 786440 | tf_op jit(solution)/shard_map/ppermute | solution.py:29
  38.8 5.4 %collective-permute-start.14 = (bf16[2,5,64,128]{3,2,1,0:T(8,128)(2,1)S(1)}, bf16[2,5,64,128]{3,2,1,0:T(8,128)(2,1)S(1)}, u32[]{:S(2)}, u32[]{:S(2)}) collective-permute-start(bf16[2,5,64,128]{3,2,1,0:T(8,128)(2,1)S(1)} %assemble.3.refs_0_), channel_id=1, source_target_pairs={{0,2},{2,0},{4,6},{6,4},{8,10},{10,8},{12,14},{14,12},{1,3},{3,1},... | collective-permute-start | bytes 491528 | tf_op jit(solution)/shard_map/ppermute | solution.py:29
  41.9 1.4 %collective-permute-start.10 = (f32[256,64]{1,0:T(8,128)S(1)}, f32[256,64]{1,0:T(8,128)S(1)}, u32[]{:S(2)}, u32[]{:S(2)}) collective-permute-start(f32[256,64]{1,0:T(8,128)S(1)} %rank_mix.1.near_ref), channel_id=1, source_target_pairs={{0,1},{1,0},{2,3},{3,2},{4,5},{5,4},{6,7},{7,6},{8,9},{9,8},{10,11... | collective-permute-start | bytes 196616 | tf_op jit(solution)/shard_map/ppermute | solution.py:29

commit v6 on v5

--- a/solution.py
+++ b/solution.py
@@ -106,6 +106,13 @@
     )(request_adapter, adapter_slot_table)
 
 
+def own_kernel(slots_ref, blocks_ref, near_ref, rest_ref):
+    del slots_ref
+    count = near_ref.shape[0]
+    near_ref[...] = blocks_ref[:count]
+    rest_ref[...] = blocks_ref[count : 2 * count]
+
+
 def take(request, me, slots_ref, quarter_refs, out_ref, at, other=None):
     where = slots_ref[request] ^ me
     for k in range(4):
@@ -205,10 +212,10 @@
 
 
 def spread_in_turn(over_x, own, earlier):
-    count = own.shape[0] // 2
+    count = own[0].shape[0]
     over_x = after(earlier, over_x)
-    over_z = swapped(jnp.concatenate([own[count:], over_x[count:]]), "req", 2)
-    return [own[:count], over_x[:count], over_z[:count], over_z[count:]]
+    over_z = swapped(jnp.concatenate([own[1], over_x[count:]]), "req", 2)
+    return [own[0], over_x[:count], over_z[:count], over_z[count:]]
 
 
 def deliver(slots, quarters, weight=0):
@@ -228,7 +235,9 @@
     down_quarters = spread(down_cut)
     half = up.shape[0] // 2
     up = after(down_cut, up)
-    up_half, up_own = up[half:], up[:half]
+    up_half = up[half:]
+    quarter = jax.ShapeDtypeStruct((half // 2, *up.shape[1:]), up.dtype)
+    up_own = in_vmem(own_kernel, "own", [quarter] * 2, slots, up)
     up_over_x = swapped(up_half, "req", 1)
     down_sent, down_came = deliver(slots, down_quarters, WEIGHT)
     far = swapped(jnp.concatenate(after(down_sent, (keys, values)), axis=1), "req", 1)

time: 46.2 us -> 45.4 us (0.983)
  waiting for transfers between devices: 11.9 us -> 10.7 us
  Pallas kernels: 9.39 us -> 9.94 us
    ppermute x15, waiting for transfers between devices: 11.9 us -> 10.7 us  [swapped(): return lax.ppermute(shard, axis, [(i, i ^ mask) for i in range(size)])]
    unnamed x8 -> x10, local copies, waits for them, and re-layouts: 0.67 us -> 1.64 us
    slice x4 -> x3, local copies, waits for them, and re-layouts: 1.89 us -> 0.95 us  [the longest x1 0.93 us: eight_way(): up_half = up[half:]]
    pallas_call x6 -> x7, Pallas kernels: 6.34 us -> 6.89 us  [in_vmem(): pl.pallas_call(kernel, in_specs=[pl.BlockSpec(memory_space=pltpu.SMEM)] *...]
  transfers between devices with their start and end apart: 15 -> 15, of which waited for: 6 -> 7; matrix products, arithmetic and copies ran while one was open for 4% -> 2% of each run, Pallas kernels for 16% -> 18%
where the time goes in v6:
time: 45.4 us; the launch traced here: 45.2 us
  starting transfers between devices  20.6 us (45%)
  waiting for transfers between devices  10.7 us (24%)
  Pallas kernels  9.94 us (22%)
  local copies, waits for them, and re-layouts  3.72 us (8%)
    ppermute x15, starting transfers between devices, swapped(): return lax.ppermute(shard, axis, [(i, i ^ mask) for i in range(size)])  20.6 us
    ppermute x15, waiting for transfers between devices, swapped(): return lax.ppermute(shard, axis, [(i, i ^ mask) for i in range(size)])  10.7 us
    pallas_call x7, Pallas kernels, in_vmem(): pl.pallas_call(kernel, in_specs=[pl.BlockSpec(memory_space=pltpu.SMEM)] *...  6.89 us
    pallas_call x1, Pallas kernels, delta_of(): pl.pallas_call(delta_kernel, in_specs=[pl.BlockSpec(memory_space=pltpu.SM...  1.86 us
    unnamed x10, local copies, waits for them, and re-layouts  1.64 us
    pallas_call x1, Pallas kernels, slots_of(): pl.pallas_call(slots_kernel, in_specs=[pl.BlockSpec(memory_space=pltpu.SM...  1.2 us
    slice x1, local copies, waits for them, and re-layouts, quarter_cut(): return [blocks[k * count:(k + 1) * count] for k in range(4)]  1.13 us
    slice x1, local copies, waits for them, and re-layouts, eight_way(): up_half = up[half:]  0.93 us
  transfers between devices with their start and end apart: 15, of which 7 were waited for; matrix products, arithmetic and copies ran while one was open for 2% of the time, Pallas kernels for 18%

profile of v6, /device:TPU:0, one launch (start us, length us, event | category | flops | bytes accessed | tf_op | source)
XLA Modules:
  0.0 45.2 jit_solution(2361301961313948677)
XLA Ops:
  0.0 1.1 %slice_bitcast_fusion = (bf16[8,64,128]{2,1,0:T(8,128)(2,1)S(1)}, bf16[8,64,128]{2,1,0:T(8,128)(2,1)S(1)}, bf16[8,64,128]{2,1,0:T(8,128)(2,1)S(1)}, bf16[8,64,128]{2,1,0:T(8,128)(2,1)S(1)}) fusion(bf16[1,32,64,128]{3,2,1,0:T(8,128)(2,1)} %bitcast.14), kind=kLoop, calls=%fused_computation.2 | loop fusion | bytes 1048576 | tf_op jit(solution)/shard_map/slice | solution.py:203
  1.1 3.0 %collective-permute-start = (bf16[8,64,128]{2,1,0:T(8,128)(2,1)S(1)}, bf16[8,64,128]{2,1,0:T(8,128)(2,1)S(1)}, u32[]{:S(2)}, u32[]{:S(2)}) collective-permute-start(bf16[8,64,128]{2,1,0:T(8,128)(2,1)S(1)} %get-tuple-element.47), channel_id=1, source_target_pairs={{0,2},{2,0},{4,6},{6,4},{8,10},{10,8},{12,14},{14,12},{1,3},{3,1},... | collective-permute-start | bytes 393224 | tf_op jit(solution)/shard_map/ppermute | solution.py:29
  4.1 1.6 %collective-permute-start.1 = (bf16[8,64,128]{2,1,0:T(8,128)(2,1)S(1)}, bf16[8,64,128]{2,1,0:T(8,128)(2,1)S(1)}, u32[]{:S(2)}, u32[]{:S(2)}) collective-permute-start(bf16[8,64,128]{2,1,0:T(8,128)(2,1)S(1)} %get-tuple-element.46), channel_id=1, source_target_pairs={{0,4},{2,6},{4,0},{6,2},{8,12},{10,14},{12,8},{14,10},{1,5},{3,7},... | collective-permute-start | bytes 393224 | tf_op jit(solution)/shard_map/ppermute | solution.py:29
  5.7 0.9 %slice.47 = bf16[10,64,128]{2,1,0:T(8,128)(2,1)S(1)} slice(bf16[20,64,128]{2,1,0:T(8,128)(2,1)} %bitcast.12), slice={[10:20], [0:64], [0:128]} | slice | bytes 327680 | tf_op jit(solution)/shard_map/slice | solution.py:238
  6.6 2.0 %collective-permute-start.6 = (bf16[10,64,128]{2,1,0:T(8,128)(2,1)S(1)}, bf16[10,64,128]{2,1,0:T(8,128)(2,1)S(1)}, u32[]{:S(2)}, u32[]{:S(2)}) collective-permute-start(bf16[10,64,128]{2,1,0:T(8,128)(2,1)S(1)} %slice.47), channel_id=1, source_target_pairs={{0,2},{2,0},{4,6},{6,4},{8,10},{10,8},{12,14},{14,12},{1,3},{3,1},... | collective-permute-start | bytes 491528 | tf_op jit(solution)/shard_map/ppermute | solution.py:29
  8.6 1.2 %slots.1.slots_ref = s32[4]{0:T(128)} custom-call(s32[4]{0:T(128)} %adapter_ref.1, s32[8]{0:T(128)} %table_ref.1), custom_call_target="tpu_custom_call" | custom-call | tf_op jit(solution)/shard_map/slots/pallas_call | solution.py:99
  9.8 1.0 %copy-done.3 = bf16[1,64,20,128]{3,1,2,0:T(8,128)(2,1)S(1)} copy-done((bf16[1,64,20,128]{3,1,2,0:T(8,128)(2,1)S(1)}, bf16[1,64,20,128]{3,1,2,0:T(8,128)(2,1)}, u32[]{:S(2)}) %copy-start.3) | copy-done | bytes 327704
  10.8 0.7 %copy-done.4 = s32[4]{0:T(128)S(1)} copy-done((s32[4]{0:T(128)S(1)}, s32[4]{0:T(128)}, u32[]{:S(2)}) %copy-start.4) | copy-done | bytes 40
  11.5 0.6 %own.1 = (bf16[5,64,128]{2,1,0:T(8,128)(2,1)S(1)}, bf16[5,64,128]{2,1,0:T(8,128)(2,1)S(1)}) custom-call(s32[4]{0:T(128)S(1)} %copy-done.4, bf16[20,64,128]{2,1,0:T(8,128)(2,1)S(1)} %bitcast.13), custom_call_target="tpu_custom_call" | custom-call | tf_op jit(solution)/shard_map/own/pallas_call | solution.py:81
  12.1 0.6 %choose.2 = (bf16[8,64,128]{2,1,0:T(8,128)(2,1)S(1)}, bf16[8,64,128]{2,1,0:T(8,128)(2,1)S(1)}, bf16[8,64,128]{2,1,0:T(8,128)(2,1)S(1)}) custom-call(s32[4]{0:T(128)S(1)} %copy-done.4, bf16[8,64,128]{2,1,0:T(8,128)(2,1)S(1)} %get-tuple-element.48.refs_0_, bf16[8,64,128]{2,1,0:T(8,128)(2,1)S(1)} %collective-permute-done.refs_1_, ...), custom_call_target="tpu_custom_call" | custom-call | flops 3000000000 | bytes 30000000 | tf_op jit(solution)/shard_map/choose/pallas_call | solution.py:81
  12.7 1.6 %collective-permute-start.3 = (bf16[8,64,128]{2,1,0:T(8,128)(2,1)S(1)}, bf16[8,64,128]{2,1,0:T(8,128)(2,1)S(1)}, u32[]{:S(2)}, u32[]{:S(2)}) collective-permute-start(bf16[8,64,128]{2,1,0:T(8,128)(2,1)S(1)} %get-tuple-element.25), channel_id=1, source_target_pairs={{0,4},{2,6},{4,0},{6,2},{8,12},{10,14},{12,8},{14,10},{1,5},{3,7},... | collective-permute-start | bytes 393224 | tf_op jit(solution)/shard_map/ppermute | solution.py:29
  14.4 2.6 %collective-permute-start.4 = (bf16[8,64,128]{2,1,0:T(8,128)(2,1)S(1)}, bf16[8,64,128]{2,1,0:T(8,128)(2,1)S(1)}, u32[]{:S(2)}, u32[]{:S(2)}) collective-permute-start(bf16[8,64,128]{2,1,0:T(8,128)(2,1)S(1)} %get-tuple-element.26), channel_id=1, source_target_pairs={{0,8},{2,10},{4,12},{6,14},{8,0},{10,2},{12,4},{14,6},{1,9},{3,11}... | collective-permute-start | bytes 393224 | tf_op jit(solution)/shard_map/ppermute | solution.py:29
  17.2 1.4 %collective-permute-start.8 = (bf16[256,1024]{1,0:T(8,128)(2,1)S(1)}, bf16[256,1024]{1,0:T(8,128)(2,1)S(1)}, u32[]{:S(2)}, u32[]{:S(2)}) collective-permute-start(bf16[256,1024]{1,0:T(8,128)(2,1)S(1)} %pad_maximum_fusion), channel_id=1, source_target_pairs={{0,2},{2,0},{4,6},{6,4},{8,10},{10,8},{12,14},{14,12},{1,3},{3,1},... | collective-permute-start | bytes 1572872 | tf_op jit(solution)/shard_map/ppermute | solution.py:29
  18.7 0.7 %collective-permute-start.7 = (bf16[10,64,128]{2,1,0:T(8,128)(2,1)S(1)}, bf16[10,64,128]{2,1,0:T(8,128)(2,1)S(1)}, u32[]{:S(2)}, u32[]{:S(2)}) collective-permute-start(bf16[10,64,128]{2,1,0:T(8,128)(2,1)S(1)} %pad_maximum_fusion.1), channel_id=1, source_target_pairs={{0,4},{2,6},{4,0},{6,2},{8,12},{10,14},{12,8},{14,10},{1,5},{3,7},... | collective-permute-start | bytes 491528 | tf_op jit(solution)/shard_map/ppermute | solution.py:29
  19.4 0.2 collective-permute-done.3.refs_4_
  19.7 5.7 %collective-permute-done.4.refs_5_ = bf16[8,64,128]{2,1,0:T(8,128)(2,1)S(1)} collective-permute-done((bf16[8,64,128]{2,1,0:T(8,128)(2,1)S(1)}, bf16[8,64,128]{2,1,0:T(8,128)(2,1)S(1)}, u32[]{:S(2)}, u32[]{:S(2)}) %collective-permute-start.4) | collective-permute-done | bytes 131104 | tf_op jit(solution)/shard_map/ppermute | solution.py:29
  25.4 1.0 %collective-permute-done.5.refs_6_ = bf16[8,64,128]{2,1,0:T(8,128)(2,1)S(1)} collective-permute-done((bf16[8,64,128]{2,1,0:T(8,128)(2,1)S(1)}, bf16[8,64,128]{2,1,0:T(8,128)(2,1)S(1)}, u32[]{:S(2)}, u32[]{:S(2)}) %collective-permute-start.5) | collective-permute-done | bytes 131104 | tf_op jit(solution)/shard_map/ppermute | solution.py:29
  26.4 0.6 %assemble.2.held_ref = bf16[2,8,64,128]{3,2,1,0:T(8,128)(2,1)S(1)} custom-call(s32[4]{0:T(128)S(1)} %copy-done.4, bf16[8,64,128]{2,1,0:T(8,128)(2,1)S(1)} %get-tuple-element.48.refs_0_, bf16[8,64,128]{2,1,0:T(8,128)(2,1)S(1)} %collective-permute-done.refs_1_, bf16[8,64,128]{2,1,0:T(8,128)(2,1)S(1)} %collective-permute-done.1.refs_2_, ...), custom_call_target="tpu_custom_call" | custom-call | flops 3000000000 | bytes 30000000 | tf_op jit(solution)/shard_map/assemble/pallas_call | solution.py:81
  27.1 0.6 %choose.3 = (bf16[5,64,128]{2,1,0:T(8,128)(2,1)S(1)}, bf16[5,64,128]{2,1,0:T(8,128)(2,1)S(1)}, bf16[5,64,128]{2,1,0:T(8,128)(2,1)S(1)}) custom-call(s32[4]{0:T(128)S(1)} %copy-done.4, bf16[5,64,128]{2,1,0:T(8,128)(2,1)S(1)} %get-tuple-element.32.refs_0_, bf16[5,64,128]{2,1,0:T(8,128)(2,1)S(1)} %get-tuple-element.33.refs_1_, ...), custom_call_target="tpu_custom_call" | custom-call | tf_op jit(solution)/shard_map/choose/pallas_call | solution.py:81
  27.7 1.7 %collective-permute-start.11 = (bf16[5,64,128]{2,1,0:T(8,128)(2,1)S(1)}, bf16[5,64,128]{2,1,0:T(8,128)(2,1)S(1)}, u32[]{:S(2)}, u32[]{:S(2)}) collective-permute-start(bf16[5,64,128]{2,1,0:T(8,128)(2,1)S(1)} %get-tuple-element.36), channel_id=1, source_target_pairs={{0,4},{2,6},{4,0},{6,2},{8,12},{10,14},{12,8},{14,10},{1,5},{3,7},... | collective-permute-start | bytes 245768 | tf_op jit(solution)/shard_map/ppermute | solution.py:29
  29.4 1.6 %collective-permute-start.12 = (bf16[5,64,128]{2,1,0:T(8,128)(2,1)S(1)}, bf16[5,64,128]{2,1,0:T(8,128)(2,1)S(1)}, u32[]{:S(2)}, u32[]{:S(2)}) collective-permute-start(bf16[5,64,128]{2,1,0:T(8,128)(2,1)S(1)} %get-tuple-element.37), channel_id=1, source_target_pairs={{0,8},{2,10},{4,12},{6,14},{8,0},{10,2},{12,4},{14,6},{1,9},{3,11}... | collective-permute-start | bytes 245768 | tf_op jit(solution)/shard_map/ppermute | solution.py:29
  31.1 1.1 %collective-permute-start.13 = (bf16[5,64,128]{2,1,0:T(8,128)(2,1)S(1)}, bf16[5,64,128]{2,1,0:T(8,128)(2,1)S(1)}, u32[]{:S(2)}, u32[]{:S(2)}) collective-permute-start(bf16[5,64,128]{2,1,0:T(8,128)(2,1)S(1)} %get-tuple-element.38), channel_id=1, source_target_pairs={{0,12},{2,14},{4,8},{6,10},{8,4},{10,6},{12,0},{14,2},{1,13},{3,15... | collective-permute-start | bytes 245768 | tf_op jit(solution)/shard_map/ppermute | solution.py:29
  32.2 0.9 %collective-permute-start.9 = (bf16[2,8,64,128]{3,2,1,0:T(8,128)(2,1)S(1)}, bf16[2,8,64,128]{3,2,1,0:T(8,128)(2,1)S(1)}, u32[]{:S(2)}, u32[]{:S(2)}) collective-permute-start(bf16[2,8,64,128]{3,2,1,0:T(8,128)(2,1)S(1)} %assemble.2.held_ref), channel_id=1, source_target_pairs={{0,2},{2,0},{4,6},{6,4},{8,10},{10,8},{12,14},{14,12},{1,3},{3,1},... | collective-permute-start | bytes 786440 | tf_op jit(solution)/shard_map/ppermute | solution.py:29
  33.1 2.7 %attend.1.context_ref = bf16[4,256,1024]{2,1,0:T(8,128)(2,1)S(1)} custom-call(bf16[256,4096]{1,0:T(8,128)(2,1)S(1)} %copy-done, bf16[256,512]{1,0:T(8,128)(2,1)S(1)} %copy-done.1, bf16[256,512]{1,0:T(8,128)(2,1)S(1)} %copy-done.2, bf16[256,1024]{1,0:T(8,128)(2,1)S(1)} %collective-permute-done.8.far_ref), custom_call_target="tpu_custom_call" | custom-call | tf_op jit(solution)/shard_map/attend/pallas_call | solution.py:81
  35.8 0.7 %collective-permute-done.12.refs_5_ = bf16[5,64,128]{2,1,0:T(8,128)(2,1)S(1)} collective-permute-done((bf16[5,64,128]{2,1,0:T(8,128)(2,1)S(1)}, bf16[5,64,128]{2,1,0:T(8,128)(2,1)S(1)}, u32[]{:S(2)}, u32[]{:S(2)}) %collective-permute-start.12) | collective-permute-done | bytes 81952 | tf_op jit(solution)/shard_map/ppermute | solution.py:29
  36.4 1.0 %collective-permute-done.13.refs_6_ = bf16[5,64,128]{2,1,0:T(8,128)(2,1)S(1)} collective-permute-done((bf16[5,64,128]{2,1,0:T(8,128)(2,1)S(1)}, bf16[5,64,128]{2,1,0:T(8,128)(2,1)S(1)}, u32[]{:S(2)}, u32[]{:S(2)}) %collective-permute-start.13) | collective-permute-done | bytes 81952 | tf_op jit(solution)/shard_map/ppermute | solution.py:29
  37.4 0.6 %assemble.3.refs_0_ = bf16[2,5,64,128]{3,2,1,0:T(8,128)(2,1)S(1)} custom-call(s32[4]{0:T(128)S(1)} %copy-done.4, bf16[5,64,128]{2,1,0:T(8,128)(2,1)S(1)} %get-tuple-element.32.refs_0_, bf16[5,64,128]{2,1,0:T(8,128)(2,1)S(1)} %get-tuple-element.33.refs_1_, bf16[5,64,128]{2,1,0:T(8,128)(2,1)S(1)} %get-tuple-element.34.refs_2_, ...), custom_call_target="tpu_custom_call" | custom-call | flops 1000000000 | bytes 10000000 | tf_op jit(solution)/shard_map/assemble/pallas_call | solution.py:81
  38.0 2.0 %collective-permute-start.14 = (bf16[2,5,64,128]{3,2,1,0:T(8,128)(2,1)S(1)}, bf16[2,5,64,128]{3,2,1,0:T(8,128)(2,1)S(1)}, u32[]{:S(2)}, u32[]{:S(2)}) collective-permute-start(bf16[2,5,64,128]{3,2,1,0:T(8,128)(2,1)S(1)} %assemble.3.refs_0_), channel_id=1, source_target_pairs={{0,2},{2,0},{4,6},{6,4},{8,10},{10,8},{12,14},{14,12},{1,3},{3,1},... | collective-permute-start | bytes 491528 | tf_op jit(solution)/shard_map/ppermute | solution.py:29
  40.0 1.2 %rank_mix.1.near_ref = f32[256,64]{1,0:T(8,128)S(1)} custom-call(s32[4]{0:T(128)S(1)} %copy-done.4, bf16[4,256,1024]{2,1,0:T(8,128)(2,1)S(1)} %attend.1.context_ref, bf16[2,8,64,128]{3,2,1,0:T(8,128)(2,1)S(1)} %assemble.2.held_ref, bf16[2,8,64,128]{3,2,1,0:T(8,128)(2,1)S(1)} %collective-permute-done.9.got_ref), custom_call_target="tpu_custom_call" | custom-call | tf_op jit(solution)/shard_map/rank_mix/pallas_call | solution.py:81
  41.3 1.3 %collective-permute-done.10.far_ref = f32[256,64]{1,0:T(8,128)S(1)} collective-permute-done((f32[256,64]{1,0:T(8,128)S(1)}, f32[256,64]{1,0:T(8,128)S(1)}, u32[]{:S(2)}, u32[]{:S(2)}) %collective-permute-start.10) | collective-permute-done | bytes 65568 | tf_op jit(solution)/shard_map/ppermute | solution.py:29
  42.7 0.7 %collective-permute-done.14.refs_1_ = bf16[2,5,64,128]{3,2,1,0:T(8,128)(2,1)S(1)} collective-permute-done((bf16[2,5,64,128]{3,2,1,0:T(8,128)(2,1)S(1)}, bf16[2,5,64,128]{3,2,1,0:T(8,128)(2,1)S(1)}, u32[]{:S(2)}, u32[]{:S(2)}) %collective-permute-start.14) | collective-permute-done | bytes 163872 | tf_op jit(solution)/shard_map/ppermute | solution.py:29
  43.4 1.9 %delta.1 = bf16[256,2560]{1,0:T(8,128)(2,1)} custom-call(s32[4]{0:T(128)S(1)} %copy-done.4, f32[256,64]{1,0:T(8,128)S(1)} %rank_mix.1.near_ref, f32[256,64]{1,0:T(8,128)S(1)} %collective-permute-done.10.far_ref, bf16[2,5,64,128]{3,2,1,0:T(8,128)(2,1)S(1)} %assemble.3.refs_0_, bf16[2,5,64,128]{3,2,1,0:T(8,128)(2,1)S(1)} %collective-permute-done.14.refs_1_), custom_call_target="tpu_custom_call" | custom-call | tf_op jit(solution)/shard_map/delta/pallas_call | solution.py:189
  (23 shorter events, 0.4 us)
Async XLA Ops:
  1.1 10.9 %collective-permute-start = (bf16[8,64,128]{2,1,0:T(8,128)(2,1)S(1)}, bf16[8,64,128]{2,1,0:T(8,128)(2,1)S(1)}, u32[]{:S(2)}, u32[]{:S(2)}) collective-permute-start(bf16[8,64,128]{2,1,0:T(8,128)(2,1)S(1)} %get-tuple-element.47), channel_id=1, source_target_pairs={{0,2},{2,0},{4,6},{6,4},{8,10},{10,8},{12,14},{14,12},{1,3},{3,1},... | collective-permute-start | bytes 393224 | tf_op jit(solution)/shard_map/ppermute | solution.py:29
  4.1 7.9 %collective-permute-start.1 = (bf16[8,64,128]{2,1,0:T(8,128)(2,1)S(1)}, bf16[8,64,128]{2,1,0:T(8,128)(2,1)S(1)}, u32[]{:S(2)}, u32[]{:S(2)}) collective-permute-start(bf16[8,64,128]{2,1,0:T(8,128)(2,1)S(1)} %get-tuple-element.46), channel_id=1, source_target_pairs={{0,4},{2,6},{4,0},{6,2},{8,12},{10,14},{12,8},{14,10},{1,5},{3,7},... | collective-permute-start | bytes 393224 | tf_op jit(solution)/shard_map/ppermute | solution.py:29
  5.7 6.4 %collective-permute-start.2 = (bf16[8,64,128]{2,1,0:T(8,128)(2,1)S(1)}, bf16[8,64,128]{2,1,0:T(8,128)(2,1)S(1)}, u32[]{:S(2)}, u32[]{:S(2)}) collective-permute-start(bf16[8,64,128]{2,1,0:T(8,128)(2,1)S(1)} %get-tuple-element.45), channel_id=1, source_target_pairs={{0,6},{2,4},{4,2},{6,0},{8,14},{10,12},{12,10},{14,8},{1,7},{3,5},... | collective-permute-start | bytes 393224 | tf_op jit(solution)/shard_map/ppermute | solution.py:29
  6.6 12.0 %collective-permute-start.6 = (bf16[10,64,128]{2,1,0:T(8,128)(2,1)S(1)}, bf16[10,64,128]{2,1,0:T(8,128)(2,1)S(1)}, u32[]{:S(2)}, u32[]{:S(2)}) collective-permute-start(bf16[10,64,128]{2,1,0:T(8,128)(2,1)S(1)} %slice.47), channel_id=1, source_target_pairs={{0,2},{2,0},{4,6},{6,4},{8,10},{10,8},{12,14},{14,12},{1,3},{3,1},... | collective-permute-start | bytes 491528 | tf_op jit(solution)/shard_map/ppermute | solution.py:29
  9.8 1.0 %copy-start.3 = (bf16[1,64,20,128]{3,1,2,0:T(8,128)(2,1)S(1)}, bf16[1,64,20,128]{3,1,2,0:T(8,128)(2,1)}, u32[]{:S(2)}) copy-start(bf16[1,64,20,128]{3,1,2,0:T(8,128)(2,1)} %param.13) | copy-start | bytes 983044
  10.8 0.7 %copy-start.4 = (s32[4]{0:T(128)S(1)}, s32[4]{0:T(128)}, u32[]{:S(2)}) copy-start(s32[4]{0:T(128)} %slots.1.slots_ref) | copy-start | bytes 52
  12.0 5.2 %copy-start.1 = (bf16[256,512]{1,0:T(8,128)(2,1)S(1)}, bf16[256,512]{1,0:T(8,128)(2,1)}, u32[]{:S(2)}) copy-start(bf16[256,512]{1,0:T(8,128)(2,1)} %key_ref.1) | copy-start | bytes 786436
  12.0 5.1 %copy-start.2 = (bf16[256,512]{1,0:T(8,128)(2,1)S(1)}, bf16[256,512]{1,0:T(8,128)(2,1)}, u32[]{:S(2)}) copy-start(bf16[256,512]{1,0:T(8,128)(2,1)} %value_ref.1) | copy-start | bytes 786436
  12.7 7.0 %collective-permute-start.3 = (bf16[8,64,128]{2,1,0:T(8,128)(2,1)S(1)}, bf16[8,64,128]{2,1,0:T(8,128)(2,1)S(1)}, u32[]{:S(2)}, u32[]{:S(2)}) collective-permute-start(bf16[8,64,128]{2,1,0:T(8,128)(2,1)S(1)} %get-tuple-element.25), channel_id=1, source_target_pairs={{0,4},{2,6},{4,0},{6,2},{8,12},{10,14},{12,8},{14,10},{1,5},{3,7},... | collective-permute-start | bytes 393224 | tf_op jit(solution)/shard_map/ppermute | solution.py:29
  14.4 11.0 %collective-permute-start.4 = (bf16[8,64,128]{2,1,0:T(8,128)(2,1)S(1)}, bf16[8,64,128]{2,1,0:T(8,128)(2,1)S(1)}, u32[]{:S(2)}, u32[]{:S(2)}) collective-permute-start(bf16[8,64,128]{2,1,0:T(8,128)(2,1)S(1)} %get-tuple-element.26), channel_id=1, source_target_pairs={{0,8},{2,10},{4,12},{6,14},{8,0},{10,2},{12,4},{14,6},{1,9},{3,11}... | collective-permute-start | bytes 393224 | tf_op jit(solution)/shard_map/ppermute | solution.py:29
  16.9 9.5 %collective-permute-start.5 = (bf16[8,64,128]{2,1,0:T(8,128)(2,1)S(1)}, bf16[8,64,128]{2,1,0:T(8,128)(2,1)S(1)}, u32[]{:S(2)}, u32[]{:S(2)}) collective-permute-start(bf16[8,64,128]{2,1,0:T(8,128)(2,1)S(1)} %get-tuple-element.27), channel_id=1, source_target_pairs={{0,12},{2,14},{4,8},{6,10},{8,4},{10,6},{12,0},{14,2},{1,13},{3,15... | collective-permute-start | bytes 393224 | tf_op jit(solution)/shard_map/ppermute | solution.py:29
  17.2 15.8 %collective-permute-start.8 = (bf16[256,1024]{1,0:T(8,128)(2,1)S(1)}, bf16[256,1024]{1,0:T(8,128)(2,1)S(1)}, u32[]{:S(2)}, u32[]{:S(2)}) collective-permute-start(bf16[256,1024]{1,0:T(8,128)(2,1)S(1)} %pad_maximum_fusion), channel_id=1, source_target_pairs={{0,2},{2,0},{4,6},{6,4},{8,10},{10,8},{12,14},{14,12},{1,3},{3,1},... | collective-permute-start | bytes 1572872 | tf_op jit(solution)/shard_map/ppermute | solution.py:29
  18.7 8.3 %collective-permute-start.7 = (bf16[10,64,128]{2,1,0:T(8,128)(2,1)S(1)}, bf16[10,64,128]{2,1,0:T(8,128)(2,1)S(1)}, u32[]{:S(2)}, u32[]{:S(2)}) collective-permute-start(bf16[10,64,128]{2,1,0:T(8,128)(2,1)S(1)} %pad_maximum_fusion.1), channel_id=1, source_target_pairs={{0,4},{2,6},{4,0},{6,2},{8,12},{10,14},{12,8},{14,10},{1,5},{3,7},... | collective-permute-start | bytes 491528 | tf_op jit(solution)/shard_map/ppermute | solution.py:29
  26.4 6.6 %copy-start = (bf16[256,4096]{1,0:T(8,128)(2,1)S(1)}, bf16[256,4096]{1,0:T(8,128)(2,1)}, u32[]{:S(2)}) copy-start(bf16[256,4096]{1,0:T(8,128)(2,1)} %query_ref.1) | copy-start | bytes 6291460
  27.7 8.0 %collective-permute-start.11 = (bf16[5,64,128]{2,1,0:T(8,128)(2,1)S(1)}, bf16[5,64,128]{2,1,0:T(8,128)(2,1)S(1)}, u32[]{:S(2)}, u32[]{:S(2)}) collective-permute-start(bf16[5,64,128]{2,1,0:T(8,128)(2,1)S(1)} %get-tuple-element.36), channel_id=1, source_target_pairs={{0,4},{2,6},{4,0},{6,2},{8,12},{10,14},{12,8},{14,10},{1,5},{3,7},... | collective-permute-start | bytes 245768 | tf_op jit(solution)/shard_map/ppermute | solution.py:29
  29.4 7.0 %collective-permute-start.12 = (bf16[5,64,128]{2,1,0:T(8,128)(2,1)S(1)}, bf16[5,64,128]{2,1,0:T(8,128)(2,1)S(1)}, u32[]{:S(2)}, u32[]{:S(2)}) collective-permute-start(bf16[5,64,128]{2,1,0:T(8,128)(2,1)S(1)} %get-tuple-element.37), channel_id=1, source_target_pairs={{0,8},{2,10},{4,12},{6,14},{8,0},{10,2},{12,4},{14,6},{1,9},{3,11}... | collective-permute-start | bytes 245768 | tf_op jit(solution)/shard_map/ppermute | solution.py:29
  31.1 6.3 %collective-permute-start.13 = (bf16[5,64,128]{2,1,0:T(8,128)(2,1)S(1)}, bf16[5,64,128]{2,1,0:T(8,128)(2,1)S(1)}, u32[]{:S(2)}, u32[]{:S(2)}) collective-permute-start(bf16[5,64,128]{2,1,0:T(8,128)(2,1)S(1)} %get-tuple-element.38), channel_id=1, source_target_pairs={{0,12},{2,14},{4,8},{6,10},{8,4},{10,6},{12,0},{14,2},{1,13},{3,15... | collective-permute-start | bytes 245768 | tf_op jit(solution)/shard_map/ppermute | solution.py:29
  32.2 7.9 %collective-permute-start.9 = (bf16[2,8,64,128]{3,2,1,0:T(8,128)(2,1)S(1)}, bf16[2,8,64,128]{3,2,1,0:T(8,128)(2,1)S(1)}, u32[]{:S(2)}, u32[]{:S(2)}) collective-permute-start(bf16[2,8,64,128]{3,2,1,0:T(8,128)(2,1)S(1)} %assemble.2.held_ref), channel_id=1, source_target_pairs={{0,2},{2,0},{4,6},{6,4},{8,10},{10,8},{12,14},{14,12},{1,3},{3,1},... | collective-permute-start | bytes 786440 | tf_op jit(solution)/shard_map/ppermute | solution.py:29
  38.0 5.4 %collective-permute-start.14 = (bf16[2,5,64,128]{3,2,1,0:T(8,128)(2,1)S(1)}, bf16[2,5,64,128]{3,2,1,0:T(8,128)(2,1)S(1)}, u32[]{:S(2)}, u32[]{:S(2)}) collective-permute-start(bf16[2,5,64,128]{3,2,1,0:T(8,128)(2,1)S(1)} %assemble.3.refs_0_), channel_id=1, source_target_pairs={{0,2},{2,0},{4,6},{6,4},{8,10},{10,8},{12,14},{14,12},{1,3},{3,1},... | collective-permute-start | bytes 491528 | tf_op jit(solution)/shard_map/ppermute | solution.py:29
  41.3 1.4 %collective-permute-start.10 = (f32[256,64]{1,0:T(8,128)S(1)}, f32[256,64]{1,0:T(8,128)S(1)}, u32[]{:S(2)}, u32[]{:S(2)}) collective-permute-start(f32[256,64]{1,0:T(8,128)S(1)} %rank_mix.1.near_ref), channel_id=1, source_target_pairs={{0,1},{1,0},{2,3},{3,2},{4,5},{5,4},{6,7},{7,6},{8,9},{9,8},{10,11... | collective-permute-start | bytes 196616 | tf_op jit(solution)/shard_map/ppermute | solution.py:29

commit v7 on v6

--- a/solution.py
+++ b/solution.py
@@ -150,6 +150,11 @@
         refs[7][1] = refs[6][...]
 
 
+def turn_kernel(slots_ref, *refs):
+    assemble_kernel(slots_ref, *refs[:7], refs[11])
+    choose_kernel(slots_ref, *refs[7:11], *refs[12:])
+
+
 def rank_kernel(slots_ref, context_ref, held_ref, got_ref, rank_ref):
     me = lax.axis_index("req")
     first = (slots_ref[me >> 1] ^ me) & 3
@@ -214,8 +219,7 @@
 def spread_in_turn(over_x, own, earlier):
     count = own[0].shape[0]
     over_x = after(earlier, over_x)
-    over_z = swapped(jnp.concatenate([own[1], over_x[count:]]), "req", 2)
-    return [own[0], over_x[:count], over_z[:count], over_z[count:]]
+    return [own[0], over_x[:count], swapped(own[1], "req", 2), swapped(over_x[count:], "req", 2)]
 
 
 def deliver(slots, quarters, weight=0):
@@ -242,9 +246,12 @@
     down_sent, down_came = deliver(slots, down_quarters, WEIGHT)
     far = swapped(jnp.concatenate(after(down_sent, (keys, values)), axis=1), "req", 1)
     up_quarters = spread_in_turn(up_over_x, up_own, down_sent)
-    down_held = assemble(slots, down_quarters, down_came, 3000_000_000)
+    both = jax.ShapeDtypeStruct((2, *down_came[0].shape), down.dtype)
+    one = jax.ShapeDtypeStruct(up_quarters[0].shape, up.dtype)
+    parts = (*down_quarters, *down_came, *up_quarters)
+    down_held, *up_sent = in_vmem(turn_kernel, "turn", [both] + [one] * 3, slots, *parts, weight=WEIGHT)
+    up_came = [swapped(panel, "req", 2 * apart) for apart, panel in enumerate(up_sent, 1)]
     down_got = swapped(down_held, "req", 1)
-    up_sent, up_came = deliver(slots, after(down_held, up_quarters))
     context = attend(queries, keys, values, after(up_sent, far))
     up_held = assemble(slots, up_quarters, after(context, up_came), 1000_000_000)
     up_got = swapped(up_held, "req", 1)

time: 45.4 us -> 46 us (1.013)
  waiting for transfers between devices: 10.7 us -> 11.8 us
  Pallas kernels: 9.94 us -> 9.39 us
    ppermute x15 -> x16, waiting for transfers between devices: 10.7 us -> 11.8 us  [swapped(): return lax.ppermute(shard, axis, [(i, i ^ mask) for i in range(size)])]
    pallas_call x7 -> x6, Pallas kernels: 6.89 us -> 6.33 us  [in_vmem(): pl.pallas_call(kernel, in_specs=[pl.BlockSpec(memory_space=pltpu.SMEM)] *...]
    ppermute x15 -> x16, starting transfers between devices: 20.6 us -> 20.7 us  [swapped(): return lax.ppermute(shard, axis, [(i, i ^ mask) for i in range(size)])]
  transfers between devices with their start and end apart: 15 -> 16, of which waited for: 7 -> 6; matrix products, arithmetic and copies ran while one was open for 2% -> 2% of each run, Pallas kernels for 18% -> 16%
where the time goes in v7:
time: 46 us; the launch traced here: 45.8 us
  starting transfers between devices  20.7 us (45%)
  waiting for transfers between devices  11.8 us (26%)
  Pallas kernels  9.39 us (20%)
  local copies, waits for them, and re-layouts  3.71 us (8%)
    ppermute x16, starting transfers between devices, swapped(): return lax.ppermute(shard, axis, [(i, i ^ mask) for i in range(size)])  20.7 us
    ppermute x16, waiting for transfers between devices, swapped(): return lax.ppermute(shard, axis, [(i, i ^ mask) for i in range(size)])  11.8 us
    pallas_call x6, Pallas kernels, in_vmem(): pl.pallas_call(kernel, in_specs=[pl.BlockSpec(memory_space=pltpu.SMEM)] *...  6.33 us
    pallas_call x1, Pallas kernels, delta_of(): pl.pallas_call(delta_kernel, in_specs=[pl.BlockSpec(memory_space=pltpu.SM...  1.86 us
    unnamed x10, local copies, waits for them, and re-layouts  1.64 us
    pallas_call x1, Pallas kernels, slots_of(): pl.pallas_call(slots_kernel, in_specs=[pl.BlockSpec(memory_space=pltpu.SM...  1.2 us
    slice x1, local copies, waits for them, and re-layouts, quarter_cut(): return [blocks[k * count:(k + 1) * count] for k in range(4)]  1.13 us
    slice x1, local copies, waits for them, and re-layouts, eight_way(): up_half = up[half:]  0.93 us
  transfers between devices with their start and end apart: 16, of which 6 were waited for; matrix products, arithmetic and copies ran while one was open for 2% of the time, Pallas kernels for 16%

profile of v7, /device:TPU:0, one launch (start us, length us, event | category | flops | bytes accessed | tf_op | source)
XLA Modules:
  0.0 45.8 jit_solution(3273990496117051057)
XLA Ops:
  0.0 1.1 %slice_bitcast_fusion = (bf16[8,64,128]{2,1,0:T(8,128)(2,1)S(1)}, bf16[8,64,128]{2,1,0:T(8,128)(2,1)S(1)}, bf16[8,64,128]{2,1,0:T(8,128)(2,1)S(1)}, bf16[8,64,128]{2,1,0:T(8,128)(2,1)S(1)}) fusion(bf16[1,32,64,128]{3,2,1,0:T(8,128)(2,1)} %bitcast.14), kind=kLoop, calls=%fused_computation.1 | loop fusion | bytes 1048576 | tf_op jit(solution)/shard_map/slice | solution.py:208
  1.1 3.0 %collective-permute-start = (bf16[8,64,128]{2,1,0:T(8,128)(2,1)S(1)}, bf16[8,64,128]{2,1,0:T(8,128)(2,1)S(1)}, u32[]{:S(2)}, u32[]{:S(2)}) collective-permute-start(bf16[8,64,128]{2,1,0:T(8,128)(2,1)S(1)} %get-tuple-element.41), channel_id=1, source_target_pairs={{0,2},{2,0},{4,6},{6,4},{8,10},{10,8},{12,14},{14,12},{1,3},{3,1},... | collective-permute-start | bytes 393224 | tf_op jit(solution)/shard_map/ppermute | solution.py:29
  4.1 1.6 %collective-permute-start.1 = (bf16[8,64,128]{2,1,0:T(8,128)(2,1)S(1)}, bf16[8,64,128]{2,1,0:T(8,128)(2,1)S(1)}, u32[]{:S(2)}, u32[]{:S(2)}) collective-permute-start(bf16[8,64,128]{2,1,0:T(8,128)(2,1)S(1)} %get-tuple-element.40), channel_id=1, source_target_pairs={{0,4},{2,6},{4,0},{6,2},{8,12},{10,14},{12,8},{14,10},{1,5},{3,7},... | collective-permute-start | bytes 393224 | tf_op jit(solution)/shard_map/ppermute | solution.py:29
  5.7 0.9 %slice.41 = bf16[10,64,128]{2,1,0:T(8,128)(2,1)S(1)} slice(bf16[20,64,128]{2,1,0:T(8,128)(2,1)} %bitcast.12), slice={[10:20], [0:64], [0:128]} | slice | bytes 327680 | tf_op jit(solution)/shard_map/slice | solution.py:242
  6.6 2.0 %collective-permute-start.6 = (bf16[10,64,128]{2,1,0:T(8,128)(2,1)S(1)}, bf16[10,64,128]{2,1,0:T(8,128)(2,1)S(1)}, u32[]{:S(2)}, u32[]{:S(2)}) collective-permute-start(bf16[10,64,128]{2,1,0:T(8,128)(2,1)S(1)} %slice.41), channel_id=1, source_target_pairs={{0,2},{2,0},{4,6},{6,4},{8,10},{10,8},{12,14},{14,12},{1,3},{3,1},... | collective-permute-start | bytes 491528 | tf_op jit(solution)/shard_map/ppermute | solution.py:29
  8.6 1.2 %slots.1.slots_ref = s32[4]{0:T(128)} custom-call(s32[4]{0:T(128)} %adapter_ref.1, s32[8]{0:T(128)} %table_ref.1), custom_call_target="tpu_custom_call" | custom-call | tf_op jit(solution)/shard_map/slots/pallas_call | solution.py:99
  9.8 1.0 %copy-done.3 = bf16[1,64,20,128]{3,1,2,0:T(8,128)(2,1)S(1)} copy-done((bf16[1,64,20,128]{3,1,2,0:T(8,128)(2,1)S(1)}, bf16[1,64,20,128]{3,1,2,0:T(8,128)(2,1)}, u32[]{:S(2)}) %copy-start.3) | copy-done | bytes 327704
  10.8 0.7 %copy-done.4 = s32[4]{0:T(128)S(1)} copy-done((s32[4]{0:T(128)S(1)}, s32[4]{0:T(128)}, u32[]{:S(2)}) %copy-start.4) | copy-done | bytes 40
  11.5 0.6 %own.1 = (bf16[5,64,128]{2,1,0:T(8,128)(2,1)S(1)}, bf16[5,64,128]{2,1,0:T(8,128)(2,1)S(1)}) custom-call(s32[4]{0:T(128)S(1)} %copy-done.4, bf16[20,64,128]{2,1,0:T(8,128)(2,1)S(1)} %bitcast.13), custom_call_target="tpu_custom_call" | custom-call | tf_op jit(solution)/shard_map/own/pallas_call | solution.py:81
  12.0 1.6 %collective-permute-start.7 = (bf16[5,64,128]{2,1,0:T(8,128)(2,1)S(1)}, bf16[5,64,128]{2,1,0:T(8,128)(2,1)S(1)}, u32[]{:S(2)}, u32[]{:S(2)}) collective-permute-start(bf16[5,64,128]{2,1,0:T(8,128)(2,1)S(1)} %get-tuple-element.28), channel_id=1, source_target_pairs={{0,4},{2,6},{4,0},{6,2},{8,12},{10,14},{12,8},{14,10},{1,5},{3,7},... | collective-permute-start | bytes 245768 | tf_op jit(solution)/shard_map/ppermute | solution.py:29
  13.7 0.6 %choose.1 = (bf16[8,64,128]{2,1,0:T(8,128)(2,1)S(1)}, bf16[8,64,128]{2,1,0:T(8,128)(2,1)S(1)}, bf16[8,64,128]{2,1,0:T(8,128)(2,1)S(1)}) custom-call(s32[4]{0:T(128)S(1)} %copy-done.4, bf16[8,64,128]{2,1,0:T(8,128)(2,1)S(1)} %get-tuple-element.42.refs_0_, bf16[8,64,128]{2,1,0:T(8,128)(2,1)S(1)} %collective-permute-done.refs_1_, ...), custom_call_target="tpu_custom_call" | custom-call | flops 3000000000 | bytes 30000000 | tf_op jit(solution)/shard_map/choose/pallas_call | solution.py:81
  14.3 0.5 %collective-permute-start.3 = (bf16[8,64,128]{2,1,0:T(8,128)(2,1)S(1)}, bf16[8,64,128]{2,1,0:T(8,128)(2,1)S(1)}, u32[]{:S(2)}, u32[]{:S(2)}) collective-permute-start(bf16[8,64,128]{2,1,0:T(8,128)(2,1)S(1)} %get-tuple-element.22), channel_id=1, source_target_pairs={{0,4},{2,6},{4,0},{6,2},{8,12},{10,14},{12,8},{14,10},{1,5},{3,7},... | collective-permute-start | bytes 393224 | tf_op jit(solution)/shard_map/ppermute | solution.py:29
  14.9 2.6 %collective-permute-start.4 = (bf16[8,64,128]{2,1,0:T(8,128)(2,1)S(1)}, bf16[8,64,128]{2,1,0:T(8,128)(2,1)S(1)}, u32[]{:S(2)}, u32[]{:S(2)}) collective-permute-start(bf16[8,64,128]{2,1,0:T(8,128)(2,1)S(1)} %get-tuple-element.23), channel_id=1, source_target_pairs={{0,8},{2,10},{4,12},{6,14},{8,0},{10,2},{12,4},{14,6},{1,9},{3,11}... | collective-permute-start | bytes 393224 | tf_op jit(solution)/shard_map/ppermute | solution.py:29
  17.4 1.3 %collective-permute-start.5 = (bf16[8,64,128]{2,1,0:T(8,128)(2,1)S(1)}, bf16[8,64,128]{2,1,0:T(8,128)(2,1)S(1)}, u32[]{:S(2)}, u32[]{:S(2)}) collective-permute-start(bf16[8,64,128]{2,1,0:T(8,128)(2,1)S(1)} %get-tuple-element.24), channel_id=1, source_target_pairs={{0,12},{2,14},{4,8},{6,10},{8,4},{10,6},{12,0},{14,2},{1,13},{3,15... | collective-permute-start | bytes 393224 | tf_op jit(solution)/shard_map/ppermute | solution.py:29
  18.9 0.6 %collective-permute-start.9 = (bf16[256,1024]{1,0:T(8,128)(2,1)S(1)}, bf16[256,1024]{1,0:T(8,128)(2,1)S(1)}, u32[]{:S(2)}, u32[]{:S(2)}) collective-permute-start(bf16[256,1024]{1,0:T(8,128)(2,1)S(1)} %pad_maximum_fusion), channel_id=1, source_target_pairs={{0,2},{2,0},{4,6},{6,4},{8,10},{10,8},{12,14},{14,12},{1,3},{3,1},... | collective-permute-start | bytes 1572872 | tf_op jit(solution)/shard_map/ppermute | solution.py:29
  19.5 0.3 collective-permute-start.8
  19.8 5.1 %collective-permute-done.8.refs_10_.refs_3_ = bf16[5,64,128]{2,1,0:T(8,128)(2,1)S(1)} collective-permute-done((bf16[5,64,128]{2,1,0:T(8,128)(2,1)S(1)}, bf16[5,64,128]{2,1,0:T(8,128)(2,1)S(1)}, u32[]{:S(2)}, u32[]{:S(2)}) %collective-permute-start.8) | collective-permute-done | bytes 81952 | tf_op jit(solution)/shard_map/ppermute | solution.py:29
  24.9 1.3 %collective-permute-done.4.refs_5_ = bf16[8,64,128]{2,1,0:T(8,128)(2,1)S(1)} collective-permute-done((bf16[8,64,128]{2,1,0:T(8,128)(2,1)S(1)}, bf16[8,64,128]{2,1,0:T(8,128)(2,1)S(1)}, u32[]{:S(2)}, u32[]{:S(2)}) %collective-permute-start.4) | collective-permute-done | bytes 131104 | tf_op jit(solution)/shard_map/ppermute | solution.py:29
  26.2 1.5 %collective-permute-done.5.refs_6_ = bf16[8,64,128]{2,1,0:T(8,128)(2,1)S(1)} collective-permute-done((bf16[8,64,128]{2,1,0:T(8,128)(2,1)S(1)}, bf16[8,64,128]{2,1,0:T(8,128)(2,1)S(1)}, u32[]{:S(2)}, u32[]{:S(2)}) %collective-permute-start.5) | collective-permute-done | bytes 131104 | tf_op jit(solution)/shard_map/ppermute | solution.py:29
  27.7 0.7 %turn.1 = (bf16[2,8,64,128]{3,2,1,0:T(8,128)(2,1)S(1)}, bf16[5,64,128]{2,1,0:T(8,128)(2,1)S(1)}, bf16[5,64,128]{2,1,0:T(8,128)(2,1)S(1)}, bf16[5,64,128]{2,1,0:T(8,128)(2,1)S(1)}) custom-call(s32[4]{0:T(128)S(1)} %copy-done.4, bf16[8,64,128]{2,1,0:T(8,128)(2,1)S(1)} %get-tuple-element.42.refs_0_, bf16[8,64,128]{2,1,0:T(8,128)(2,1)S(1)} %collective-permute-done.refs_1_, ...), custom_call_target="tpu_custom_call" | custom-call | flops 3000000000 | bytes 30000000 | tf_op jit(solution)/shard_map/turn/pallas_call | solution.py:81
  28.4 1.7 %collective-permute-start.12 = (bf16[5,64,128]{2,1,0:T(8,128)(2,1)S(1)}, bf16[5,64,128]{2,1,0:T(8,128)(2,1)S(1)}, u32[]{:S(2)}, u32[]{:S(2)}) collective-permute-start(bf16[5,64,128]{2,1,0:T(8,128)(2,1)S(1)} %get-tuple-element.29), channel_id=1, source_target_pairs={{0,4},{2,6},{4,0},{6,2},{8,12},{10,14},{12,8},{14,10},{1,5},{3,7},... | collective-permute-start | bytes 245768 | tf_op jit(solution)/shard_map/ppermute | solution.py:29
  30.1 1.1 %collective-permute-start.13 = (bf16[5,64,128]{2,1,0:T(8,128)(2,1)S(1)}, bf16[5,64,128]{2,1,0:T(8,128)(2,1)S(1)}, u32[]{:S(2)}, u32[]{:S(2)}) collective-permute-start(bf16[5,64,128]{2,1,0:T(8,128)(2,1)S(1)} %get-tuple-element.30), channel_id=1, source_target_pairs={{0,8},{2,10},{4,12},{6,14},{8,0},{10,2},{12,4},{14,6},{1,9},{3,11}... | collective-permute-start | bytes 245768 | tf_op jit(solution)/shard_map/ppermute | solution.py:29
  31.1 1.7 %collective-permute-start.14 = (bf16[5,64,128]{2,1,0:T(8,128)(2,1)S(1)}, bf16[5,64,128]{2,1,0:T(8,128)(2,1)S(1)}, u32[]{:S(2)}, u32[]{:S(2)}) collective-permute-start(bf16[5,64,128]{2,1,0:T(8,128)(2,1)S(1)} %get-tuple-element.31), channel_id=1, source_target_pairs={{0,12},{2,14},{4,8},{6,10},{8,4},{10,6},{12,0},{14,2},{1,13},{3,15... | collective-permute-start | bytes 245768 | tf_op jit(solution)/shard_map/ppermute | solution.py:29
  32.8 0.5 %collective-permute-start.10 = (bf16[2,8,64,128]{3,2,1,0:T(8,128)(2,1)S(1)}, bf16[2,8,64,128]{3,2,1,0:T(8,128)(2,1)S(1)}, u32[]{:S(2)}, u32[]{:S(2)}) collective-permute-start(bf16[2,8,64,128]{3,2,1,0:T(8,128)(2,1)S(1)} %get-tuple-element.35.held_ref), channel_id=1, source_target_pairs={{0,2},{2,0},{4,6},{6,4},{8,10},{10,8},{12,14},{14,12},{1,3},{3,1},... | collective-permute-start | bytes 786440 | tf_op jit(solution)/shard_map/ppermute | solution.py:29
  33.4 2.7 %attend.1.context_ref = bf16[4,256,1024]{2,1,0:T(8,128)(2,1)S(1)} custom-call(bf16[256,4096]{1,0:T(8,128)(2,1)S(1)} %copy-done, bf16[256,512]{1,0:T(8,128)(2,1)S(1)} %copy-done.1, bf16[256,512]{1,0:T(8,128)(2,1)S(1)} %copy-done.2, bf16[256,1024]{1,0:T(8,128)(2,1)S(1)} %collective-permute-done.9.far_ref), custom_call_target="tpu_custom_call" | custom-call | tf_op jit(solution)/shard_map/attend/pallas_call | solution.py:81
  36.1 1.9 %collective-permute-done.13.refs_5_ = bf16[5,64,128]{2,1,0:T(8,128)(2,1)S(1)} collective-permute-done((bf16[5,64,128]{2,1,0:T(8,128)(2,1)S(1)}, bf16[5,64,128]{2,1,0:T(8,128)(2,1)S(1)}, u32[]{:S(2)}, u32[]{:S(2)}) %collective-permute-start.13) | collective-permute-done | bytes 81952 | tf_op jit(solution)/shard_map/ppermute | solution.py:29
  37.9 0.6 %assemble.1.refs_0_ = bf16[2,5,64,128]{3,2,1,0:T(8,128)(2,1)S(1)} custom-call(s32[4]{0:T(128)S(1)} %copy-done.4, bf16[5,64,128]{2,1,0:T(8,128)(2,1)S(1)} %get-tuple-element.26.refs_7_.refs_0_, bf16[5,64,128]{2,1,0:T(8,128)(2,1)S(1)} %get-tuple-element.44.refs_8_.refs_1_, bf16[5,64,128]{2,1,0:T(8,128)(2,1)S(1)} %collective-permute-done.7.refs_9_.refs_2_, ...), custom_call_target="tpu_custom_call" | custom-call | flops 1000000000 | bytes 10000000 | tf_op jit(solution)/shard_map/assemble/pallas_call | solution.py:81
  38.5 2.1 %collective-permute-start.15 = (bf16[2,5,64,128]{3,2,1,0:T(8,128)(2,1)S(1)}, bf16[2,5,64,128]{3,2,1,0:T(8,128)(2,1)S(1)}, u32[]{:S(2)}, u32[]{:S(2)}) collective-permute-start(bf16[2,5,64,128]{3,2,1,0:T(8,128)(2,1)S(1)} %assemble.1.refs_0_), channel_id=1, source_target_pairs={{0,2},{2,0},{4,6},{6,4},{8,10},{10,8},{12,14},{14,12},{1,3},{3,1},... | collective-permute-start | bytes 491528 | tf_op jit(solution)/shard_map/ppermute | solution.py:29
  40.7 1.2 %rank_mix.1.near_ref = f32[256,64]{1,0:T(8,128)S(1)} custom-call(s32[4]{0:T(128)S(1)} %copy-done.4, bf16[4,256,1024]{2,1,0:T(8,128)(2,1)S(1)} %attend.1.context_ref, bf16[2,8,64,128]{3,2,1,0:T(8,128)(2,1)S(1)} %get-tuple-element.35.held_ref, bf16[2,8,64,128]{3,2,1,0:T(8,128)(2,1)S(1)} %collective-permute-done.10.got_ref), custom_call_target="tpu_custom_call" | custom-call | tf_op jit(solution)/shard_map/rank_mix/pallas_call | solution.py:81
  42.0 1.3 %collective-permute-done.11.far_ref = f32[256,64]{1,0:T(8,128)S(1)} collective-permute-done((f32[256,64]{1,0:T(8,128)S(1)}, f32[256,64]{1,0:T(8,128)S(1)}, u32[]{:S(2)}, u32[]{:S(2)}) %collective-permute-start.11) | collective-permute-done | bytes 65568 | tf_op jit(solution)/shard_map/ppermute | solution.py:29
  43.3 0.7 %collective-permute-done.15.refs_1_ = bf16[2,5,64,128]{3,2,1,0:T(8,128)(2,1)S(1)} collective-permute-done((bf16[2,5,64,128]{3,2,1,0:T(8,128)(2,1)S(1)}, bf16[2,5,64,128]{3,2,1,0:T(8,128)(2,1)S(1)}, u32[]{:S(2)}, u32[]{:S(2)}) %collective-permute-start.15) | collective-permute-done | bytes 163872 | tf_op jit(solution)/shard_map/ppermute | solution.py:29
  44.0 1.9 %delta.1 = bf16[256,2560]{1,0:T(8,128)(2,1)} custom-call(s32[4]{0:T(128)S(1)} %copy-done.4, f32[256,64]{1,0:T(8,128)S(1)} %rank_mix.1.near_ref, f32[256,64]{1,0:T(8,128)S(1)} %collective-permute-done.11.far_ref, bf16[2,5,64,128]{3,2,1,0:T(8,128)(2,1)S(1)} %assemble.1.refs_0_, bf16[2,5,64,128]{3,2,1,0:T(8,128)(2,1)S(1)} %collective-permute-done.15.refs_1_), custom_call_target="tpu_custom_call" | custom-call | tf_op jit(solution)/shard_map/delta/pallas_call | solution.py:194
  (22 shorter events, 0.2 us)
Async XLA Ops:
  1.1 12.6 %collective-permute-start = (bf16[8,64,128]{2,1,0:T(8,128)(2,1)S(1)}, bf16[8,64,128]{2,1,0:T(8,128)(2,1)S(1)}, u32[]{:S(2)}, u32[]{:S(2)}) collective-permute-start(bf16[8,64,128]{2,1,0:T(8,128)(2,1)S(1)} %get-tuple-element.41), channel_id=1, source_target_pairs={{0,2},{2,0},{4,6},{6,4},{8,10},{10,8},{12,14},{14,12},{1,3},{3,1},... | collective-permute-start | bytes 393224 | tf_op jit(solution)/shard_map/ppermute | solution.py:29
  4.1 9.6 %collective-permute-start.1 = (bf16[8,64,128]{2,1,0:T(8,128)(2,1)S(1)}, bf16[8,64,128]{2,1,0:T(8,128)(2,1)S(1)}, u32[]{:S(2)}, u32[]{:S(2)}) collective-permute-start(bf16[8,64,128]{2,1,0:T(8,128)(2,1)S(1)} %get-tuple-element.40), channel_id=1, source_target_pairs={{0,4},{2,6},{4,0},{6,2},{8,12},{10,14},{12,8},{14,10},{1,5},{3,7},... | collective-permute-start | bytes 393224 | tf_op jit(solution)/shard_map/ppermute | solution.py:29
  5.7 8.0 %collective-permute-start.2 = (bf16[8,64,128]{2,1,0:T(8,128)(2,1)S(1)}, bf16[8,64,128]{2,1,0:T(8,128)(2,1)S(1)}, u32[]{:S(2)}, u32[]{:S(2)}) collective-permute-start(bf16[8,64,128]{2,1,0:T(8,128)(2,1)S(1)} %get-tuple-element.39), channel_id=1, source_target_pairs={{0,6},{2,4},{4,2},{6,0},{8,14},{10,12},{12,10},{14,8},{1,7},{3,5},... | collective-permute-start | bytes 393224 | tf_op jit(solution)/shard_map/ppermute | solution.py:29
  6.6 12.2 %collective-permute-start.6 = (bf16[10,64,128]{2,1,0:T(8,128)(2,1)S(1)}, bf16[10,64,128]{2,1,0:T(8,128)(2,1)S(1)}, u32[]{:S(2)}, u32[]{:S(2)}) collective-permute-start(bf16[10,64,128]{2,1,0:T(8,128)(2,1)S(1)} %slice.41), channel_id=1, source_target_pairs={{0,2},{2,0},{4,6},{6,4},{8,10},{10,8},{12,14},{14,12},{1,3},{3,1},... | collective-permute-start | bytes 491528 | tf_op jit(solution)/shard_map/ppermute | solution.py:29
  9.8 1.0 %copy-start.3 = (bf16[1,64,20,128]{3,1,2,0:T(8,128)(2,1)S(1)}, bf16[1,64,20,128]{3,1,2,0:T(8,128)(2,1)}, u32[]{:S(2)}) copy-start(bf16[1,64,20,128]{3,1,2,0:T(8,128)(2,1)} %param.13) | copy-start | bytes 983044
  10.8 0.7 %copy-start.4 = (s32[4]{0:T(128)S(1)}, s32[4]{0:T(128)}, u32[]{:S(2)}) copy-start(s32[4]{0:T(128)} %slots.1.slots_ref) | copy-start | bytes 52
  12.0 6.8 %copy-start.1 = (bf16[256,512]{1,0:T(8,128)(2,1)S(1)}, bf16[256,512]{1,0:T(8,128)(2,1)}, u32[]{:S(2)}) copy-start(bf16[256,512]{1,0:T(8,128)(2,1)} %key_ref.1) | copy-start | bytes 786436
  12.0 6.8 %copy-start.2 = (bf16[256,512]{1,0:T(8,128)(2,1)S(1)}, bf16[256,512]{1,0:T(8,128)(2,1)}, u32[]{:S(2)}) copy-start(bf16[256,512]{1,0:T(8,128)(2,1)} %value_ref.1) | copy-start | bytes 786436
  12.0 7.5 %collective-permute-start.7 = (bf16[5,64,128]{2,1,0:T(8,128)(2,1)S(1)}, bf16[5,64,128]{2,1,0:T(8,128)(2,1)S(1)}, u32[]{:S(2)}, u32[]{:S(2)}) collective-permute-start(bf16[5,64,128]{2,1,0:T(8,128)(2,1)S(1)} %get-tuple-element.28), channel_id=1, source_target_pairs={{0,4},{2,6},{4,0},{6,2},{8,12},{10,14},{12,8},{14,10},{1,5},{3,7},... | collective-permute-start | bytes 245768 | tf_op jit(solution)/shard_map/ppermute | solution.py:29
  14.3 10.5 %collective-permute-start.3 = (bf16[8,64,128]{2,1,0:T(8,128)(2,1)S(1)}, bf16[8,64,128]{2,1,0:T(8,128)(2,1)S(1)}, u32[]{:S(2)}, u32[]{:S(2)}) collective-permute-start(bf16[8,64,128]{2,1,0:T(8,128)(2,1)S(1)} %get-tuple-element.22), channel_id=1, source_target_pairs={{0,4},{2,6},{4,0},{6,2},{8,12},{10,14},{12,8},{14,10},{1,5},{3,7},... | collective-permute-start | bytes 393224 | tf_op jit(solution)/shard_map/ppermute | solution.py:29
  14.9 11.4 %collective-permute-start.4 = (bf16[8,64,128]{2,1,0:T(8,128)(2,1)S(1)}, bf16[8,64,128]{2,1,0:T(8,128)(2,1)S(1)}, u32[]{:S(2)}, u32[]{:S(2)}) collective-permute-start(bf16[8,64,128]{2,1,0:T(8,128)(2,1)S(1)} %get-tuple-element.23), channel_id=1, source_target_pairs={{0,8},{2,10},{4,12},{6,14},{8,0},{10,2},{12,4},{14,6},{1,9},{3,11}... | collective-permute-start | bytes 393224 | tf_op jit(solution)/shard_map/ppermute | solution.py:29
  17.4 10.3 %collective-permute-start.5 = (bf16[8,64,128]{2,1,0:T(8,128)(2,1)S(1)}, bf16[8,64,128]{2,1,0:T(8,128)(2,1)S(1)}, u32[]{:S(2)}, u32[]{:S(2)}) collective-permute-start(bf16[8,64,128]{2,1,0:T(8,128)(2,1)S(1)} %get-tuple-element.24), channel_id=1, source_target_pairs={{0,12},{2,14},{4,8},{6,10},{8,4},{10,6},{12,0},{14,2},{1,13},{3,15... | collective-permute-start | bytes 393224 | tf_op jit(solution)/shard_map/ppermute | solution.py:29
  18.9 14.5 %collective-permute-start.9 = (bf16[256,1024]{1,0:T(8,128)(2,1)S(1)}, bf16[256,1024]{1,0:T(8,128)(2,1)S(1)}, u32[]{:S(2)}, u32[]{:S(2)}) collective-permute-start(bf16[256,1024]{1,0:T(8,128)(2,1)S(1)} %pad_maximum_fusion), channel_id=1, source_target_pairs={{0,2},{2,0},{4,6},{6,4},{8,10},{10,8},{12,14},{14,12},{1,3},{3,1},... | collective-permute-start | bytes 1572872 | tf_op jit(solution)/shard_map/ppermute | solution.py:29
  19.5 5.4 %collective-permute-start.8 = (bf16[5,64,128]{2,1,0:T(8,128)(2,1)S(1)}, bf16[5,64,128]{2,1,0:T(8,128)(2,1)S(1)}, u32[]{:S(2)}, u32[]{:S(2)}) collective-permute-start(bf16[5,64,128]{2,1,0:T(8,128)(2,1)S(1)} %get-tuple-element.43), channel_id=1, source_target_pairs={{0,4},{2,6},{4,0},{6,2},{8,12},{10,14},{12,8},{14,10},{1,5},{3,7},... | collective-permute-start | bytes 245768 | tf_op jit(solution)/shard_map/ppermute | solution.py:29
  27.7 5.7 %copy-start = (bf16[256,4096]{1,0:T(8,128)(2,1)S(1)}, bf16[256,4096]{1,0:T(8,128)(2,1)}, u32[]{:S(2)}) copy-start(bf16[256,4096]{1,0:T(8,128)(2,1)} %query_ref.1) | copy-start | bytes 6291460
  28.4 7.7 %collective-permute-start.12 = (bf16[5,64,128]{2,1,0:T(8,128)(2,1)S(1)}, bf16[5,64,128]{2,1,0:T(8,128)(2,1)S(1)}, u32[]{:S(2)}, u32[]{:S(2)}) collective-permute-start(bf16[5,64,128]{2,1,0:T(8,128)(2,1)S(1)} %get-tuple-element.29), channel_id=1, source_target_pairs={{0,4},{2,6},{4,0},{6,2},{8,12},{10,14},{12,8},{14,10},{1,5},{3,7},... | collective-permute-start | bytes 245768 | tf_op jit(solution)/shard_map/ppermute | solution.py:29
  30.1 7.9 %collective-permute-start.13 = (bf16[5,64,128]{2,1,0:T(8,128)(2,1)S(1)}, bf16[5,64,128]{2,1,0:T(8,128)(2,1)S(1)}, u32[]{:S(2)}, u32[]{:S(2)}) collective-permute-start(bf16[5,64,128]{2,1,0:T(8,128)(2,1)S(1)} %get-tuple-element.30), channel_id=1, source_target_pairs={{0,8},{2,10},{4,12},{6,14},{8,0},{10,2},{12,4},{14,6},{1,9},{3,11}... | collective-permute-start | bytes 245768 | tf_op jit(solution)/shard_map/ppermute | solution.py:29
  31.1 6.8 %collective-permute-start.14 = (bf16[5,64,128]{2,1,0:T(8,128)(2,1)S(1)}, bf16[5,64,128]{2,1,0:T(8,128)(2,1)S(1)}, u32[]{:S(2)}, u32[]{:S(2)}) collective-permute-start(bf16[5,64,128]{2,1,0:T(8,128)(2,1)S(1)} %get-tuple-element.31), channel_id=1, source_target_pairs={{0,12},{2,14},{4,8},{6,10},{8,4},{10,6},{12,0},{14,2},{1,13},{3,15... | collective-permute-start | bytes 245768 | tf_op jit(solution)/shard_map/ppermute | solution.py:29
  32.8 7.9 %collective-permute-start.10 = (bf16[2,8,64,128]{3,2,1,0:T(8,128)(2,1)S(1)}, bf16[2,8,64,128]{3,2,1,0:T(8,128)(2,1)S(1)}, u32[]{:S(2)}, u32[]{:S(2)}) collective-permute-start(bf16[2,8,64,128]{3,2,1,0:T(8,128)(2,1)S(1)} %get-tuple-element.35.held_ref), channel_id=1, source_target_pairs={{0,2},{2,0},{4,6},{6,4},{8,10},{10,8},{12,14},{14,12},{1,3},{3,1},... | collective-permute-start | bytes 786440 | tf_op jit(solution)/shard_map/ppermute | solution.py:29
  38.5 5.4 %collective-permute-start.15 = (bf16[2,5,64,128]{3,2,1,0:T(8,128)(2,1)S(1)}, bf16[2,5,64,128]{3,2,1,0:T(8,128)(2,1)S(1)}, u32[]{:S(2)}, u32[]{:S(2)}) collective-permute-start(bf16[2,5,64,128]{3,2,1,0:T(8,128)(2,1)S(1)} %assemble.1.refs_0_), channel_id=1, source_target_pairs={{0,2},{2,0},{4,6},{6,4},{8,10},{10,8},{12,14},{14,12},{1,3},{3,1},... | collective-permute-start | bytes 491528 | tf_op jit(solution)/shard_map/ppermute | solution.py:29
  41.9 1.4 %collective-permute-start.11 = (f32[256,64]{1,0:T(8,128)S(1)}, f32[256,64]{1,0:T(8,128)S(1)}, u32[]{:S(2)}, u32[]{:S(2)}) collective-permute-start(f32[256,64]{1,0:T(8,128)S(1)} %rank_mix.1.near_ref), channel_id=1, source_target_pairs={{0,1},{1,0},{2,3},{3,2},{4,5},{5,4},{6,7},{7,6},{8,9},{9,8},{10,11... | collective-permute-start | bytes 196616 | tf_op jit(solution)/shard_map/ppermute | solution.py:29
